TPU v7x, 32 devices: a whole 2x2x4 slice. The times are simulated.
32 devices in a mesh: dp: 8 (over y, x, core), tensor: 4 (over z).
Axes of the slice: x: 2, y: 2, z: 4, core: 2. Of those that a mesh axis runs over, the one named last changes fastest.
Arguments:
- inputs: bfloat16 [8, 4096, 1024], P('dp', 'tensor'), may hold values from -6 to 6
- skip_input: bfloat16 [8, 4096, 1024], P('dp', 'tensor'), may hold values from -6 to 6
- lengths: int32 [8, 4], P('dp'), may hold values from 1 to 2048, 4096 in all within a row
- time_steps: int32 [8, 4], P('dp'), may hold values from 0 to 999
- w_skip_in: bfloat16 [1024, 1024], replicated, may hold values from -0.125 to 0.125
- w_skip_res: bfloat16 [1024, 1024], replicated, may hold values from -0.125 to 0.125
- w_ada: bfloat16 [256, 4096], replicated, may hold values from -0.375 to 0.375
- w_qkv: bfloat16 [3, 1024, 1024], P(None, None, 'tensor'), may hold values from -0.1875 to 0.1875
- w_out: bfloat16 [1024, 1024], P('tensor'), may hold values from -1.5 to 1.5
- w_up: bfloat16 [1024, 4096], P(None, 'tensor'), may hold values from -0.1875 to 0.1875
- w_down: bfloat16 [4096, 1024], P('tensor'), may hold values from -0.09375 to 0.09375
- cotangent: bfloat16 [8, 4096, 1024], P('dp', 'tensor'), may hold values from -6 to 6
Outputs:
- block_out: float32 [8, 4096, 1024], P('dp', 'tensor')
- grad_inputs: float32 [8, 4096, 1024], P('dp', 'tensor')
- grad_skips: float32 [8, 4096, 1024], P('dp', 'tensor')
- grad_skip_in: float32 [1024, 1024], replicated
- grad_skip_res: float32 [1024, 1024], replicated
- grad_ada: float32 [256, 4096], replicated
- grad_qkv: float32 [3, 1024, 1024], P(None, None, 'tensor')
- grad_out_proj: float32 [1024, 1024], P('tensor')
- grad_up: float32 [1024, 4096], P(None, 'tensor')
- grad_down: float32 [4096, 1024], P('tensor')
Inputs may be any that keep to these rules, and one draw needn't show every extreme that they name: The 4 lengths of each row add up to 4096, and the longest of each row has exactly 2048 frames.
All inputs are finite; a program needn't handle non-finite values.
Results may differ from a plain program's by a relative error of at most 0.018.
Values may be sent and summed in bfloat16 or wider, within the bound.
A program may use at most 384 MiB of HBM per device.

v0:
```python
import math

import jax
import jax.numpy as jnp
from jax import lax
from jax.sharding import PartitionSpec as P

HEAD_DIM = 64


norm_epsilon = 1e-06


def modulated_norm(hidden, shift_part, scale_part):
    center = hidden - jnp.mean(hidden, axis=-1, keepdims=True)
    spread = jnp.mean(center * center, axis=-1, keepdims=True)
    return center * lax.rsqrt(spread + norm_epsilon) * (1.0 + scale_part) + shift_part


def gelu_tanh(pre_act):
    return jax.nn.gelu(pre_act, approximate=True)


def rotate_heads(values, cosine_table, sine_table):
    half_width = values.shape[-1] // 2
    first_half = values[..., :half_width]
    second_half = values[..., half_width:]
    return jnp.concatenate(
        [
            first_half * cosine_table - second_half * sine_table,
            second_half * cosine_table + first_half * sine_table,
        ],
        axis=-1,
    )


def rotate_back(grads_in, cosine_table, sine_table):
    half_width = grads_in.shape[-1] // 2
    first_half = grads_in[..., :half_width]
    second_half = grads_in[..., half_width:]
    return jnp.concatenate(
        [
            first_half * cosine_table + second_half * sine_table,
            second_half * cosine_table - first_half * sine_table,
        ],
        axis=-1,
    )


def frame_layout(lengths, time_steps, row_length, head_width, embed_width):
    utterances = lengths.shape[1]
    ends_at = jnp.cumsum(lengths, axis=1, dtype=jnp.int32)
    starts_at = ends_at - lengths
    positions = jnp.arange(row_length, dtype=jnp.int32)
    segment = jnp.sum(
        (positions[None, :, None] >= ends_at[:, None, :]).astype(jnp.int32), axis=2, dtype=jnp.int32
    )
    member = segment[:, :, None] == jnp.arange(utterances, dtype=jnp.int32)[None, None, :]
    offsets = jnp.sum(jnp.where(member, starts_at[:, None, :], 0), axis=2, dtype=jnp.int32)
    places = (positions[None, :] - offsets).astype(jnp.float32)
    rotary_rate = jnp.exp(
        -math.log(10000.0) * (2.0 * jnp.arange(head_width // 2, dtype=jnp.float32) / head_width)
    )
    angles = places[:, :, None, None] * rotary_rate
    time_rate = jnp.exp(
        -math.log(10000.0) * (jnp.arange(embed_width // 2, dtype=jnp.float32) / (embed_width // 2))
    )
    phases = time_steps.astype(jnp.float32)[:, :, None] * time_rate
    embedding = jnp.concatenate([jnp.sin(phases), jnp.cos(phases)], axis=-1)
    return (segment, member, jnp.cos(angles), jnp.sin(angles), embedding)


def block_scores(query_block, key_rot, segment_block, segment, scale_value):
    scores = (
        jnp.einsum("rqhe,rkhe->rhqk", query_block, key_rot, preferred_element_type=jnp.float32)
        * scale_value
    )
    allowed = (segment_block[:, :, None] == segment[:, None, :])[:, None, :, :]
    return jnp.where(allowed, scores, -1e30)


def attend(query_rot, key_rot, value_low, segment, block_rows, scale_value):
    rows_here, length, heads_here, head_width = query_rot.shape

    def one_block(block_index):
        block_start = block_index * block_rows
        query_block = lax.dynamic_slice_in_dim(query_rot, block_start, block_rows, 1)
        segment_block = lax.dynamic_slice_in_dim(segment, block_start, block_rows, 1)
        scores = block_scores(query_block, key_rot, segment_block, segment, scale_value)
        row_peak = jnp.max(scores, axis=-1, keepdims=True)
        weights = jnp.exp(scores - row_peak)
        row_total = jnp.sum(weights, axis=-1, keepdims=True)
        probs_low = (weights / row_total).astype(jnp.bfloat16)
        context = jnp.einsum(
            "rhqk,rkhe->rqhe", probs_low, value_low, preferred_element_type=jnp.float32
        )
        return (context.astype(jnp.bfloat16), (row_peak + jnp.log(row_total))[..., 0])

    contexts, log_sums = lax.map(one_block, jnp.arange(length // block_rows, dtype=jnp.int32))
    contexts = jnp.moveaxis(contexts, 0, 1).reshape(rows_here, length, heads_here * head_width)
    return (contexts, log_sums)


def attend_back(
    query_rot, key_rot, value_low, segment, log_sums, grad_context, block_rows, scale_value
):
    rows_here, length, heads_here, head_width = query_rot.shape

    def one_block(running, block_index):
        grad_keys, grad_values = running
        block_start = block_index * block_rows
        query_block = lax.dynamic_slice_in_dim(query_rot, block_start, block_rows, 1)
        segment_block = lax.dynamic_slice_in_dim(segment, block_start, block_rows, 1)
        grad_block = lax.dynamic_slice_in_dim(grad_context, block_start, block_rows, 1)
        scores = block_scores(query_block, key_rot, segment_block, segment, scale_value)
        prob_rows = jnp.exp(scores - log_sums[block_index][..., None])
        grad_probs = jnp.einsum(
            "rqhe,rkhe->rhqk", grad_block, value_low, preferred_element_type=jnp.float32
        )
        row_delta = jnp.sum(prob_rows * grad_probs, axis=-1, keepdims=True)
        grad_scores = (prob_rows * (grad_probs - row_delta)).astype(jnp.bfloat16)
        grad_query = (
            jnp.einsum("rhqk,rkhe->rqhe", grad_scores, key_rot, preferred_element_type=jnp.float32)
            * scale_value
        )
        grad_keys = (
            grad_keys
            + jnp.einsum(
                "rhqk,rqhe->rkhe", grad_scores, query_block, preferred_element_type=jnp.float32
            )
            * scale_value
        )
        grad_values = grad_values + jnp.einsum(
            "rhqk,rqhe->rkhe",
            prob_rows.astype(jnp.bfloat16),
            grad_block,
            preferred_element_type=jnp.float32,
        )
        return ((grad_keys, grad_values), grad_query)

    zero_keys = jnp.zeros(query_rot.shape, jnp.float32)
    (grad_keys, grad_values), grad_queries = lax.scan(
        one_block, (zero_keys, zero_keys), jnp.arange(length // block_rows, dtype=jnp.int32)
    )
    grad_queries = jnp.moveaxis(grad_queries, 0, 1).reshape(
        rows_here, length, heads_here, head_width
    )
    return (grad_queries, grad_keys, grad_values)


def front_half(
    inputs,
    skip_input,
    w_skip_in,
    w_skip_res,
    w_qkv,
    w_out,
    modulation,
    segment,
    cosine_table,
    sine_table,
    block_rows,
    scale_value,
):
    base_stream = jnp.einsum("rld,de->rle", inputs, w_skip_in, preferred_element_type=jnp.float32)
    base_stream = base_stream + jnp.einsum(
        "rld,de->rle", skip_input, w_skip_res, preferred_element_type=jnp.float32
    )
    normed_low = modulated_norm(base_stream, modulation[0], modulation[1]).astype(jnp.bfloat16)
    normed_all = lax.all_gather(normed_low, "tensor", axis=1, tiled=True)
    projected = jnp.einsum("rld,kdc->krlc", normed_all, w_qkv, preferred_element_type=jnp.float32)
    split_shape = (normed_all.shape[0], normed_all.shape[1], -1, cosine_table.shape[-1] * 2)
    query_rot = rotate_heads(projected[0].reshape(split_shape), cosine_table, sine_table).astype(
        jnp.bfloat16
    )
    key_rot = rotate_heads(projected[1].reshape(split_shape), cosine_table, sine_table).astype(
        jnp.bfloat16
    )
    value_low = projected[2].reshape(split_shape).astype(jnp.bfloat16)
    context_low, log_sums = attend(query_rot, key_rot, value_low, segment, block_rows, scale_value)
    head_terms = jnp.einsum("rlc,cd->rld", context_low, w_out, preferred_element_type=jnp.float32)
    hidden_one = base_stream + lax.psum_scatter(
        head_terms, "tensor", scatter_dimension=1, tiled=True
    )
    return (
        base_stream,
        normed_all,
        query_rot,
        key_rot,
        value_low,
        context_low,
        log_sums,
        hidden_one,
    )


def feed_half(hidden_one, shift_two, scale_two, w_up):
    ffn_low = modulated_norm(hidden_one, shift_two, scale_two).astype(jnp.bfloat16)
    ffn_all = lax.all_gather(ffn_low, "tensor", axis=1, tiled=True)
    before = jnp.einsum("rld,df->rlf", ffn_all, w_up, preferred_element_type=jnp.float32)
    activated = gelu_tanh(before).astype(jnp.bfloat16)
    return (ffn_all, before, activated)


def on_device(
    inputs,
    skip_input,
    lengths,
    time_steps,
    w_skip_in,
    w_skip_res,
    w_ada,
    w_qkv,
    w_out,
    w_up,
    w_down,
    cotangent,
):
    slice_rows = inputs.shape[1]
    row_length = slice_rows * lax.axis_size("tensor")
    head_width = HEAD_DIM
    block_rows = min(512, row_length // 2)
    scale_value = head_width ** (-0.5)
    segment, member, cosine_table, sine_table, embedding = frame_layout(
        lengths, time_steps, row_length, head_width, w_ada.shape[0]
    )
    member_here = lax.dynamic_slice_in_dim(
        member, lax.axis_index("tensor") * slice_rows, slice_rows, 1
    ).astype(jnp.float32)
    silu_low = jax.nn.silu(embedding).astype(jnp.bfloat16)
    per_utterance = jnp.einsum("rut,tm->rum", silu_low, w_ada, preferred_element_type=jnp.float32)
    frame_mod = jnp.einsum(
        "rlu,rum->rlm", member_here, per_utterance, precision=lax.Precision.HIGHEST
    )
    modulation = jnp.split(frame_mod, 4, axis=-1)
    saved_front = front_half(
        inputs,
        skip_input,
        w_skip_in,
        w_skip_res,
        w_qkv,
        w_out,
        modulation,
        segment,
        cosine_table,
        sine_table,
        block_rows,
        scale_value,
    )
    kept_ffn = feed_half(saved_front[7], modulation[2], modulation[3], w_up)
    ffn_terms = jnp.einsum("rlf,fd->rld", kept_ffn[2], w_down, preferred_element_type=jnp.float32)
    block_out = saved_front[7] + lax.psum_scatter(
        ffn_terms.astype(jnp.bfloat16), "tensor", scatter_dimension=1, tiled=True
    ).astype(jnp.float32)
    saved_front = front_half(
        inputs,
        skip_input,
        w_skip_in,
        w_skip_res,
        w_qkv,
        w_out,
        modulation,
        segment,
        cosine_table,
        sine_table,
        block_rows,
        scale_value,
    )
    kept_ffn = feed_half(saved_front[7], modulation[2], modulation[3], w_up)
    base_stream, normed_all, query_rot, key_rot, value_low, context_low, log_sums, hidden_one = (
        saved_front
    )
    ffn_all, before, activated = kept_ffn
    cot_all = lax.all_gather(cotangent, "tensor", axis=1, tiled=True)
    grad_down = jnp.einsum("rlf,rld->fd", activated, cot_all, preferred_element_type=jnp.float32)
    grad_act = jnp.einsum("rld,fd->rlf", cot_all, w_down, preferred_element_type=jnp.float32)
    gelu_pull = jax.vjp(gelu_tanh, before)[1]
    grad_before = gelu_pull(grad_act)[0].astype(jnp.bfloat16)
    grad_up = jnp.einsum("rld,rlf->df", ffn_all, grad_before, preferred_element_type=jnp.float32)
    ffn_back = jnp.einsum("rlf,df->rld", grad_before, w_up, preferred_element_type=jnp.float32)
    grad_ffn_in = lax.psum_scatter(
        ffn_back.astype(jnp.bfloat16), "tensor", scatter_dimension=1, tiled=True
    ).astype(jnp.float32)
    norm_pull = jax.vjp(modulated_norm, hidden_one, modulation[2], modulation[3])[1]
    grad_hidden_norm, grad_shift_two, grad_scale_two = norm_pull(grad_ffn_in)
    grad_hidden = cotangent.astype(jnp.float32) + grad_hidden_norm
    grad_hidden_all = lax.all_gather(grad_hidden.astype(jnp.bfloat16), "tensor", axis=1, tiled=True)
    grad_out_proj = jnp.einsum(
        "rlc,rld->cd", context_low, grad_hidden_all, preferred_element_type=jnp.float32
    )
    grad_context = jnp.einsum(
        "rld,cd->rlc", grad_hidden_all, w_out, preferred_element_type=jnp.float32
    )
    grad_context = grad_context.astype(jnp.bfloat16).reshape(query_rot.shape)
    grad_queries, grad_keys, grad_values = attend_back(
        query_rot, key_rot, value_low, segment, log_sums, grad_context, block_rows, scale_value
    )
    grad_proj = jnp.stack(
        [
            rotate_back(grad_queries, cosine_table, sine_table),
            rotate_back(grad_keys, cosine_table, sine_table),
            grad_values,
        ]
    ).astype(jnp.bfloat16)
    grad_proj = grad_proj.reshape(3, normed_all.shape[0], normed_all.shape[1], -1)
    grad_qkv = jnp.einsum(
        "rld,krlc->kdc", normed_all, grad_proj, preferred_element_type=jnp.float32
    )
    normed_back = jnp.einsum("krlc,kdc->rld", grad_proj, w_qkv, preferred_element_type=jnp.float32)
    grad_normed = lax.psum_scatter(
        normed_back.astype(jnp.bfloat16), "tensor", scatter_dimension=1, tiled=True
    ).astype(jnp.float32)
    norm_pull_one = jax.vjp(modulated_norm, base_stream, modulation[0], modulation[1])[1]
    grad_base_norm, grad_shift_one, grad_scale_one = norm_pull_one(grad_normed)
    grad_base = (grad_hidden + grad_base_norm).astype(jnp.bfloat16)
    grad_inputs = jnp.einsum(
        "rle,de->rld", grad_base, w_skip_in, preferred_element_type=jnp.float32
    )
    grad_skips = jnp.einsum(
        "rle,de->rld", grad_base, w_skip_res, preferred_element_type=jnp.float32
    )
    grad_skip_in = jnp.einsum("rld,rle->de", inputs, grad_base, preferred_element_type=jnp.float32)
    grad_skip_res = jnp.einsum(
        "rld,rle->de", skip_input, grad_base, preferred_element_type=jnp.float32
    )
    grad_mod = jnp.concatenate(
        [grad_shift_one, grad_scale_one, grad_shift_two, grad_scale_two], axis=-1
    )
    grad_per_utt = jnp.einsum(
        "rlu,rlm->rum", member_here, grad_mod, precision=lax.Precision.HIGHEST
    )
    grad_ada = jnp.einsum(
        "rut,rum->tm", silu_low.astype(jnp.float32), grad_per_utt, precision=lax.Precision.HIGHEST
    )
    grad_skip_in, grad_skip_res, grad_ada = lax.psum(
        (grad_skip_in, grad_skip_res, grad_ada), ("dp", "tensor")
    )
    grad_qkv, grad_out_proj, grad_up, grad_down = (
        lax.psum(grad_qkv.astype(jnp.bfloat16), "dp").astype(jnp.float32),
        lax.psum(grad_out_proj.astype(jnp.bfloat16), "dp").astype(jnp.float32),
        lax.psum(grad_up.astype(jnp.bfloat16), "dp").astype(jnp.float32),
        lax.psum(grad_down.astype(jnp.bfloat16), "dp").astype(jnp.float32),
    )
    return (
        block_out,
        grad_inputs,
        grad_skips,
        grad_skip_in,
        grad_skip_res,
        grad_ada,
        grad_qkv,
        grad_out_proj,
        grad_up,
        grad_down,
    )


def solution(mesh):
    placed = (
        P("dp", "tensor", None),
        P("dp", "tensor", None),
        P("dp", None),
        P("dp", None),
        P(),
        P(),
        P(),
        P(None, None, "tensor"),
        P("tensor", None),
        P(None, "tensor"),
        P("tensor", None),
        P("dp", "tensor", None),
    )
    return jax.shard_map(
        on_device,
        mesh=mesh,
        in_specs=placed,
        out_specs=(
            P("dp", "tensor", None),
            P("dp", "tensor", None),
            P("dp", "tensor", None),
            P(),
            P(),
            P(),
            P(None, None, "tensor"),
            P("tensor", None),
            P(None, "tensor"),
            P("tensor", None),
        ),
        check_vma=False,
    )
```

profile of v0, /device:TPU:0, one launch (start us, length us, event | category | flops | bytes accessed | tf_op | source)
XLA Modules:
  0.0 3904.8 jit_solution(12399641378816180243)
XLA Ops:
  41.3 150.3 %all-gather.6.cloned.1.call-done = bf16[1,4096,1024]{1,2,0:T(8,128)(2,1)} async-done(((bf16[1,1024,1024]{1,2,0:T(8,128)(2,1)}), bf16[1,4096,1024]{1,2,0:T(8,128)(2,1)}) %all-gather.6.cloned.1.call-update) | async-done | bytes 8388624 | tf_op jit(solution)/shard_map/all_gather | solution.py:170
  217.1 409.5 %while.38 = (s32[]{:T(128)}, bf16[8,1,512,4,64]{2,4,3,1,0:T(8,128)(2,1)}, f32[8,1,4,512]{3,2,1,0:T(4,128)}, s32[8]{0:T(128)S(1)}, s32[1,4096]{1,0:T(1,128)S(1)},...) while((s32[]{:T(128)}, ...), condition=%wide.region_16.17_spmd, body=%wide.region_13.16_spmd.sunk | while | flops 2250373120 | bytes 122247400 | solution.py:99
  251.1 17.0 fusion.336
  302.2 16.9 fusion.336
  353.3 17.0 fusion.336
  404.4 16.9 fusion.336
  455.6 17.0 fusion.336
  506.7 17.0 fusion.336
  557.8 17.0 fusion.336
  608.9 16.9 fusion.336
  640.0 278.6 %reduce-scatter.10.cloned.1.call-done = f32[1,1024,1024]{1,2,0:T(8,128)} async-done(((f32[1,4096,1024]{1,2,0:T(8,128)}), f32[1,1024,1024]{1,2,0:T(8,128)}) %reduce-scatter.10.cloned.1.call-update) | async-done | bytes 4194320 | tf_op jit(solution)/shard_map/reduce_scatter | solution.py:182
  932.2 149.9 %all-gather.12.cloned.1.call-done = bf16[1,4096,1024]{1,2,0:T(8,128)(2,1)} async-done(((bf16[1,1024,1024]{1,2,0:T(8,128)(2,1)}), bf16[1,4096,1024]{1,2,0:T(8,128)(2,1)}) %all-gather.12.cloned.1.call-update) | async-done | bytes 8388624 | tf_op jit(solution)/shard_map/all_gather | solution.py:199
  1096.9 134.5 %all-gather.10.cloned.1.call-done = bf16[1,4096,1024]{2,1,0:T(8,128)(2,1)} async-done(((bf16[1,1024,1024]{2,1,0:T(8,128)(2,1)}), bf16[1,4096,1024]{2,1,0:T(8,128)(2,1)}) %all-gather.10.cloned.1.call-update) | async-done | bytes 8388624 | tf_op jit(solution)/shard_map/all_gather | solution.py:274
  1231.4 22.5 fusion.146
  1272.8 138.8 %reduce-scatter.12.cloned.1.call-done = bf16[1,1024,1024]{1,2,0:T(8,128)(2,1)} async-done(((bf16[1,4096,1024]{1,2,0:T(8,128)(2,1)}), bf16[1,1024,1024]{1,2,0:T(8,128)(2,1)}) %reduce-scatter.12.cloned.1.call-update) | async-done | bytes 2097168 | tf_op jit(solution)/shard_map/reduce_scatter | solution.py:281
  1426.6 150.4 %all-gather.14.cloned.1.call-done = bf16[1,4096,1024]{1,2,0:T(8,128)(2,1)} async-done(((bf16[1,1024,1024]{1,2,0:T(8,128)(2,1)}), bf16[1,4096,1024]{1,2,0:T(8,128)(2,1)}) %all-gather.14.cloned.1.call-update) | async-done | bytes 8388624 | tf_op jit(solution)/shard_map/all_gather | solution.py:287
  1584.1 1018.4 %while.39 = (s32[]{:T(128)}, f32[1,4096,4,64]{1,3,2,0:T(8,128)}, f32[1,4096,4,64]{1,3,2,0:T(8,128)}, f32[8,1,512,4,64]{2,0,4,3,1:T(8,128)}, s32[8]{0:T(128)S(1)}...) while((s32[]{:T(128)}, f32[1,4096,4,64]{1,3,2,0:T(8,128)}, ...), condition=%wide.region_25.26_spmd.clone, body=%wide.region_23.25_spmd.clone.sunk | while | flops 5502007296 | bytes 353974592 | solution.py:142
  1590.8 17.3 fusion.345
  1608.1 17.1 fusion.347
  1625.2 26.2 multiply_reduce_fusion.6
  1651.3 28.4 multiply_convert_fusion.6
  1715.6 17.3 fusion.345
  1732.9 18.6 fusion.347
  1751.4 26.2 multiply_reduce_fusion.6
  1777.6 28.4 multiply_convert_fusion.6
  1843.2 17.3 fusion.345
  1860.4 18.6 fusion.347
  1879.0 26.2 multiply_reduce_fusion.6
  1905.2 28.4 multiply_convert_fusion.6
  1970.7 17.3 fusion.345
  1988.0 18.6 fusion.347
  2006.6 26.2 multiply_reduce_fusion.6
  2032.8 28.4 multiply_convert_fusion.6
  2098.3 17.3 fusion.345
  2115.6 18.6 fusion.347
  2134.2 26.2 multiply_reduce_fusion.6
  2160.3 28.4 multiply_convert_fusion.6
  2225.9 17.3 fusion.345
  2243.2 18.6 fusion.347
  2261.8 26.2 multiply_reduce_fusion.6
  2287.9 28.4 multiply_convert_fusion.6
  2353.5 17.3 fusion.345
  2370.8 18.6 fusion.347
  2389.3 26.2 multiply_reduce_fusion.6
  2415.5 28.4 multiply_convert_fusion.6
  2481.1 17.3 fusion.345
  2498.4 18.6 fusion.347
  2516.9 26.2 multiply_reduce_fusion.6
  2543.1 28.4 multiply_convert_fusion.6
  2647.4 279.2 %while.37 = (s32[]{:T(128)}, bf16[8,1,512,4,64]{2,4,3,1,0:T(8,128)(2,1)}, s32[8]{0:T(128)S(1)}, s32[1,4096]{1,0:T(1,128)S(1)}, bf16[1,4096,4,64]{1,3,2,0:T(8,128...) while((s32[]{:T(128)}, ...), condition=%wide.region_8.9_spmd, body=%wide.region_5.8_spmd.sunk | while | flops 3298961408 | bytes 13408447 | solution.py:99
  2665.9 16.5 fusion.332
  2700.7 16.5 fusion.332
  2735.6 16.5 fusion.332
  2770.5 16.6 fusion.332
  2805.4 16.5 fusion.332
  2840.2 16.5 fusion.332
  2875.1 16.5 fusion.332
  2909.9 16.5 fusion.332
  2944.4 273.4 %reduce-scatter.6.cloned.1.call-done = f32[1,1024,1024]{1,2,0:T(8,128)} async-done(((f32[1,4096,1024]{1,2,0:T(8,128)}), f32[1,1024,1024]{1,2,0:T(8,128)}) %reduce-scatter.6.cloned.1.call-update) | async-done | bytes 4194320 | tf_op jit(solution)/shard_map/reduce_scatter | solution.py:182
  3311.7 75.9 %all-gather.8.cloned.1.call-done = bf16[1,4096,1024]{1,2,0:T(8,128)(2,1)} async-done(((bf16[1,1024,1024]{1,2,0:T(8,128)(2,1)}), bf16[1,4096,1024]{1,2,0:T(8,128)(2,1)}) %all-gather.8.cloned.1.call-update) | async-done | bytes 8388624 | tf_op jit(solution)/shard_map/all_gather | solution.py:199
  3387.6 25.6 convert_bitcast_fusion.1
  3413.3 81.4 %all-reduce.7.cloned.1.call-done = (bf16[3,1024,256]{1,2,0:T(8,128)(2,1)}, bf16[256,1024]{1,0:T(8,128)(2,1)}, bf16[1024,1024]{1,0:T(8,128)(2,1)}, bf16[1024,1024]{1,0:T(8,128)(2,1)}) async-done(((bf16[3,1024,256]{1,2,0:T(8,128)(2,1)}, bf16[256,1024]{1,0:T(8,128)(2,1)}, bf16[1024,1024]{1,0:T(8,128)(2,1)}, bf16[1024,1024]{1,0:T(8,128)(2,1)}), (bf16[3,1024,256]{1,2,0:T(8,128)(2,1)}, ...) | async-done | bytes 6291472 | tf_op jit(solution)/shard_map/psum | solution.py:339
  3516.9 218.1 %all-reduce.5.cloned.1.call-done = (f32[1024,1024]{0,1:T(8,128)}, f32[1024,1024]{0,1:T(8,128)}, f32[256,4096]{1,0:T(8,128)}) async-done(((f32[1024,1024]{0,1:T(8,128)}, f32[1024,1024]{0,1:T(8,128)}, f32[256,4096]{1,0:T(8,128)}), (f32[1024,1024]{0,1:T(8,128)}, f32[1024,1024]{0,1:T(8,128)}, f32[256,4096]{1,0:T(8,128)})) %all-reduce.5.cloned.1.call-update) | async-done | bytes 12582928 | tf_op jit(solution)/shard_map/psum | solution.py:335
  3745.7 135.8 %reduce-scatter.8.cloned.1.call-done = bf16[1,1024,1024]{1,2,0:T(8,128)(2,1)} async-done(((bf16[1,4096,1024]{1,2,0:T(8,128)(2,1)}), bf16[1,1024,1024]{1,2,0:T(8,128)(2,1)}) %reduce-scatter.8.cloned.1.call-update) | async-done | bytes 2097168 | tf_op jit(solution)/shard_map/reduce_scatter | solution.py:252
  (399 shorter events, 1031.1 us)
Async XLA Ops:
  7.2 1074.9 %copy-start = (bf16[1024,1024]{1,0:T(8,128)(2,1)S(1)}, bf16[1024,1024]{1,0:T(8,128)(2,1)}, u32[]{:S(2)}) copy-start(bf16[1024,1024]{1,0:T(8,128)(2,1)} %param.27) | copy-start | bytes 6291460
  7.2 184.5 %all-gather.6.cloned.1.call-start = ((), (), s32[]{:S(2)}) async-start(), calls=%async_computation.5 | async-start | bytes 10485760 | tf_op jit(solution)/shard_map/all_gather | solution.py:170
  9.0 12.1 copy-start.40
  9.0 4.9 copy-start.46
  9.0 4.9 copy-start.49
  16.5 11.6 copy-start.32
  19.0 9.1 copy-start.36
  19.0 9.1 copy-start.34
  19.1 9.0 copy-start.41
  19.1 9.0 copy-start.43
  28.1 5.8 copy-start.2
  34.0 5.3 copy-start.51
  39.2 879.4 %reduce-scatter.10.cloned.1.call-start = ((), (), s32[]{:S(2)}) async-start(), calls=%async_computation.10 | async-start | bytes 20971520 | tf_op jit(solution)/shard_map/reduce_scatter | solution.py:182
  41.3 170.6 %copy-start.19 = (f32[4096,32]{0,1:T(8,128)}, f32[4096,32]{0,1:T(8,128)S(1)}, u32[]{:S(2)}) copy-start(f32[4096,32]{0,1:T(8,128)S(1)} %get-tuple-element.309) | copy-start | bytes 1572868
  41.3 170.6 %copy-start.21 = (f32[4096,32]{0,1:T(8,128)}, f32[4096,32]{0,1:T(8,128)S(1)}, u32[]{:S(2)}) copy-start(f32[4096,32]{0,1:T(8,128)S(1)} %get-tuple-element.310) | copy-start | bytes 1572868
  201.8 4.5 copy-start.16
  220.1 15.9 copy-start.3
  271.2 15.9 copy-start.3
  322.3 16.0 copy-start.3
  373.4 15.9 copy-start.3
  424.6 16.0 copy-start.3
  475.7 16.0 copy-start.3
  526.8 15.9 copy-start.3
  577.9 16.0 copy-start.3
  626.6 5.1 copy-start.25
  639.9 442.1 %all-gather.12.cloned.1.call-start = ((), (), s32[]{:S(2)}) async-start(), calls=%async_computation.11 | async-start | bytes 10485760 | tf_op jit(solution)/shard_map/all_gather | solution.py:199
  931.5 299.9 %all-gather.10.cloned.1.call-start = ((), (), s32[]{:S(2)}) async-start(), calls=%async_computation.9 | async-start | bytes 10485760 | tf_op jit(solution)/shard_map/all_gather | solution.py:274
  932.1 479.6 %reduce-scatter.12.cloned.1.call-start = ((), (), s32[]{:S(2)}) async-start(), calls=%async_computation.12 | async-start | bytes 10485760 | tf_op jit(solution)/shard_map/reduce_scatter | solution.py:281
  1268.8 308.2 %all-gather.14.cloned.1.call-start = ((), (), s32[]{:S(2)}) async-start(), calls=%async_computation.13 | async-start | bytes 10485760 | tf_op jit(solution)/shard_map/all_gather | solution.py:287
  1411.7 5.5 copy-start.7
  1411.7 5.9 copy-start.13
  1417.6 6.7 copy-start.14
  1426.5 1512.1 %reduce-scatter.14.cloned.1.call-start = ((), (), s32[]{:S(2)}) async-start(), calls=%async_computation.14 | async-start | bytes 10485760 | tf_op jit(solution)/shard_map/reduce_scatter | solution.py:310
  1679.8 11.1 copy-start.1
  1806.0 11.1 copy-start.1
  1933.6 11.1 copy-start.1
  2061.2 11.1 copy-start.1
  2188.8 11.1 copy-start.1
  2316.4 11.1 copy-start.1
  2443.9 11.1 copy-start.1
  2571.5 11.1 copy-start.1
  2602.5 5.0 copy-start.20
  2602.6 5.0 copy-start.22
  2613.6 5.5 copy-start.23
  2645.7 572.1 %reduce-scatter.6.cloned.1.call-start = ((), (), s32[]{:S(2)}) async-start(), calls=%async_computation.6 | async-start | bytes 20971520 | tf_op jit(solution)/shard_map/reduce_scatter | solution.py:182
  2938.5 5.9 copy-start.37
  2938.5 279.4 %copy-start.35 = (f32[1024]{0:T(1024)S(1)}, f32[1024]{0:T(1024)}, u32[]{:S(2)}) copy-start(f32[1024]{0:T(1024)} %copy-done.34) | copy-start | bytes 12292
  2938.5 449.1 %all-gather.8.cloned.1.call-start = ((), (), s32[]{:S(2)}) async-start(), calls=%async_computation.7 | async-start | bytes 10485760 | tf_op jit(solution)/shard_map/all_gather | solution.py:199
  3217.9 6.9 copy-start.10
  3217.9 7.1 copy-start.11
  3217.9 8.7 copy-start.15
  3224.2 12.9 copy-start.8
  3237.1 257.6 %all-reduce.7.cloned.1.call-start = ((), (), s32[]{:S(2)}) async-start(), calls=%async_computation.16 | async-start | bytes 12582912 | tf_op jit(solution)/shard_map/psum | solution.py:339
  3237.1 38.4 slice-start
  3252.5 16.3 copy-start.18
  3252.5 23.0 slice-start.1
  3268.7 6.8 copy-start.27
  3268.7 6.8 copy-start.28
  3268.8 6.8 copy-start.29
  3283.7 451.2 %all-reduce.5.cloned.1.call-start = ((), (), s32[]{:S(2)}) async-start(), calls=%async_computation.15 | async-start | bytes 25165824 | tf_op jit(solution)/shard_map/psum | solution.py:335
  3288.5 10.5 copy-start.42
  3288.5 10.5 copy-start.44
  3311.7 569.9 %reduce-scatter.8.cloned.1.call-start = ((), (), s32[]{:S(2)}) async-start(), calls=%async_computation.8 | async-start | bytes 10485760 | tf_op jit(solution)/shard_map/reduce_scatter | solution.py:252
  3508.0 4.4 copy-start.50
  (17 other events, 52.8 us)
Sparse Core Ops, SparseCore 0:
  39.3 152.3 all-gather.5
  640.1 278.4 reduce-scatter.9
  931.7 150.3 all-gather.11
  1083.5 147.8 all-gather.9
  1268.9 142.6 reduce-scatter.11
  1426.6 150.3 all-gather.13
  2645.9 142.6 reduce-scatter.13
  2938.6 279.1 reduce-scatter.5
  3237.2 150.3 all-gather.7
  3391.6 102.9 all-reduce.6
  3502.8 232.1 all-reduce.4
  3737.3 144.2 reduce-scatter.7
where the time goes:
time: 3920 us; the launch traced here: 3900 us
  waiting for transfers between devices  1790 us (46%)
  matrix products  1350 us (34%)
  other arithmetic  496 us (13%)
  local copies, waits for them, and re-layouts  217 us (6%)
    reduce_scatter x2, waiting for transfers between devices, front_half(): lax.psum_scatter(head_terms, 'tensor', scatter_dimension=1, tiled=True)  552 us
    dot_general x16, matrix products, one_block(): jnp.einsum('rhqk,rkhe->rqhe', probs_low, value_low, preferred_element_typ...  268 us
    dot_general x16, matrix products, block_scores(): jnp.einsum('rqhe,rkhe->rhqk', query_block, key_rot, preferred_element_typ...  266 us
    convert_element_type x8, other arithmetic, one_block(): grad_scores = (prob_rows * (grad_probs - row_delta)).astype(jnp.bfloat16)  227 us
    all_gather x2, waiting for transfers between devices, feed_half(): ffn_all = lax.all_gather(ffn_low, 'tensor', axis=1, tiled=True)  226 us
    psum x1, waiting for transfers between devices, on_device(): lax.psum((grad_skip_in, grad_skip_res, grad_ada), ('dp', 'tensor'))  218 us
    dot_general x8, matrix products, one_block(): jnp.einsum('rqhe,rkhe->rhqk', grad_block, value_low, preferred_element_ty...  209 us
    all_gather x1, waiting for transfers between devices, on_device(): lax.all_gather(grad_hidden.astype(jnp.bfloat16), 'tensor', axis=1, tiled=...  150 us
  transfers between devices with their start and end apart: 12, of which 11 were waited for; matrix products, arithmetic and copies ran while one was open for 11% of the time, Pallas kernels for 0%

commit v1 on v0

v1 whole, which is shorter than its diff:
```python
import functools
import math

import jax
import jax.numpy as jnp
from jax import lax
from jax.experimental import pallas as pl
from jax.experimental.pallas import tpu as pltpu
from jax.sharding import PartitionSpec as P

HEAD_DIM = 64
LANES = 128
MASKED = -1e30
LOG2E = math.log2(math.e)
MIB = 2**20
BF = jnp.bfloat16
F32 = jnp.float32
norm_epsilon = 1e-06
NT = (((1,), (1,)), ((), ()))
TN = (((0,), (0,)), ((), ()))


def stored_block(block, own, per_part):
    shift = per_part.bit_length() - 1
    part = lax.shift_right_logical(block, shift)
    return ((part ^ own) << shift) | (block & (per_part - 1))


def swap_halves(values):
    lane = lax.broadcasted_iota(jnp.int32, values.shape, 1)
    return jnp.where(lane % 64 < 32, pltpu.roll(values, 96, 1), pltpu.roll(values, 32, 1))


def project_kernel(normed_ref, weight_ref, cos_ref, sin_ref, out_ref, *, pairs):
    normed = normed_ref[...]
    cosine = cos_ref[...]
    sine = sin_ref[...]
    width = pairs * LANES
    for kind in range(3):
        weight = weight_ref[kind * width : (kind + 1) * width, :]
        part = lax.dot_general(normed, weight, NT, preferred_element_type=F32)
        for pair in range(pairs):
            cut = part[:, pair * LANES : (pair + 1) * LANES]
            if kind < 2:
                cut = cut * cosine + swap_halves(cut) * sine
            if kind == 0:
                cut = cut * (LOG2E * HEAD_DIM**-0.5)
            out_ref[pair * 3 + kind] = cut.astype(BF)


def project(normed_all, weight, cosine, sine, pairs):
    length, depth = normed_all.shape
    rows = 512
    return pl.pallas_call(
        functools.partial(project_kernel, pairs=pairs),
        grid=(length // rows,),
        in_specs=[
            pl.BlockSpec((rows, depth), lambda i: (i, 0)),
            pl.BlockSpec(weight.shape, lambda i: (0, 0)),
            pl.BlockSpec((rows, LANES), lambda i: (i, 0)),
            pl.BlockSpec((rows, LANES), lambda i: (i, 0)),
        ],
        out_specs=pl.BlockSpec((3 * pairs, rows, LANES), lambda i: (0, i, 0)),
        out_shape=jax.ShapeDtypeStruct((3 * pairs, length, LANES), BF),
        compiler_params=pltpu.CompilerParams(vmem_limit_bytes=40 * MIB),
        name="project",
    )(normed_all, weight, cosine, sine)


def attend_kernel(
    own_ref, low_ref, high_ref, q_ref, k_ref, v_ref, qmark_ref, kmark_ref, ctx_ref, lse_ref, keys, vals,
    *, bq, bk, per_part,
):
    step = pl.program_id(0)
    length = kmark_ref.shape[0]
    own = own_ref[0]

    @pl.when(step == 0)
    def _():
        lane = lax.broadcasted_iota(jnp.int32, (512, LANES), 1)

        @pl.loop(0, length // 512)
        def _(i):
            rows = pl.ds(pl.multiple_of(i * 512, 512), 512)
            keys[rows, :LANES] = k_ref[0, rows, :]
            keys[rows, LANES:] = kmark_ref[rows, :]
            v = v_ref[0, rows, :]
            one = jnp.ones_like(v)
            vals[0, rows, :] = jnp.where(lane < 64, v, one)
            vals[1, rows, :] = jnp.where(lane < 64, one, v)

    first = lax.broadcasted_iota(jnp.int32, (bq, LANES), 1) < 64
    q = q_ref[0]
    mark = qmark_ref[...]
    zero = jnp.zeros_like(q)
    queries = (
        jnp.concatenate([jnp.where(first, q, zero), mark], axis=1),
        jnp.concatenate([jnp.where(first, zero, q), mark], axis=1),
    )

    def body(j, carry):
        rows = pl.ds(pl.multiple_of(stored_block(j, own, per_part // bk) * bk, bk), bk)
        block = keys[rows, :]
        new = []
        for head in range(2):
            peak, total = carry[head]
            scores = lax.dot_general(queries[head], block, NT, preferred_element_type=F32)
            higher = jnp.maximum(peak, jnp.max(scores, axis=1, keepdims=True))
            weights = jnp.exp2(scores - higher).astype(BF)
            total = total * jnp.exp2(peak - higher) + jnp.dot(
                weights, vals[head, rows, :], preferred_element_type=F32
            )
            new.append((higher, total))
        return tuple(new)

    init = (jnp.full((bq, 1), -3e38, F32), jnp.zeros((bq, LANES), F32))
    (peak_a, sum_a), (peak_b, sum_b) = lax.fori_loop(low_ref[step], high_ref[step], body, (init, init))
    weight_sum = pltpu.roll(jnp.where(first, sum_b, sum_a), 64, 1)
    ctx_ref[0] = (jnp.where(first, sum_a, sum_b) / weight_sum).astype(BF)
    lse_ref[...] = jnp.where(first, peak_a, peak_b) + jnp.log2(weight_sum)


def attend(qkv, pair, qmark, kmark, own, low, high, bq, bk, per_part):
    length = qmark.shape[0]
    row = lambda i, *_: (i, 0)
    whole = lambda i, *_: (0, 0)
    return pl.pallas_call(
        functools.partial(attend_kernel, bq=bq, bk=bk, per_part=per_part),
        grid_spec=pltpu.PrefetchScalarGridSpec(
            num_scalar_prefetch=3,
            grid=(length // bq,),
            in_specs=[
                pl.BlockSpec((1, bq, LANES), lambda i, *_: (3 * pair, i, 0)),
                pl.BlockSpec((1, length, LANES), lambda i, *_: (3 * pair + 1, 0, 0)),
                pl.BlockSpec((1, length, LANES), lambda i, *_: (3 * pair + 2, 0, 0)),
                pl.BlockSpec((bq, LANES), row),
                pl.BlockSpec((length, LANES), whole),
            ],
            out_specs=[
                pl.BlockSpec((1, bq, LANES), lambda i, *_: (i // (per_part // bq), i % (per_part // bq), 0)),
                pl.BlockSpec((bq, LANES), row),
            ],
            scratch_shapes=[pltpu.VMEM((length, 2 * LANES), BF), pltpu.VMEM((2, length, LANES), BF)],
        ),
        out_shape=[
            jax.ShapeDtypeStruct((length // per_part, per_part, LANES), BF),
            jax.ShapeDtypeStruct((length, LANES), F32),
        ],
        compiler_params=pltpu.CompilerParams(
            dimension_semantics=("arbitrary",), vmem_limit_bytes=48 * MIB
        ),
        cost_estimate=pl.CostEstimate(
            flops=int(0.9 * 4 * length * length * LANES), bytes_accessed=8 * length * LANES, transcendentals=length * length
        ),
        name="attend",
    )(own, low, high, qkv, qkv, qkv, qmark, kmark)


def three_parts(value):
    high = value.astype(BF).astype(F32)
    rest = value - high
    middle = rest.astype(BF).astype(F32)
    return high, middle, (rest - middle).astype(BF).astype(F32)


def attend_back_kernel(
    own_ref, low_ref, high_ref, q_ref, k_ref, v_ref, do_ref, ctx_ref, lse_ref, qmark_ref, kmark_ref, cos_ref,
    sin_ref, out_ref, keys, vals, key_heads, query_heads, grad_heads, dq_sum,
    *, bq, bk, utt, per_part,
):
    length = kmark_ref.shape[0]
    own = own_ref[0]
    pb = 512
    lane = lax.broadcasted_iota(jnp.int32, (pb, LANES), 1)
    first = lane < 64

    @pl.loop(0, length // pb)
    def _(i):
        rows = pl.ds(pl.multiple_of(i * pb, pb), pb)
        at, within = i // (per_part // pb), pl.ds(pl.multiple_of(i % (per_part // pb) * pb, pb), pb)
        k = k_ref[0, rows, :]
        zero = jnp.zeros_like(k)
        mark = kmark_ref[rows, :]
        keys[rows, :LANES] = k
        keys[rows, LANES:] = mark
        vals[rows, :LANES] = v_ref[0, rows, :]
        vals[rows, LANES:] = mark
        q = q_ref[0, rows, :]
        grad = do_ref[at, within, :]
        qmark = qmark_ref[rows, :].astype(F32)
        lse = lse_ref[rows, :]
        product = grad.astype(F32) * ctx_ref[at, within, :].astype(F32)
        for head in range(2):
            mine = first if head == 0 else jnp.logical_not(first)
            key_heads[head, rows, :] = jnp.where(mine, k, zero)
            query_heads[head, rows, :LANES] = jnp.where(mine, q, zero)
            grad_heads[head, rows, :LANES] = jnp.where(mine, grad, zero)
            high, middle, low = three_parts(-lse[:, 64 * head : 64 * head + 1])
            query_heads[head, rows, LANES:] = jnp.where(
                lane == utt, high, jnp.where(lane == utt + 1, middle, jnp.where(lane == utt + 2, low, qmark))
            ).astype(BF)
            delta = jnp.sum(jnp.where(mine, product, 0.0), axis=1, keepdims=True)
            high, middle, low = three_parts(-delta)
            grad_heads[head, rows, LANES:] = jnp.where(
                lane == utt, high, jnp.where(lane == utt + 1, middle, jnp.where(lane == utt + 2, low, 0.0))
            ).astype(BF)
        dq_sum[rows, :] = jnp.zeros((pb, LANES), F32)

    @pl.loop(0, length // bk)
    def _(j):
        key_rows = pl.ds(pl.multiple_of(j * bk, bk), bk)
        key_block = keys[key_rows, :]
        value_block = vals[key_rows, :]

        def body(i, carry):
            dk, dv = carry
            rows = pl.ds(pl.multiple_of(stored_block(i, own, per_part // bq) * bq, bq), bq)
            dq = dq_sum[rows, :]
            for head in range(2):
                query = query_heads[head, rows, :]
                grad = grad_heads[head, rows, :]
                probs = jnp.exp2(lax.dot_general(key_block, query, NT, preferred_element_type=F32))
                pulled = lax.dot_general(value_block, grad, NT, preferred_element_type=F32)
                grad_scores = (probs * pulled).astype(BF)
                dv = dv + jnp.dot(probs.astype(BF), grad[:, :LANES], preferred_element_type=F32)
                dk = dk + jnp.dot(grad_scores, query[:, :LANES], preferred_element_type=F32)
                dq = dq + lax.dot_general(
                    grad_scores, key_heads[head, key_rows, :], TN, preferred_element_type=F32
                )
            dq_sum[rows, :] = dq
            return dk, dv

        zero = jnp.zeros((bk, LANES), F32)
        dk, dv = lax.fori_loop(low_ref[j], high_ref[j], body, (zero, zero))
        at, within = j // (per_part // bk), pl.ds(pl.multiple_of(j % (per_part // bk) * bk, bk), bk)
        out_ref[at, 2, within, :] = dv.astype(BF)
        dk = dk * (1.0 / LOG2E)
        out_ref[at, 1, within, :] = (dk * cos_ref[key_rows, :] - swap_halves(dk) * sin_ref[key_rows, :]).astype(BF)

    @pl.loop(0, length // pb)
    def _(i):
        rows = pl.ds(pl.multiple_of(i * pb, pb), pb)
        at, within = i // (per_part // pb), pl.ds(pl.multiple_of(i % (per_part // pb) * pb, pb), pb)
        dq = dq_sum[rows, :] * HEAD_DIM**-0.5
        out_ref[at, 0, within, :] = (dq * cos_ref[rows, :] - swap_halves(dq) * sin_ref[rows, :]).astype(BF)


def attend_back(
    qkv, pair, grad, ctx, lse, qmark, kmark, cosine, sine, own, low, high, bq, bk, utt, per_part
):
    length = qmark.shape[0]
    in_smem = pl.BlockSpec(memory_space=pltpu.SMEM)
    whole = pl.BlockSpec((length, LANES), lambda i: (0, 0))
    parts = length // per_part
    by_part = pl.BlockSpec((parts, per_part, LANES), lambda i: (0, 0, 0))
    cut = lambda kind: pl.BlockSpec((1, length, LANES), lambda i: (3 * pair + kind, 0, 0))
    wide = pltpu.VMEM((length, 2 * LANES), BF)
    return pl.pallas_call(
        functools.partial(attend_back_kernel, bq=bq, bk=bk, utt=utt, per_part=per_part),
        grid=(1,),
        in_specs=[in_smem] * 3 + [cut(0), cut(1), cut(2)] + [by_part] * 2 + [whole] * 5,
        out_specs=pl.BlockSpec((parts, 3, per_part, LANES), lambda i: (0, 0, 0, 0)),
        out_shape=jax.ShapeDtypeStruct((parts, 3, per_part, LANES), BF),
        scratch_shapes=[
            wide,
            wide,
            pltpu.VMEM((2, length, LANES), BF),
            pltpu.VMEM((2, length, 2 * LANES), BF),
            pltpu.VMEM((2, length, 2 * LANES), BF),
            pltpu.VMEM((length, LANES), F32),
        ],
        compiler_params=pltpu.CompilerParams(vmem_limit_bytes=56 * MIB),
        cost_estimate=pl.CostEstimate(
            flops=int(0.9 * 10 * length * length * LANES), bytes_accessed=30 * length * LANES, transcendentals=length * length
        ),
        name="attend_back",
    )(own, low, high, qkv, qkv, qkv, grad, ctx, lse, qmark, kmark, cosine, sine)


def frame_marks(lengths, places, utt):
    ends = jnp.cumsum(lengths)
    starts = ends - lengths
    segment = jnp.sum((places[:, None] >= ends[None, :]).astype(jnp.int32), axis=1, dtype=jnp.int32)
    member = segment[:, None] == jnp.arange(utt, dtype=jnp.int32)[None, :]
    offsets = jnp.sum(jnp.where(member, starts[None, :], 0), axis=1, dtype=jnp.int32)
    return segment, member, offsets


def block_ranges(lengths, blocks, size, other):
    ends = jnp.cumsum(lengths)
    starts = ends - lengths
    at_first = blocks * size
    at_last = at_first + (size - 1)
    index = jnp.arange(lengths.shape[0], dtype=jnp.int32)
    seg_first = jnp.sum((at_first[:, None] >= ends[None]).astype(jnp.int32), axis=1)
    seg_last = jnp.sum((at_last[:, None] >= ends[None]).astype(jnp.int32), axis=1)
    low = jnp.sum(jnp.where(index[None] == seg_first[:, None], starts[None], 0), axis=1)
    high = jnp.sum(jnp.where(index[None] == seg_last[:, None], ends[None], 0), axis=1)
    return (low // other).astype(jnp.int32), ((high + other - 1) // other).astype(jnp.int32)


def feed_kernel(
    x_own_ref, x_other_ref, cot_own_ref, cot_other_ref, up_ref, down_ref,
    out_own_ref, out_other_ref, gin_own_ref, gin_other_ref, gup_ref, gdown_ref, out_sum, gin_sum,
):
    step = pl.program_id(0)
    last = pl.num_programs(0) - 1
    up = up_ref[...]
    down = down_ref[...]
    root = math.sqrt(2.0 / math.pi)
    gup = gdown = None
    for side, (x_ref, cot_ref) in enumerate(((x_own_ref, cot_own_ref), (x_other_ref, cot_other_ref))):
        x = x_ref[...]
        cot = cot_ref[...]
        before = lax.dot_general(x, up, NT, preferred_element_type=F32)
        grad_act = lax.dot_general(cot, down, NT, preferred_element_type=F32)
        square = before * before
        bend = jnp.tanh(root * before * (1.0 + 0.044715 * square))
        half = 0.5 * (1.0 + bend)
        activated = (before * half).astype(BF)
        slope = half + 0.5 * before * (1.0 - bend * bend) * (root + (3.0 * 0.044715 * root) * square)
        grad_before = (grad_act * slope).astype(BF)
        out = jnp.dot(activated, down, preferred_element_type=F32)
        gin = jnp.dot(grad_before, up, preferred_element_type=F32)
        gd = lax.dot_general(activated, cot, TN, preferred_element_type=F32)
        gu = lax.dot_general(grad_before, x, TN, preferred_element_type=F32)
        gup = gu if side == 0 else gup + gu
        gdown = gd if side == 0 else gdown + gd

        @pl.when(step == 0)
        def _():
            out_sum[side] = out
            gin_sum[side] = gin

        @pl.when(step > 0)
        def _():
            out_sum[side] += out
            gin_sum[side] += gin

    gup_ref[...] = gup.astype(BF)
    gdown_ref[...] = gdown.astype(BF)

    @pl.when(step == last)
    def _():
        out_own_ref[...] = out_sum[0]
        out_other_ref[...] = out_sum[1].astype(BF)
        gin_own_ref[...] = gin_sum[0]
        gin_other_ref[...] = gin_sum[1].astype(BF)


def feed(x_own, x_other, cot_own, cot_other, up, down):
    frames, depth = x_own.shape
    units = up.shape[0]
    chunk = 256
    whole = pl.BlockSpec((frames, depth), lambda j: (0, 0))
    cut = pl.BlockSpec((chunk, depth), lambda j: (j, 0))
    shape = lambda *s: jax.ShapeDtypeStruct(*s)
    return pl.pallas_call(
        feed_kernel,
        grid=(units // chunk,),
        in_specs=[whole] * 4 + [cut] * 2,
        out_specs=[whole] * 4 + [cut] * 2,
        out_shape=[
            shape((frames, depth), F32),
            shape((frames, depth), BF),
            shape((frames, depth), F32),
            shape((frames, depth), BF),
            shape((units, depth), BF),
            shape((units, depth), BF),
        ],
        scratch_shapes=[pltpu.VMEM((2, frames, depth), F32), pltpu.VMEM((2, frames, depth), F32)],
        compiler_params=pltpu.CompilerParams(
            dimension_semantics=("arbitrary",), vmem_limit_bytes=60 * MIB
        ),
        cost_estimate=pl.CostEstimate(
            flops=24 * frames * depth * units, bytes_accessed=40 * frames * depth, transcendentals=2 * frames * units
        ),
        name="feed",
    )(x_own, x_other, cot_own, cot_other, up, down)


SUM_WIDTH = 256


def sum_kernel(x_ref, out_ref, held, first_in, half_in, sems, *, rows_all, parts):
    d = lax.axis_index("dp")
    z = lax.axis_index("tensor")
    total = x_ref.shape[0]
    half = total // 2
    core = d % 2
    dp_bits = [1 << k for k in range(1, rows_all.bit_length() - 1)]
    z_bits = [1 << k for k in reversed(range(parts.bit_length() - 1))]
    steps = [
        [("dp", bit) for bit in dp_bits] + [("tensor", bit) for bit in z_bits],
        [("dp", bit) for bit in reversed(dp_bits)] + [("tensor", bit) for bit in z_bits],
    ]

    def device(axis, bit):
        return (d ^ bit, z) if axis == "dp" else (d, z ^ bit)

    barrier = pltpu.get_barrier_semaphore()
    everyone = [("dp", 1)] + steps[0]
    for axis, bit in everyone:
        pl.semaphore_signal(barrier, inc=1, device_id=device(axis, bit), device_id_type=pl.DeviceIdType.MESH)
    pl.semaphore_wait(barrier, len(everyone))

    def rows(start, size):
        return pl.ds(pl.multiple_of(start, 16), size)

    def send(source, target, at, axis, bit):
        copy = pltpu.make_async_remote_copy(
            src_ref=source,
            dst_ref=target,
            send_sem=sems.at[2 * at],
            recv_sem=sems.at[2 * at + 1],
            device_id=device(axis, bit),
            device_id_type=pl.DeviceIdType.MESH,
        )
        copy.start()
        return copy

    def add_into(target, start, one, one_at, two, size):
        step = min(size, 128)

        @pl.loop(0, size // step)
        def _(i):
            a = one[rows(one_at + i * step, step), :].astype(F32)
            b = two[pl.ds(pl.multiple_of(i * step, step), step), :].astype(F32)
            target[rows(start + i * step, step), :] = (a + b).astype(BF)

    at = 0
    copy = send(x_ref.at[rows((1 - core) * half, half), :], first_in, at, "dp", 1)
    copy.wait()
    add_into(held, 0, x_ref, core * half, first_in, half)
    at += 1

    quarter = half // 2
    starts = [0, quarter]
    size = quarter
    begin = [0, quarter]
    kept = []
    for step in range(len(steps[0])):
        size //= 2
        copies = []
        for side in range(2):
            axis, bit = steps[side][step]
            upper = ((d if axis == "dp" else z) // bit) % 2
            keep = starts[side] + upper * size
            away = starts[side] + (1 - upper) * size
            target = half_in.at[pl.ds(begin[side], size), :]
            copies.append(send(held.at[rows(away, size), :], target, at, axis, bit))
            starts[side] = keep
            at += 1
        for side in range(2):
            copies[side].wait()
            add_into(held, starts[side], held, starts[side], half_in.at[pl.ds(begin[side], size), :], size)
            begin[side] += size
        kept.append((list(starts), size))

    def settle(start, n):
        out_ref[rows(core * half + start, n), :] = held[rows(start, n), :]

    for side in range(2):
        settle(starts[side], size)
    for step in reversed(range(len(steps[0]))):
        copies = []
        for side in range(2):
            axis, bit = steps[side][step]
            mine = out_ref.at[rows(core * half + starts[side], size), :]
            copies.append(send(mine, mine, at, axis, bit))
            at += 1
        for side in range(2):
            copies[side].wait()
        starts = kept[step - 1][0] if step > 0 else [0, quarter]
        size *= 2
    mine = out_ref.at[rows(core * half, half), :]
    send(mine, mine, at, "dp", 1).wait()


def sum_everywhere(value, rows_all, parts):
    total, width = value.shape
    stages = rows_all.bit_length() + parts.bit_length() - 3
    whole = pl.BlockSpec(memory_space=pltpu.VMEM)
    return pl.pallas_call(
        functools.partial(sum_kernel, rows_all=rows_all, parts=parts),
        in_specs=[whole],
        out_specs=whole,
        out_shape=jax.ShapeDtypeStruct(value.shape, BF),
        scratch_shapes=[
            pltpu.VMEM((total // 2, width), BF),
            pltpu.VMEM((total // 2, width), BF),
            pltpu.VMEM((total // 2, width), BF),
            pltpu.SemaphoreType.DMA((2 * (2 + 4 * stages),)),
        ],
        compiler_params=pltpu.CompilerParams(
            collective_id=0, has_side_effects=True, vmem_limit_bytes=32 * MIB
        ),
        name="sum_everywhere",
    )(value)


def norm_parts(hidden):
    center = hidden - jnp.mean(hidden, axis=-1, keepdims=True)
    inverse = lax.rsqrt(jnp.mean(center * center, axis=-1, keepdims=True) + norm_epsilon)
    return center * inverse, inverse


def norm_pull(unit, inverse, grad, scale):
    pulled = grad * (1.0 + scale)
    return (
        pulled
        - jnp.mean(pulled, axis=-1, keepdims=True)
        - unit * jnp.mean(pulled * unit, axis=-1, keepdims=True)
    ) * inverse


def dot(a, b, dims=(((1,), (0,)), ((), ()))):
    return lax.dot_general(a, b, dims, preferred_element_type=F32)


def exact(pattern, a, b):
    return jnp.einsum(pattern, a, b, precision=lax.Precision.HIGHEST)


def on_device(
    inputs, skip_input, lengths, time_steps, w_skip_in, w_skip_res, w_ada, w_qkv, w_out, w_up, w_down, cotangent
):
    parts = lax.axis_size("tensor")
    rows_all = lax.axis_size("dp")
    half = parts // 2
    columns = rows_all // 2
    d = lax.axis_index("dp")
    z = lax.axis_index("tensor")
    core, column = d % 2, d // 2
    stays = z // half == core
    part = core * half + z % half
    inputs, skip_input, cotangent = inputs[0], skip_input[0], cotangent[0]
    frames, depth = inputs.shape
    length = frames * parts
    heads_here = w_out.shape[0] // HEAD_DIM
    pairs = heads_here * HEAD_DIM // LANES
    utt = lengths.shape[1]
    both = ("dp", "tensor")

    def relocate(value):
        pattern = [
            (i * parts + j, ((i // 2) * 2 + j // half) * parts + (i % 2) * half + j % half)
            for i in range(rows_all)
            for j in range(parts)
            if i % 2 != j // half
        ]
        return jnp.where(stays, value, lax.ppermute(value, both, pattern))

    def partner(value, b):
        pattern = [
            (i * parts + j, (i ^ (b // half)) * parts + (j // half) * half + ((j % half) ^ (b % half)))
            for i in range(rows_all)
            for j in range(parts)
        ]
        return lax.ppermute(value, both, pattern)

    def exchange(blocks):
        return [blocks[0]] + [partner(blocks[b], b) for b in range(1, parts)]

    same_core = [[2 * i + k for i in range(columns)] for k in range(2)]

    ws = w_qkv.shape[2]
    qkv_rows = jnp.transpose(w_qkv, (0, 2, 1)).reshape(3 * ws, depth)
    per_q, per_o = 3 * ws // rows_all, ws // rows_all
    slice_head = jnp.concatenate(
        [
            lax.dynamic_slice_in_dim(qkv_rows, d * per_q, per_q, 0),
            lax.dynamic_slice_in_dim(w_out, d * per_o, per_o, 0),
        ]
    )
    head_rows = lax.all_gather(lax.all_gather(slice_head, "tensor"), "dp")
    head_rows = jnp.transpose(head_rows, (1, 0, 2, 3))
    order = part ^ jnp.arange(parts, dtype=jnp.int32)
    head_rows = jnp.take(head_rows, order, axis=0)
    w_heads = head_rows[:, :, :per_q].reshape(parts, 3 * ws, depth)
    w_out_all = head_rows[:, :, per_q:].reshape(parts, ws, depth)

    units = w_down.shape[0]
    per_u = units // rows_all
    at = core * (units // 2) + column * per_u
    slice_feed = jnp.stack(
        [
            jnp.transpose(lax.dynamic_slice_in_dim(w_up, at, per_u, 1)),
            lax.dynamic_slice_in_dim(w_down, at, per_u, 0),
        ]
    )
    feed_rows = lax.all_gather(lax.all_gather(slice_feed, "tensor", axis=1), "dp", axis=1, axis_index_groups=same_core)
    feed_rows = feed_rows.reshape(2, columns * parts * per_u, depth)

    other_lengths = partner(lengths, half)
    other_steps = partner(time_steps, half)
    lengths_work = jnp.where(stays, lengths, other_lengths)[0]
    steps_work = jnp.where(stays, time_steps, other_steps)[0]

    time_rate = jnp.exp(
        -math.log(10000.0) * (jnp.arange(w_ada.shape[0] // 2, dtype=F32) / (w_ada.shape[0] // 2))
    )

    def embed(steps):
        phases = steps.astype(F32)[:, None] * time_rate
        return jax.nn.silu(jnp.concatenate([jnp.sin(phases), jnp.cos(phases)], axis=-1)).astype(BF)

    def modulation(silu_low, member, at, wide):
        per_utterance = dot(silu_low, w_ada[:, at : at + wide])
        return exact("lu,um->lm", member.astype(F32), per_utterance)

    spot = jnp.arange(frames, dtype=jnp.int32)
    _, member_home, _ = frame_marks(lengths[0], z * frames + spot, utt)
    shift_one, scale_one = jnp.split(modulation(embed(time_steps[0]), member_home, 0, 2 * depth), 2, axis=-1)
    base_home = dot(inputs, w_skip_in) + dot(skip_input, w_skip_res)
    unit_home, _ = norm_parts(base_home)
    normed = relocate((unit_home * (1.0 + scale_one) + shift_one).astype(BF))
    base = relocate(base_home.astype(BF))
    cot = relocate(cotangent)

    silu_low = embed(steps_work)
    _, member, _ = frame_marks(lengths_work, part * frames + spot, utt)
    mods = jnp.split(modulation(silu_low, member, 0, 4 * depth), 4, axis=-1)
    across = [normed] + [partner(normed, b) for b in range(1, half)]
    blocks = across + [partner(value, half) for value in across]
    normed_all = jnp.concatenate(blocks)

    index = jnp.arange(length, dtype=jnp.int32)
    places = (part ^ (index // frames)) * frames + index % frames
    segment, _, offsets = frame_marks(lengths_work, places, utt)
    rotary_rate = jnp.exp(-math.log(10000.0) * (2.0 * jnp.arange(HEAD_DIM // 2, dtype=F32) / HEAD_DIM))
    angles = (places - offsets).astype(F32)[:, None] * rotary_rate
    cosine = jnp.tile(jnp.cos(angles), (1, 4))
    sine_half = jnp.sin(angles)
    sine = jnp.tile(jnp.concatenate([-sine_half, sine_half], axis=1), (1, 2))
    lane = jnp.arange(LANES, dtype=jnp.int32)[None, :]
    same = segment[:, None] == lane
    qmark = jnp.where((lane < utt) & jnp.logical_not(same), MASKED, 0.0).astype(BF)
    kmark = (same | ((lane >= utt) & (lane < utt + 3))).astype(BF)

    qkv = project(normed_all, w_heads[0], cosine, sine, pairs)

    def ranges(size, other):
        per = frames // size
        stored = jnp.arange(length // size, dtype=jnp.int32)
        natural = (part ^ (stored // per)) * per + stored % per
        return block_ranges(lengths_work, natural, size, other)

    own = part.astype(jnp.int32)[None]
    bq, bk = 512, 512
    low, high = ranges(bq, bk)
    low_back, high_back = ranges(bk, bq)
    ctx_pairs, lse_pairs, ctx_mine = [], [], []
    for pair in range(pairs):
        ctx, lse = attend(qkv, pair, qmark, kmark, own, low, high, bq, bk, frames)
        ctx_pairs.append(ctx)
        lse_pairs.append(lse)
        ctx_mine.append(exchange([ctx[b] for b in range(parts)]))
    context = jnp.concatenate(
        [ctx_mine[pair][b] for b in range(parts) for pair in range(pairs)], axis=1
    )
    w_out_work = w_out_all.reshape(parts * ws, depth)
    hidden = base.astype(F32) + dot(context, w_out_work)
    unit_two, inverse_two = norm_parts(hidden)
    ffn_in = (unit_two * (1.0 + mods[3]) + mods[2]).astype(BF)

    ffn_other = partner(ffn_in, half)
    cot_other = partner(cot, half)
    out_own, out_send, gin_own, gin_send, gup, gdown = feed(
        ffn_in, ffn_other, cot, cot_other, feed_rows[0], feed_rows[1]
    )
    grad_ffn_in = gin_own + partner(gin_send, half).astype(F32)
    block_out = hidden + out_own + partner(out_send, half).astype(F32)
    block_out = relocate(block_out.astype(BF)).astype(F32)

    grad_hidden = cot.astype(F32) + norm_pull(unit_two, inverse_two, grad_ffn_in, mods[3])
    grad_hidden_low = grad_hidden.astype(BF)
    grad_context = dot(grad_hidden_low, w_out_work, NT).astype(BF)
    grad_out = dot(context, grad_hidden_low, TN).astype(BF)
    member_wide = member.astype(F32)
    sums_two = exact("lu,lm->um", member_wide, jnp.concatenate([grad_ffn_in, grad_ffn_in * unit_two], axis=1))

    grad_out = jnp.take(grad_out.reshape(parts, 2, ws // 2, depth), order, axis=0)
    mine = lax.dynamic_slice_in_dim(grad_out, core, 1, 1)[:, 0]
    theirs = lax.dynamic_slice_in_dim(grad_out, 1 - core, 1, 1)[:, 0]
    grad_out = (mine.astype(F32) + partner(theirs, half).astype(F32)).astype(BF)

    grad_out = jnp.transpose(grad_out.reshape(parts, columns, per_o, depth), (1, 0, 2, 3))
    grad_feed = jnp.concatenate(
        [gup.reshape(columns, parts, per_u, depth), gdown.reshape(columns, parts, per_u, depth), grad_out], axis=2
    )
    grad_feed = lax.psum_scatter(grad_feed, "dp", scatter_dimension=0, axis_index_groups=same_core)
    grad_feed = lax.psum_scatter(grad_feed, "tensor", scatter_dimension=0)
    grad_feed = lax.all_gather(grad_feed, "dp", axis=0)
    grad_feed = jnp.transpose(grad_feed.reshape(columns, 2, 2 * per_u + per_o, depth), (1, 0, 2, 3)).astype(F32)
    grad_up = jnp.transpose(grad_feed[:, :, :per_u].reshape(units, depth))
    grad_down = grad_feed[:, :, per_u : 2 * per_u].reshape(units, depth)
    grad_out = grad_feed[:, :, 2 * per_u :].reshape(ws, depth)

    grad_mine = []
    for pair in range(pairs):
        cut = [
            grad_context[:, b * ws + pair * LANES : b * ws + (pair + 1) * LANES] for b in range(parts)
        ]
        grad = jnp.stack(exchange(cut))
        grads = attend_back(
            qkv, pair, grad, ctx_pairs[pair], lse_pairs[pair], qmark, kmark, cosine, sine, own,
            low_back, high_back, bq, bk, utt, frames,
        )
        grad_mine.append(grads)
    grad_heads = jnp.concatenate(
        [grad_mine[pair][:, kind].reshape(length, LANES) for kind in range(3) for pair in range(pairs)], axis=1
    )
    grad_qkv = relocate(dot(normed_all, grad_heads, TN).astype(BF))
    grad_qkv = lax.psum(grad_qkv, "dp").astype(F32).reshape(depth, 3, ws)
    grad_qkv = jnp.transpose(grad_qkv, (1, 0, 2))

    returned = [exchange([grads[b] for b in range(parts)]) for grads in grad_mine]
    grad_rows = jnp.concatenate(
        [returned[pair][b][kind] for b in range(parts) for kind in range(3) for pair in range(pairs)], axis=1
    )
    grad_normed = dot(grad_rows, w_heads.reshape(parts * 3 * ws, depth))
    unit_one, inverse_one = norm_parts(base.astype(F32))
    grad_base = (grad_hidden + norm_pull(unit_one, inverse_one, grad_normed, mods[1])).astype(BF)
    sums_one = exact("lu,lm->um", member_wide, jnp.concatenate([grad_normed, grad_normed * unit_one], axis=1))

    inputs_work = relocate(inputs)
    skips_work = relocate(skip_input)
    grad_skip = jnp.concatenate(
        [
            dot(frames_in, grad_base, TN).astype(BF)[:, k * SUM_WIDTH : (k + 1) * SUM_WIDTH]
            for frames_in in (inputs_work, skips_work)
            for k in range(depth // SUM_WIDTH)
        ]
    )
    grad_skip = sum_everywhere(grad_skip, rows_all, parts).reshape(2, depth // SUM_WIDTH, depth, SUM_WIDTH)
    grad_skip = jnp.transpose(grad_skip, (0, 2, 1, 3)).reshape(2, depth, depth).astype(F32)

    grad_base_home = relocate(grad_base)
    grad_inputs = dot(grad_base_home, w_skip_in, NT)
    grad_skips = dot(grad_base_home, w_skip_res, NT)

    steps_all = lax.all_gather(time_steps[0], "dp")
    silu_all = embed(steps_all.reshape(-1)).astype(F32)
    row_work = column * 2 + z // half
    sums = jnp.concatenate([sums_one, sums_two], axis=1)
    slots = jnp.arange(rows_all, dtype=jnp.int32)[:, None, None] == row_work
    sums_all = lax.psum(jnp.where(slots, sums[None], 0.0), both).reshape(rows_all * utt, 4 * depth)
    grad_ada = exact("ut,um->tm", silu_all, sums_all)

    return (
        block_out[None],
        grad_inputs[None],
        grad_skips[None],
        grad_skip[0],
        grad_skip[1],
        grad_ada,
        grad_qkv,
        grad_out,
        grad_up,
        grad_down,
    )


def solution(mesh):
    placed = (
        P("dp", "tensor", None),
        P("dp", "tensor", None),
        P("dp", None),
        P("dp", None),
        P(),
        P(),
        P(),
        P(None, None, "tensor"),
        P("tensor", None),
        P(None, "tensor"),
        P("tensor", None),
        P("dp", "tensor", None),
    )
    return jax.shard_map(
        on_device,
        mesh=mesh,
        in_specs=placed,
        out_specs=(
            P("dp", "tensor", None),
            P("dp", "tensor", None),
            P("dp", "tensor", None),
            P(),
            P(),
            P(),
            P(None, None, "tensor"),
            P("tensor", None),
            P(None, "tensor"),
            P("tensor", None),
        ),
        check_vma=False,
    )
```

time: 3920 us -> 1340 us (0.34)
  waiting for transfers between devices: 1790 us -> 277 us
  matrix products: 1350 us -> 87.6 us
  Pallas kernels: 0 us -> 551 us
  other arithmetic: 496 us -> 91.6 us
  starting transfers between devices: 0.5 us -> 166 us
  local copies, waits for them, and re-layouts: 217 us -> 129 us
    dot_general x87 -> x18, matrix products: 1240 us -> 87.6 us  [the longest x13 62.9 us: dot(): return lax.dot_general(a, b, dims, preferred_element_type=F32)]
    reduce_scatter x5 -> x1, waiting for transfers between devices: 827 us -> 22 us  [on_device(): grad_feed = lax.psum_scatter(grad_feed, 'tensor', scatter_dimension=0)]
    all_gather x5, waiting for transfers between devices: 661 us -> 95.3 us  [the longest x1 39.9 us: on_device(): lax.all_gather(slice_feed, 'tensor', axis=1)]
    pallas_call x0 -> x7, Pallas kernels: none -> 551 us  [the longest x1 180 us: sum_everywhere(): pl.pallas_call(functools.partial(sum_kernel, rows_all=rows_all, parts=par...]
    convert_element_type x17 -> x10, other arithmetic: 255 us -> 20.2 us  [the longest x1 5.87 us: on_device(): ffn_in = (unit_two * (1.0 + mods[3]) + mods[2]).astype(BF)]
    psum x2, waiting for transfers between devices: 299 us -> 87.1 us  [the longest x1 54.8 us: on_device(): grad_qkv = lax.psum(grad_qkv, 'dp').astype(F32).reshape(depth, 3, ws)]
    ppermute x0 -> x36, starting transfers between devices: none -> 166 us  [the longest x28 150 us: partner(): return lax.ppermute(value, both, pattern)]
    reduce_sum x18 -> x12, other arithmetic: 148 us -> 10 us  [the longest x1 5.66 us: norm_pull(): jnp.mean(pulled, axis=-1, keepdims=True)]
  transfers between devices with their start and end apart: 12 -> 45, of which waited for: 11 -> 19; matrix products, arithmetic and copies ran while one was open for 11% -> 18% of each run, Pallas kernels for 0% -> 35%
where the time goes in v1:
time: 1340 us; the launch traced here: 1350 us
  Pallas kernels  551 us (41%)
  waiting for transfers between devices  277 us (21%)
  starting transfers between devices  166 us (12%)
  local copies, waits for them, and re-layouts  129 us (10%)
  other arithmetic  91.6 us (7%)
  matrix products  87.6 us (7%)
  blocking collectives  34.1 us (3%)
  between operations  15.3 us (1%)
    pallas_call x1, Pallas kernels, sum_everywhere(): pl.pallas_call(functools.partial(sum_kernel, rows_all=rows_all, parts=par...  180 us
    pallas_call x2, Pallas kernels, attend_back(): pl.pallas_call(functools.partial(attend_back_kernel, bq=bq, bk=bk, utt=ut...  164 us
    ppermute x28, starting transfers between devices, partner(): return lax.ppermute(value, both, pattern)  150 us
    pallas_call x2, Pallas kernels, attend(): pl.pallas_call(functools.partial(attend_kernel, bq=bq, bk=bk, per_part=pe...  112 us
    pallas_call x1, Pallas kernels, feed(): pl.pallas_call(feed_kernel, grid=(units // chunk,), in_specs=[whole] * 4...  83.8 us
    ppermute x28, waiting for transfers between devices, partner(): return lax.ppermute(value, both, pattern)  72 us
    dot_general x13, matrix products, dot(): return lax.dot_general(a, b, dims, preferred_element_type=F32)  62.9 us
    psum x1, waiting for transfers between devices, on_device(): grad_qkv = lax.psum(grad_qkv, 'dp').astype(F32).reshape(depth, 3, ws)  54.8 us
  transfers between devices with their start and end apart: 45, of which 19 were waited for; matrix products, arithmetic and copies ran while one was open for 18% of the time, Pallas kernels for 35%

profile of v1, /device:TPU:0, one launch (start us, length us, event | category | flops | bytes accessed | tf_op | source)
XLA Modules:
  0.0 1351.4 jit_solution(5437390011494869764)
XLA Ops:
  15.6 27.7 %all-gather.13.cloned.1.call-done = bf16[512,1024]{1,0:T(8,128)(2,1)} async-done(((bf16[128,1024]{1,0:T(8,128)(2,1)}), bf16[512,1024]{1,0:T(8,128)(2,1)}) %all-gather.13.cloned.1.call-update) | async-done | bytes 1048592 | tf_op jit(solution)/shard_map/all_gather | solution.py:576
  46.3 4.7 fusion.112
  55.4 3.5 fusion.47
  68.9 3.1 broadcast_select_fusion.3
  76.2 39.9 %all-gather.17.cloned.1.call-done = bf16[2,512,1024]{2,1,0:T(8,128)(2,1)} async-done(((bf16[2,128,1024]{2,1,0:T(8,128)(2,1)}), bf16[2,512,1024]{2,1,0:T(8,128)(2,1)}) %all-gather.17.cloned.1.call-update) | async-done | bytes 2097168 | tf_op jit(solution)/shard_map/all_gather | solution.py:592
  118.5 9.8 fusion.46
  137.3 86.3 %collective-permute-start.4 = (bf16[1024,1024]{1,0:T(8,128)(2,1)}, bf16[1024,1024]{1,0:T(8,128)(2,1)S(1)}, u32[]{:S(2)}, u32[]{:S(2)}) collective-permute-start(bf16[1024,1024]{1,0:T(8,128)(2,1)} %broadcast_select_fusion.3), channel_id=1, source_target_pairs={{0,4},{1,5},{2,6},{3,7},{4,0},{5,1},{6,2},{7,3},{8,12},{9,13},{10,... | collective-permute-start | bytes 6291464 | tf_op jit(solution)/shard_map/ppermute | solution.py:560
  223.7 17.5 %collective-permute-start.5 = (bf16[1024,1024]{1,0:T(8,128)(2,1)}, bf16[1024,1024]{1,0:T(8,128)(2,1)S(1)}, u32[]{:S(2)}, u32[]{:S(2)}) collective-permute-start(bf16[1024,1024]{1,0:T(8,128)(2,1)} %collective-permute-done.3), channel_id=1, source_target_pairs={{0,4},{1,5},{2,6},{3,7},{4,0},{5,1},{6,2},{7,3},{8,12},{9,13},{10,... | collective-permute-start | bytes 6291464 | tf_op jit(solution)/shard_map/ppermute | solution.py:560
  244.1 3.3 broadcast_select_fusion.2.cot_own_ref
  252.8 6.1 pad_maximum_fusion.1.normed_ref
  258.9 6.0 fusion.123
  264.9 5.0 gather_fusion.1
  269.9 5.0 gather_fusion.2
  275.0 5.5 maximum_select_fusion
  280.6 3.4 copy-done.16
  284.0 11.6 project.1.q_ref.k_ref.v_ref
  298.1 50.3 %attend.2 = (bf16[4,1024,128]{2,1,0:T(8,128)(2,1)S(1)}, f32[4096,128]{1,0:T(8,128)S(1)}) custom-call(s32[1]{0:T(128)} %bitcast.2.own_ref, s32[8]{0:T(128)S(1)} %get-tuple-element.99.low_ref, s32[8]{0:T(128)S(1)} %get-tuple-element.98.high_ref, bf16[6,4096,128]{2,1,0:T(8,128)(2,1)} %copy-done.3, bf16[6,4096,128]{2,1,0:T(8,128)(2,1)} %copy-done.3, ...), custom_call_target="tpu_custom_call" | custom-call | flops 7730940928 | bytes 4194304 | tf_op jit(solution)/shard_map/attend/pallas_call | solution.py:127
  349.3 61.9 %attend.3 = (bf16[4,1024,128]{2,1,0:T(8,128)(2,1)S(1)}, f32[4096,128]{1,0:T(8,128)S(1)}) custom-call(s32[1]{0:T(128)} %bitcast.2.own_ref, s32[8]{0:T(128)S(1)} %get-tuple-element.99.low_ref, s32[8]{0:T(128)S(1)} %get-tuple-element.98.high_ref, bf16[6,4096,128]{2,1,0:T(8,128)(2,1)} %copy-done.3, bf16[6,4096,128]{2,1,0:T(8,128)(2,1)} %copy-done.3, ...), custom_call_target="tpu_custom_call" | custom-call | flops 7730940928 | bytes 4194304 | tf_op jit(solution)/shard_map/attend/pallas_call | solution.py:127
  417.2 3.1 collective-permute-done.7
  422.0 4.6 collective-permute-done.10
  426.7 5.2 collective-permute-done.11
  435.0 5.9 fusion.20.x_own_ref
  440.9 6.2 fusion.122
  447.1 83.8 %feed.1 = (f32[1024,1024]{1,0:T(8,128)}, bf16[1024,1024]{1,0:T(8,128)(2,1)}, f32[1024,1024]{1,0:T(8,128)}, bf16[1024,1024]{1,0:T(8,128)(2,1)}, bf16[2048,1024]{1,0:T(8,128)(2,1)}, /*index=5*/bf16[2048,1024]{1,0:T(8,128)(2,1)}) custom-call(bf16[1024,1024]{1,0:T(8,128)(2,1)} %fusion.20.x_own_ref, bf16[1024,1024]{1,0:T(8,128)(2,1)} %collective-permute-done.13.x_other_ref, ...), custom_call_target="tpu_custom_call" | custom-call | flops 51539607552 | bytes 41943040 | tf_op jit(solution)/shard_map/feed/pallas_call | solution.py:358
  531.5 4.1 collective-permute-done.18
  535.5 7.0 fusion.24
  542.5 5.7 fusion.118
  548.2 5.7 multiply_add_fusion
  554.0 3.8 convolution_convert_fusion
  557.7 3.6 gather_fusion
  569.4 7.4 pad_maximum_fusion
  576.9 5.4 convolution_convert_fusion.1
  585.7 4.0 slice.354
  593.0 3.5 fusion.4
  600.1 4.7 collective-permute-done.19
  604.8 4.5 collective-permute-done.21
  610.4 82.3 %attend_back.3 = bf16[4,3,1024,128]{3,2,1,0:T(8,128)(2,1)} custom-call(s32[1]{0:T(128)} %bitcast.2.own_ref, s32[8]{0:T(128)} %copy-done.9, s32[8]{0:T(128)} %copy-done.8, bf16[6,4096,128]{2,1,0:T(8,128)(2,1)} %copy-done.3, bf16[6,4096,128]{2,1,0:T(8,128)(2,1)} %copy-done.3, bf16[6,4096,128]{2,1,0:T(8,128)(2,1)} %copy-done.3, ...), custom_call_target="tpu_custom_call" | custom-call | flops 19327352832 | bytes 15728640 | tf_op jit(solution)/shard_map/attend_back/pallas_call | solution.py:258
  694.7 81.6 %attend_back.2 = bf16[4,3,1024,128]{3,2,1,0:T(8,128)(2,1)} custom-call(s32[1]{0:T(128)} %bitcast.2.own_ref, s32[8]{0:T(128)} %copy-done.9, s32[8]{0:T(128)} %copy-done.8, bf16[6,4096,128]{2,1,0:T(8,128)(2,1)} %copy-done.3, bf16[6,4096,128]{2,1,0:T(8,128)(2,1)} %copy-done.3, bf16[6,4096,128]{2,1,0:T(8,128)(2,1)} %copy-done.3, ...), custom_call_target="tpu_custom_call" | custom-call | flops 19327352832 | bytes 15728640 | tf_op jit(solution)/shard_map/attend_back/pallas_call | solution.py:258
  785.1 11.7 convolution_convert_fusion.2
  806.3 13.7 %collective-permute-done.25 = bf16[3,1024,128]{2,1,0:T(8,128)(2,1)S(1)} collective-permute-done((bf16[3,1024,128]{2,1,0:T(8,128)(2,1)S(1)}, bf16[3,1024,128]{2,1,0:T(8,128)(2,1)S(1)}, u32[]{:S(2)}, u32[]{:S(2)}) %collective-permute-start.25) | collective-permute-done | bytes 786464 | tf_op jit(solution)/shard_map/ppermute | solution.py:560
  820.1 24.3 %collective-permute-start.29 = (bf16[3,1024,128]{2,1,0:T(8,128)(2,1)S(1)}, bf16[3,1024,128]{2,1,0:T(8,128)(2,1)S(1)}, u32[]{:S(2)}, u32[]{:S(2)}) collective-permute-start(bf16[3,1024,128]{2,1,0:T(8,128)(2,1)S(1)} %get-tuple-element.63), channel_id=1, source_target_pairs={{0,5},{1,4},{2,7},{3,6},{4,1},{5,0},{6,3},{7,2},{8,13},{9,12},{10,... | collective-permute-start | bytes 2359304 | tf_op jit(solution)/shard_map/ppermute | solution.py:560
  845.1 8.1 collective-permute-done.26
  853.1 5.0 collective-permute-start.30
  866.4 3.4 collective-permute-done.29
  870.6 16.1 %collective-permute-done.30 = bf16[3,1024,128]{2,1,0:T(8,128)(2,1)S(1)} collective-permute-done((bf16[3,1024,128]{2,1,0:T(8,128)(2,1)S(1)}, bf16[3,1024,128]{2,1,0:T(8,128)(2,1)S(1)}, u32[]{:S(2)}, u32[]{:S(2)}) %collective-permute-start.30) | collective-permute-done | bytes 786464 | tf_op jit(solution)/shard_map/ppermute | solution.py:560
  890.5 13.9 %fusion.119 = (f32[1024]{0:T(1024)S(1)}, f32[1024]{0:T(1024)S(1)}, f32[1024,1024]{1,0:T(8,128)S(1)}) fusion(f32[1024,4096]{1,0:T(8,128)} %fusion.46, f32[1024]{0:T(1024)S(1)} %add_rsqrt_fusion, f32[1024]{0:T(1024)S(1)} %broadcast_multiply_fusion.1, bf16[1024,1024]{1,0:T(8,128)(2,1)} %get-tuple-element.39, bf16[1024,3072]{1,0:T(8,128)(2,1)} %fusion.48, ...), kind=kOutput, calls=%fused_computation.296 | convolution fusion | flops 6450837504 | bytes 23085056 | tf_op jit(solution)/shard_map/dot_general | solution.py:518
  904.5 4.4 fusion.10
  920.4 22.0 %reduce-scatter.5.cloned.1.call-done = bf16[1,288,1024]{2,1,0:T(8,128)(2,1)} async-done(((bf16[4,288,1024]{2,1,0:T(8,128)(2,1)}), bf16[1,288,1024]{2,1,0:T(8,128)(2,1)}) %reduce-scatter.5.cloned.1.call-update) | async-done | bytes 589840 | tf_op jit(solution)/shard_map/reduce_scatter | solution.py:693
  944.4 34.1 %all-gather.4 = s32[8,1,4]{2,1,0:T(1,128)S(1)} all-gather(s32[1,1,4]{2,1,0:T(1,128)S(1)} %bitcast.302), channel_id=1, replica_groups=mesh['dp'=8,'tensor'=4] {'dp'}, dimensions={0}, use_global_device_ids=true | all-gather | bytes 144 | tf_op jit(solution)/shard_map/all_gather | solution.py:743
  983.0 4.7 fusion.36
  990.9 180.0 %sum_everywhere.1 = bf16[8192,256]{1,0:T(8,128)(2,1)S(1)} custom-call(bf16[8192,256]{1,0:T(8,128)(2,1)S(1)} %slice_dynamic-update-slice_fusion.x_ref), custom_call_target="tpu_custom_call" | custom-call | tf_op jit(solution)/shard_map/sum_everywhere/pallas_call | solution.py:484
  1174.9 3.0 copy.121
  1183.7 32.3 %all-reduce.4.cloned.1.call-done = f32[32,4096]{1,0:T(8,128)} async-done(((f32[32,4096]{1,0:T(8,128)}), f32[32,4096]{1,0:T(8,128)}) %all-reduce.4.cloned.1.call-update) | async-done | bytes 524304 | tf_op jit(solution)/shard_map/psum | solution.py:748
  1216.0 5.0 fusion.83
  1223.3 54.8 %all-reduce.6.cloned.1.call-done = bf16[3,1024,256]{2,1,0:T(8,128)(2,1)} async-done(((bf16[3,1024,256]{2,1,0:T(8,128)(2,1)}), bf16[3,1024,256]{2,1,0:T(8,128)(2,1)}) %all-reduce.6.cloned.1.call-update) | async-done | bytes 1572880 | tf_op jit(solution)/shard_map/psum | solution.py:715
  1278.1 3.5 transpose.76
  1281.6 4.6 convolution_bitcast_fusion
  1286.3 4.4 convolution_bitcast_fusion.1
  1290.6 27.7 %all-gather.11.cloned.1.call-done = bf16[8,288,1024]{2,1,0:T(8,128)(2,1)} async-done(((bf16[1,288,1024]{2,1,0:T(8,128)(2,1)}), bf16[8,288,1024]{2,1,0:T(8,128)(2,1)}) %all-gather.11.cloned.1.call-update) | async-done | bytes 4718608 | tf_op jit(solution)/shard_map/all_gather | solution.py:694
  1318.3 3.5 convert_bitcast_fusion
  1321.9 4.5 fusion.120
  1327.9 5.3 copy.114
  1333.2 5.5 reshape.358
  1338.7 4.9 copy.115
  (327 shorter events, 153.2 us)
Async XLA Ops:
  7.2 43.8 %copy-start = (bf16[1024,1024]{1,0:T(8,128)(2,1)S(1)}, bf16[1024,1024]{1,0:T(8,128)(2,1)}, u32[]{:S(2)}) copy-start(bf16[1024,1024]{1,0:T(8,128)(2,1)} %param.17) | copy-start | bytes 6291460
  7.2 36.1 %all-gather.13.cloned.1.call-start = ((), (), s32[]{:S(2)}) async-start(), calls=%async_computation.6 | async-start | bytes 1310720 | tf_op jit(solution)/shard_map/all_gather | solution.py:576
  7.2 36.1 %copy-start.45 = (s32[1,4]{1,0:T(1,128)S(1)}, s32[1,4]{1,0:T(1,128)}, u32[]{:S(2)}) copy-start(s32[1,4]{1,0:T(1,128)} %param.15) | copy-start | bytes 52
  7.3 36.2 %copy-start.47 = (s32[1,4]{1,0:T(1,128)S(1)}, s32[1,4]{1,0:T(1,128)}, u32[]{:S(2)}) copy-start(s32[1,4]{1,0:T(1,128)} %param.14) | copy-start | bytes 52
  12.5 103.6 %all-gather.17.cloned.1.call-start = ((), (), s32[]{:S(2)}) async-start(), calls=%async_computation.8 | async-start | bytes 2621440 | tf_op jit(solution)/shard_map/all_gather | solution.py:592
  15.6 243.4 %all-gather.15.cloned.1.call-start = ((), (), s32[]{:S(2)}) async-start(), calls=%async_computation.7 | async-start | bytes 9437184 | tf_op jit(solution)/shard_map/all_gather | solution.py:576
  43.3 397.6 %all-gather.19.cloned.1.call-start = ((), (), s32[]{:S(2)}) async-start(), calls=%async_computation.9 | async-start | bytes 10485760 | tf_op jit(solution)/shard_map/all_gather | solution.py:592
  43.4 10.7 collective-permute-start.12
  43.5 20.2 %collective-permute-start.1 = (s32[1,4]{1,0:T(1,128)S(1)}, s32[1,4]{1,0:T(1,128)S(1)}, u32[]{:S(2)}, u32[]{:S(2)}) collective-permute-start(s32[1,4]{1,0:T(1,128)S(1)} %copy-done.47), channel_id=1, source_target_pairs={{0,4},{1,5},{2,6},{3,7},{4,0},{5,1},{6,2},{7,3},{8,12},{9,13},{10,... | collective-permute-start | bytes 56 | tf_op jit(solution)/shard_map/ppermute | solution.py:560
  44.0 200.1 %collective-permute-start.14 = (bf16[1024,1024]{1,0:T(8,128)(2,1)}, bf16[1024,1024]{1,0:T(8,128)(2,1)}, u32[]{:S(2)}, u32[]{:S(2)}) collective-permute-start(bf16[1024,1024]{1,0:T(8,128)(2,1)} %bitcast.284), channel_id=1, source_target_pairs={{2,4},{3,5},{4,2},{5,3},{10,12},{11,13},{12,10},{13,11},{18,20},{1... | collective-permute-start | bytes 6291464 | tf_op jit(solution)/shard_map/ppermute | solution.py:552
  61.6 7.2 collective-permute-start.2
  63.8 184.4 %collective-permute-start = (bf16[1024,1024]{1,0:T(8,128)(2,1)}, bf16[1024,1024]{1,0:T(8,128)(2,1)}, u32[]{:S(2)}, u32[]{:S(2)}) collective-permute-start(bf16[1024,1024]{1,0:T(8,128)(2,1)} %get-tuple-element.53), channel_id=1, source_target_pairs={{2,4},{3,5},{4,2},{5,3},{10,12},{11,13},{12,10},{13,11},{18,20},{1... | collective-permute-start | bytes 6291464 | tf_op jit(solution)/shard_map/ppermute | solution.py:552
  72.0 151.7 %collective-permute-start.3 = (bf16[1024,1024]{1,0:T(8,128)(2,1)}, bf16[1024,1024]{1,0:T(8,128)(2,1)}, u32[]{:S(2)}, u32[]{:S(2)}) collective-permute-start(bf16[1024,1024]{1,0:T(8,128)(2,1)} %broadcast_select_fusion.3), channel_id=1, source_target_pairs={{0,1},{1,0},{2,3},{3,2},{4,5},{5,4},{6,7},{7,6},{8,9},{9,8},{10,11... | collective-permute-start | bytes 6291464 | tf_op jit(solution)/shard_map/ppermute | solution.py:560
  116.1 774.3 %reduce-scatter.7.cloned.1.call-start = ((), (), s32[]{:S(2)}) async-start(), calls=%async_computation.10 | async-start | bytes 11796480
  116.5 11.8 copy-start.38
  137.2 110.9 %copy-start.28 = (bf16[1024,1024]{1,0:T(8,128)(2,1)S(1)}, bf16[1024,1024]{1,0:T(8,128)(2,1)}, u32[]{:S(2)}) copy-start(bf16[1024,1024]{1,0:T(8,128)(2,1)} %get-tuple-element.53) | copy-start | bytes 6291460
  137.3 112.8 %collective-permute-start.4 = (bf16[1024,1024]{1,0:T(8,128)(2,1)}, bf16[1024,1024]{1,0:T(8,128)(2,1)S(1)}, u32[]{:S(2)}, u32[]{:S(2)}) collective-permute-start(bf16[1024,1024]{1,0:T(8,128)(2,1)} %broadcast_select_fusion.3), channel_id=1, source_target_pairs={{0,4},{1,5},{2,6},{3,7},{4,0},{5,1},{6,2},{7,3},{8,12},{9,13},{10,... | collective-permute-start | bytes 6291464 | tf_op jit(solution)/shard_map/ppermute | solution.py:560
  223.7 26.5 %collective-permute-start.5 = (bf16[1024,1024]{1,0:T(8,128)(2,1)}, bf16[1024,1024]{1,0:T(8,128)(2,1)S(1)}, u32[]{:S(2)}, u32[]{:S(2)}) collective-permute-start(bf16[1024,1024]{1,0:T(8,128)(2,1)} %collective-permute-done.3), channel_id=1, source_target_pairs={{0,4},{1,5},{2,6},{3,7},{4,0},{5,1},{6,2},{7,3},{8,12},{9,13},{10,... | collective-permute-start | bytes 6291464 | tf_op jit(solution)/shard_map/ppermute | solution.py:560
  241.3 108.0 %copy-start.8 = (s32[8]{0:T(128)}, s32[8]{0:T(128)S(1)}, u32[]{:S(2)}) copy-start(s32[8]{0:T(128)S(1)} %get-tuple-element.98.high_ref) | copy-start | bytes 100
  241.3 108.0 %copy-start.9 = (s32[8]{0:T(128)}, s32[8]{0:T(128)S(1)}, u32[]{:S(2)}) copy-start(s32[8]{0:T(128)S(1)} %get-tuple-element.99.low_ref) | copy-start | bytes 100
  247.4 199.7 %collective-permute-start.15 = (bf16[1024,1024]{1,0:T(8,128)(2,1)}, bf16[1024,1024]{1,0:T(8,128)(2,1)}, u32[]{:S(2)}, u32[]{:S(2)}) collective-permute-start(bf16[1024,1024]{1,0:T(8,128)(2,1)} %broadcast_select_fusion.2.cot_own_ref), channel_id=1, source_target_pairs={{0,4},{1,5},{2,6},{3,7},{4,0},{5,1},{6,2},{7,3},{8,12},{9,13},{10,... | collective-permute-start | bytes 6291464 | tf_op jit(solution)/shard_map/ppermute | solution.py:560
  284.0 14.2 %copy-start.6 = (bf16[4096,128]{1,0:T(8,128)(2,1)S(1)}, bf16[4096,128]{1,0:T(8,128)(2,1)}, u32[]{:S(2)}) copy-start(bf16[4096,128]{1,0:T(8,128)(2,1)} %fusion.33.kmark_ref) | copy-start | bytes 3145732
  284.0 14.2 %copy-start.7 = (bf16[4096,128]{1,0:T(8,128)(2,1)S(1)}, bf16[4096,128]{1,0:T(8,128)(2,1)}, u32[]{:S(2)}) copy-start(bf16[4096,128]{1,0:T(8,128)(2,1)} %select_convert_fusion.qmark_ref) | copy-start | bytes 3145732
  348.4 62.8 %copy-start.10 = (f32[4096,128]{1,0:T(8,128)}, f32[4096,128]{1,0:T(8,128)S(1)}, u32[]{:S(2)}) copy-start(f32[4096,128]{1,0:T(8,128)S(1)} %get-tuple-element.26.lse_ref) | copy-start | bytes 6291460
  348.4 62.9 %copy-start.4 = (bf16[4,1024,128]{2,1,0:T(8,128)(2,1)}, bf16[4,1024,128]{2,1,0:T(8,128)(2,1)S(1)}, u32[]{:S(2)}) copy-start(bf16[4,1024,128]{2,1,0:T(8,128)(2,1)S(1)} %get-tuple-element.20.ctx_ref) | copy-start | bytes 3145732
  348.5 67.6 %collective-permute-start.6 = (bf16[1024,128]{1,0:T(8,128)(2,1)S(1)}, bf16[1024,128]{1,0:T(8,128)(2,1)S(1)}, u32[]{:S(2)}, u32[]{:S(2)}) collective-permute-start(bf16[1024,128]{1,0:T(8,128)(2,1)S(1)} %get-tuple-element.79), channel_id=1, source_target_pairs={{0,1},{1,0},{2,3},{3,2},{4,5},{5,4},{6,7},{7,6},{8,9},{9,8},{10,11... | collective-permute-start | bytes 786440 | tf_op jit(solution)/shard_map/ppermute | solution.py:560
  411.2 10.7 copy-start.5
  411.3 20.7 %copy-start.18 = (bf16[1024,1024]{1,0:T(8,128)(2,1)S(1)}, bf16[1024,1024]{1,0:T(8,128)(2,1)}, u32[]{:S(2)}) copy-start(bf16[1024,1024]{1,0:T(8,128)(2,1)} %get-tuple-element.39) | copy-start | bytes 6291460
  411.4 8.9 collective-permute-start.7
  412.7 9.0 collective-permute-start.8
  415.6 18.8 %copy-start.33 = (bf16[4,8,32,1024]{3,2,1,0:T(8,128)(2,1)}, bf16[4,8,32,1024]{3,2,1,0:T(8,128)(2,1)S(1)}, u32[]{:S(2)}) copy-start(bf16[4,8,32,1024]{3,2,1,0:T(8,128)(2,1)S(1)} %slice.313) | copy-start | bytes 6291460
  415.6 6.3 collective-permute-start.9
  416.2 10.4 collective-permute-start.10
  420.3 11.6 collective-permute-start.11
  440.9 6.2 collective-permute-start.13
  530.9 4.6 collective-permute-start.18
  531.4 16.8 %collective-permute-start.16 = (bf16[1024,1024]{1,0:T(8,128)(2,1)}, bf16[1024,1024]{1,0:T(8,128)(2,1)}, u32[]{:S(2)}, u32[]{:S(2)}) collective-permute-start(bf16[1024,1024]{1,0:T(8,128)(2,1)} %get-tuple-element.23), channel_id=1, source_target_pairs={{0,4},{1,5},{2,6},{3,7},{4,0},{5,1},{6,2},{7,3},{8,12},{9,13},{10,... | collective-permute-start | bytes 6291464 | tf_op jit(solution)/shard_map/ppermute | solution.py:560
  564.6 2.9 collective-permute-start.35
  576.8 365.6 %reduce-scatter.5.cloned.1.call-start = ((), (), s32[]{:S(2)}) async-start(), calls=%async_computation.4 | async-start | bytes 2949120 | tf_op jit(solution)/shard_map/reduce_scatter | solution.py:693
  583.6 8.9 collective-permute-start.22
  589.7 6.8 collective-permute-start.23
  589.8 8.2 collective-permute-start.24
  590.7 14.1 %collective-permute-start.19 = (bf16[1024,128]{1,0:T(8,128)(2,1)}, bf16[1024,128]{1,0:T(8,128)(2,1)S(1)}, u32[]{:S(2)}, u32[]{:S(2)}) collective-permute-start(bf16[1024,128]{1,0:T(8,128)(2,1)} %get-tuple-element.72), channel_id=1, source_target_pairs={{0,1},{1,0},{2,3},{3,2},{4,5},{5,4},{6,7},{7,6},{8,9},{9,8},{10,11... | collective-permute-start | bytes 786440 | tf_op jit(solution)/shard_map/ppermute | solution.py:560
  591.9 12.9 collective-permute-start.20
  592.5 16.7 %collective-permute-start.21 = (bf16[1024,128]{1,0:T(8,128)(2,1)}, bf16[1024,128]{1,0:T(8,128)(2,1)S(1)}, u32[]{:S(2)}, u32[]{:S(2)}) collective-permute-start(bf16[1024,128]{1,0:T(8,128)(2,1)} %get-tuple-element.70), channel_id=1, source_target_pairs={{0,5},{1,4},{2,7},{3,6},{4,1},{5,0},{6,3},{7,2},{8,13},{9,12},{10,... | collective-permute-start | bytes 786440 | tf_op jit(solution)/shard_map/ppermute | solution.py:560
  785.1 13.6 %copy-start.25 = (bf16[4,3,1024,128]{3,2,1,0:T(8,128)(2,1)S(1)}, bf16[4,3,1024,128]{3,2,1,0:T(8,128)(2,1)}, u32[]{:S(2)}) copy-start(bf16[4,3,1024,128]{3,2,1,0:T(8,128)(2,1)} %attend_back.2) | copy-start | bytes 9437188
  796.8 116.2 %collective-permute-start.34 = (bf16[1024,768]{0,1:T(8,128)(2,1)}, bf16[1024,768]{0,1:T(8,128)(2,1)}, u32[]{:S(2)}, u32[]{:S(2)}) collective-permute-start(bf16[1024,768]{0,1:T(8,128)(2,1)} %convolution_convert_fusion.2), channel_id=1, source_target_pairs={{2,4},{3,5},{4,2},{5,3},{10,12},{11,13},{12,10},{13,11},{18,20},{1... | collective-permute-start | bytes 4718600 | tf_op jit(solution)/shard_map/ppermute | solution.py:552
  798.9 21.1 %collective-permute-start.25 = (bf16[3,1024,128]{2,1,0:T(8,128)(2,1)S(1)}, bf16[3,1024,128]{2,1,0:T(8,128)(2,1)S(1)}, u32[]{:S(2)}, u32[]{:S(2)}) collective-permute-start(bf16[3,1024,128]{2,1,0:T(8,128)(2,1)S(1)} %get-tuple-element.65), channel_id=1, source_target_pairs={{0,1},{1,0},{2,3},{3,2},{4,5},{5,4},{6,7},{7,6},{8,9},{9,8},{10,11... | collective-permute-start | bytes 2359304 | tf_op jit(solution)/shard_map/ppermute | solution.py:560
  802.9 50.2 %collective-permute-start.26 = (bf16[3,1024,128]{2,1,0:T(8,128)(2,1)S(1)}, bf16[3,1024,128]{2,1,0:T(8,128)(2,1)S(1)}, u32[]{:S(2)}, u32[]{:S(2)}) collective-permute-start(bf16[3,1024,128]{2,1,0:T(8,128)(2,1)S(1)} %get-tuple-element.62), channel_id=1, source_target_pairs={{0,1},{1,0},{2,3},{3,2},{4,5},{5,4},{6,7},{7,6},{8,9},{9,8},{10,11... | collective-permute-start | bytes 2359304 | tf_op jit(solution)/shard_map/ppermute | solution.py:560
  804.2 57.7 %collective-permute-start.27 = (bf16[3,1024,128]{2,1,0:T(8,128)(2,1)S(1)}, bf16[3,1024,128]{2,1,0:T(8,128)(2,1)S(1)}, u32[]{:S(2)}, u32[]{:S(2)}) collective-permute-start(bf16[3,1024,128]{2,1,0:T(8,128)(2,1)S(1)} %get-tuple-element.64), channel_id=1, source_target_pairs={{0,4},{1,5},{2,6},{3,7},{4,0},{5,1},{6,2},{7,3},{8,12},{9,13},{10,... | collective-permute-start | bytes 2359304 | tf_op jit(solution)/shard_map/ppermute | solution.py:560
  804.5 58.1 %collective-permute-start.28 = (bf16[3,1024,128]{2,1,0:T(8,128)(2,1)S(1)}, bf16[3,1024,128]{2,1,0:T(8,128)(2,1)S(1)}, u32[]{:S(2)}, u32[]{:S(2)}) collective-permute-start(bf16[3,1024,128]{2,1,0:T(8,128)(2,1)S(1)} %get-tuple-element.61), channel_id=1, source_target_pairs={{0,4},{1,5},{2,6},{3,7},{4,0},{5,1},{6,2},{7,3},{8,12},{9,13},{10,... | collective-permute-start | bytes 2359304 | tf_op jit(solution)/shard_map/ppermute | solution.py:560
  820.1 49.8 %collective-permute-start.29 = (bf16[3,1024,128]{2,1,0:T(8,128)(2,1)S(1)}, bf16[3,1024,128]{2,1,0:T(8,128)(2,1)S(1)}, u32[]{:S(2)}, u32[]{:S(2)}) collective-permute-start(bf16[3,1024,128]{2,1,0:T(8,128)(2,1)S(1)} %get-tuple-element.63), channel_id=1, source_target_pairs={{0,5},{1,4},{2,7},{3,6},{4,1},{5,0},{6,3},{7,2},{8,13},{9,12},{10,... | collective-permute-start | bytes 2359304 | tf_op jit(solution)/shard_map/ppermute | solution.py:560
  853.1 33.6 %collective-permute-start.30 = (bf16[3,1024,128]{2,1,0:T(8,128)(2,1)S(1)}, bf16[3,1024,128]{2,1,0:T(8,128)(2,1)S(1)}, u32[]{:S(2)}, u32[]{:S(2)}) collective-permute-start(bf16[3,1024,128]{2,1,0:T(8,128)(2,1)S(1)} %get-tuple-element.60), channel_id=1, source_target_pairs={{0,5},{1,4},{2,7},{3,6},{4,1},{5,0},{6,3},{7,2},{8,13},{9,12},{10,... | collective-permute-start | bytes 2359304 | tf_op jit(solution)/shard_map/ppermute | solution.py:560
  890.5 325.5 %all-reduce.4.cloned.1.call-start = ((), (), s32[]{:S(2)}) async-start(), calls=%async_computation.2 | async-start | bytes 1048576 | tf_op jit(solution)/shard_map/psum | solution.py:748
  890.5 14.0 %copy-start.20 = (bf16[1024,1024]{1,0:T(8,128)(2,1)S(1)}, bf16[1024,1024]{1,0:T(8,128)(2,1)}, u32[]{:S(2)}) copy-start(bf16[1024,1024]{1,0:T(8,128)(2,1)} %get-tuple-element.39) | copy-start | bytes 6291460
  890.5 14.0 %copy-start.23 = (f32[1024,1024]{1,0:T(8,128)S(1)}, f32[1024,1024]{1,0:T(8,128)}, u32[]{:S(2)}) copy-start(f32[1024,1024]{1,0:T(8,128)} %copy-done.22) | copy-start | bytes 12582916
  913.0 31.4 %copy-start.46 = (s32[1,4]{1,0:T(1,128)S(1)}, s32[1,4]{1,0:T(1,128)}, u32[]{:S(2)}) copy-start(s32[1,4]{1,0:T(1,128)} %param.15) | copy-start | bytes 52
  913.0 65.6 %copy-start.44 = (f32[128]{0:T(128)S(1)}, f32[128]{0:T(128)}, u32[]{:S(2)}) copy-start(f32[128]{0:T(128)} %copy-done.43) | copy-start | bytes 1540
  913.0 365.1 %all-reduce.6.cloned.1.call-start = ((), (), s32[]{:S(2)}) async-start(), calls=%async_computation.3 | async-start | bytes 3145728 | tf_op jit(solution)/shard_map/psum | solution.py:715
  918.4 399.9 %all-gather.11.cloned.1.call-start = ((), (), s32[]{:S(2)}) async-start(), calls=%async_computation.5 | async-start | bytes 5308416 | tf_op jit(solution)/shard_map/all_gather | solution.py:694
  918.5 64.5 %collective-permute-start.32 = (bf16[1024,1024]{1,0:T(8,128)(2,1)}, bf16[1024,1024]{1,0:T(8,128)(2,1)}, u32[]{:S(2)}, u32[]{:S(2)}) collective-permute-start(bf16[1024,1024]{1,0:T(8,128)(2,1)} %bitcast.305), channel_id=1, source_target_pairs={{2,4},{3,5},{4,2},{5,3},{10,12},{11,13},{12,10},{13,11},{18,20},{1... | collective-permute-start | bytes 6291464 | tf_op jit(solution)/shard_map/ppermute | solution.py:552
  942.5 45.6 %collective-permute-start.33 = (bf16[1024,1024]{1,0:T(8,128)(2,1)}, bf16[1024,1024]{1,0:T(8,128)(2,1)}, u32[]{:S(2)}, u32[]{:S(2)}) collective-permute-start(bf16[1024,1024]{1,0:T(8,128)(2,1)} %bitcast.306), channel_id=1, source_target_pairs={{2,4},{3,5},{4,2},{5,3},{10,12},{11,13},{12,10},{13,11},{18,20},{1... | collective-permute-start | bytes 6291464 | tf_op jit(solution)/shard_map/ppermute | solution.py:552
  978.8 242.2 %collective-permute-start.17 = (bf16[1024,1024]{1,0:T(8,128)(2,1)}, bf16[1024,1024]{1,0:T(8,128)(2,1)}, u32[]{:S(2)}, u32[]{:S(2)}) collective-permute-start(bf16[1024,1024]{1,0:T(8,128)(2,1)} %get-tuple-element.51), channel_id=1, source_target_pairs={{2,4},{3,5},{4,2},{5,3},{10,12},{11,13},{12,10},{13,11},{18,20},{1... | collective-permute-start | bytes 6291464 | tf_op jit(solution)/shard_map/ppermute | solution.py:552
  980.9 300.8 %collective-permute-start.31 = (bf16[1024,1024]{1,0:T(8,128)(2,1)}, bf16[1024,1024]{1,0:T(8,128)(2,1)}, u32[]{:S(2)}, u32[]{:S(2)}) collective-permute-start(bf16[1024,1024]{1,0:T(8,128)(2,1)} %get-tuple-element.49), channel_id=1, source_target_pairs={{2,4},{3,5},{4,2},{5,3},{10,12},{11,13},{12,10},{13,11},{18,20},{1... | collective-permute-start | bytes 6291464 | tf_op jit(solution)/shard_map/ppermute | solution.py:552
  (35 other events, 186.6 us)
Sparse Core Ops, SparseCore 0:
  12.6 30.6 all-gather.12
  45.4 70.6 all-gather.16
  118.0 55.1 all-gather.14
  174.9 114.8 all-gather.18
  576.9 93.2 reduce-scatter.6
  890.6 51.8 reduce-scatter.4
  948.3 267.6 all-reduce.3
  1220.1 57.9 all-reduce.5
  1280.0 38.2 all-gather.10

commit v2 on v1

v2 whole, which is shorter than its diff:
```python
import functools
import math

import jax
import jax.numpy as jnp
from jax import lax
from jax.experimental import pallas as pl
from jax.experimental.pallas import tpu as pltpu
from jax.sharding import PartitionSpec as P

HEAD_DIM = 64
LANES = 128
MASKED = -1e30
LOG2E = math.log2(math.e)
MIB = 2**20
BF = jnp.bfloat16
F32 = jnp.float32
norm_epsilon = 1e-06
NT = (((1,), (1,)), ((), ()))
TN = (((0,), (0,)), ((), ()))


def cost(microseconds):
    return pl.CostEstimate(flops=int(microseconds * 1.1e9), bytes_accessed=0, transcendentals=0)


def stored_block(block, own, per_part):
    shift = per_part.bit_length() - 1
    part = lax.shift_right_logical(block, shift)
    return ((part ^ own) << shift) | (block & (per_part - 1))


def swap_halves(values):
    lane = lax.broadcasted_iota(jnp.int32, values.shape, 1)
    return jnp.where(lane % 64 < 32, pltpu.roll(values, 96, 1), pltpu.roll(values, 32, 1))


def mesh_spot(parts):
    d = lax.axis_index("dp")
    z = lax.axis_index("tensor")
    return d, z, d % 2, parts // 2


def partner_of(d, z, b, half):
    return d ^ (b // half), z ^ (b % half)


def remote_copy(source, target, sems, at, device):
    return pltpu.make_async_remote_copy(
        src_ref=source,
        dst_ref=target,
        send_sem=sems.at[2 * at],
        recv_sem=sems.at[2 * at + 1],
        device_id=device,
        device_id_type=pl.DeviceIdType.MESH,
    )


PIECES = 4


def in_pieces(source, target, sems, at, device, pieces=range(PIECES)):
    rows = source.shape[0] // PIECES
    return [
        remote_copy(
            source.at[k * rows : (k + 1) * rows, :], target.at[k * rows : (k + 1) * rows, :], sems, at + k, device
        )
        for k in pieces
    ]


def remote(source, target, sems, at, device):
    copy = remote_copy(source, target, sems, at, device)
    copy.start()
    return copy


def greet(devices):
    barrier = pltpu.get_barrier_semaphore()
    for device in devices:
        pl.semaphore_signal(barrier, inc=1, device_id=device, device_id_type=pl.DeviceIdType.MESH)
    pl.semaphore_wait(barrier, len(devices))


def project_kernel(normed_ref, weight_ref, cos_ref, sin_ref, out_ref, *, pairs):
    normed = normed_ref[...]
    cosine = cos_ref[...]
    sine = sin_ref[...]
    width = pairs * LANES
    for kind in range(3):
        weight = weight_ref[kind * width : (kind + 1) * width, :]
        part = lax.dot_general(normed, weight, NT, preferred_element_type=F32)
        for pair in range(pairs):
            cut = part[:, pair * LANES : (pair + 1) * LANES]
            if kind < 2:
                cut = cut * cosine + swap_halves(cut) * sine
            if kind == 0:
                cut = cut * (LOG2E * HEAD_DIM**-0.5)
            out_ref[pair * 3 + kind] = cut.astype(BF)


def project(normed_all, weight, cosine, sine, pairs):
    length, depth = normed_all.shape
    rows = 512
    return pl.pallas_call(
        functools.partial(project_kernel, pairs=pairs),
        grid=(length // rows,),
        in_specs=[
            pl.BlockSpec((rows, depth), lambda i: (i, 0)),
            pl.BlockSpec(weight.shape, lambda i: (0, 0)),
            pl.BlockSpec((rows, LANES), lambda i: (i, 0)),
            pl.BlockSpec((rows, LANES), lambda i: (i, 0)),
        ],
        out_specs=pl.BlockSpec((3 * pairs, rows, LANES), lambda i: (0, i, 0)),
        out_shape=jax.ShapeDtypeStruct((3 * pairs, length, LANES), BF),
        compiler_params=pltpu.CompilerParams(vmem_limit_bytes=40 * MIB),
        cost_estimate=cost(11),
        name="project",
    )(normed_all, weight, cosine, sine)


def attend_kernel(
    own_ref, low_ref, high_ref, q_ref, k_ref, v_ref, qmark_ref, kmark_ref, ctx_ref, lse_ref, keys, vals,
    *, bq, bk, per_part,
):
    step = pl.program_id(0)
    length = kmark_ref.shape[0]
    own = own_ref[0]

    @pl.when(step == 0)
    def _():
        lane = lax.broadcasted_iota(jnp.int32, (512, LANES), 1)

        @pl.loop(0, length // 512)
        def _(i):
            rows = pl.ds(pl.multiple_of(i * 512, 512), 512)
            keys[rows, :LANES] = k_ref[0, rows, :]
            keys[rows, LANES:] = kmark_ref[rows, :]
            v = v_ref[0, rows, :]
            one = jnp.ones_like(v)
            vals[0, rows, :] = jnp.where(lane < 64, v, one)
            vals[1, rows, :] = jnp.where(lane < 64, one, v)

    first = lax.broadcasted_iota(jnp.int32, (bq, LANES), 1) < 64
    q = q_ref[0]
    mark = qmark_ref[...]
    zero = jnp.zeros_like(q)
    queries = (
        jnp.concatenate([jnp.where(first, q, zero), mark], axis=1),
        jnp.concatenate([jnp.where(first, zero, q), mark], axis=1),
    )

    def body(j, carry):
        rows = pl.ds(pl.multiple_of(stored_block(j, own, per_part // bk) * bk, bk), bk)
        block = keys[rows, :]
        new = []
        for head in range(2):
            peak, total = carry[head]
            scores = lax.dot_general(queries[head], block, NT, preferred_element_type=F32)
            higher = jnp.maximum(peak, jnp.max(scores, axis=1, keepdims=True))
            weights = jnp.exp2(scores - higher).astype(BF)
            total = total * jnp.exp2(peak - higher) + jnp.dot(
                weights, vals[head, rows, :], preferred_element_type=F32
            )
            new.append((higher, total))
        return tuple(new)

    init = (jnp.full((bq, 1), -3e38, F32), jnp.zeros((bq, LANES), F32))
    (peak_a, sum_a), (peak_b, sum_b) = lax.fori_loop(low_ref[step], high_ref[step], body, (init, init))
    weight_sum = pltpu.roll(jnp.where(first, sum_b, sum_a), 64, 1)
    ctx_ref[0] = (jnp.where(first, sum_a, sum_b) / weight_sum).astype(BF)
    lse_ref[...] = jnp.where(first, peak_a, peak_b) + jnp.log2(weight_sum)


def attend(qkv, pair, qmark, kmark, own, low, high, bq, bk, per_part):
    length = qmark.shape[0]
    row = lambda i, *_: (i, 0)
    whole = lambda i, *_: (0, 0)
    return pl.pallas_call(
        functools.partial(attend_kernel, bq=bq, bk=bk, per_part=per_part),
        grid_spec=pltpu.PrefetchScalarGridSpec(
            num_scalar_prefetch=3,
            grid=(length // bq,),
            in_specs=[
                pl.BlockSpec((1, bq, LANES), lambda i, *_: (3 * pair, i, 0)),
                pl.BlockSpec((1, length, LANES), lambda i, *_: (3 * pair + 1, 0, 0)),
                pl.BlockSpec((1, length, LANES), lambda i, *_: (3 * pair + 2, 0, 0)),
                pl.BlockSpec((bq, LANES), row),
                pl.BlockSpec((length, LANES), whole),
            ],
            out_specs=[
                pl.BlockSpec((1, bq, LANES), lambda i, *_: (i // (per_part // bq), i % (per_part // bq), 0)),
                pl.BlockSpec((bq, LANES), row),
            ],
            scratch_shapes=[pltpu.VMEM((length, 2 * LANES), BF), pltpu.VMEM((2, length, LANES), BF)],
        ),
        out_shape=[
            jax.ShapeDtypeStruct((length // per_part, per_part, LANES), BF),
            jax.ShapeDtypeStruct((length, LANES), F32),
        ],
        compiler_params=pltpu.CompilerParams(
            dimension_semantics=("arbitrary",), vmem_limit_bytes=48 * MIB
        ),
        cost_estimate=cost(37),
        name="attend",
    )(own, low, high, qkv, qkv, qkv, qmark, kmark)


def three_parts(value):
    high = value.astype(BF).astype(F32)
    rest = value - high
    middle = rest.astype(BF).astype(F32)
    return high, middle, (rest - middle).astype(BF).astype(F32)


def attend_back_kernel(
    own_ref, low_ref, high_ref, q_ref, k_ref, v_ref, do_ref, ctx_ref, lse_ref, qmark_ref, kmark_ref, cos_ref,
    sin_ref, out_ref, keys, vals, key_heads, query_heads, grad_heads, dq_sum,
    *, bq, bk, utt, per_part,
):
    length = kmark_ref.shape[0]
    own = own_ref[0]
    pb = 512
    lane = lax.broadcasted_iota(jnp.int32, (pb, LANES), 1)
    first = lane < 64

    @pl.loop(0, length // pb)
    def _(i):
        rows = pl.ds(pl.multiple_of(i * pb, pb), pb)
        at, within = i // (per_part // pb), pl.ds(pl.multiple_of(i % (per_part // pb) * pb, pb), pb)
        k = k_ref[0, rows, :]
        zero = jnp.zeros_like(k)
        mark = kmark_ref[rows, :]
        keys[rows, :LANES] = k
        keys[rows, LANES:] = mark
        vals[rows, :LANES] = v_ref[0, rows, :]
        vals[rows, LANES:] = mark
        q = q_ref[0, rows, :]
        grad = do_ref[at, within, :]
        qmark = qmark_ref[rows, :].astype(F32)
        lse = lse_ref[rows, :]
        product = grad.astype(F32) * ctx_ref[at, within, :].astype(F32)
        for head in range(2):
            mine = first if head == 0 else jnp.logical_not(first)
            key_heads[head, rows, :] = jnp.where(mine, k, zero)
            query_heads[head, rows, :LANES] = jnp.where(mine, q, zero)
            grad_heads[head, rows, :LANES] = jnp.where(mine, grad, zero)
            high, middle, low = three_parts(-lse[:, 64 * head : 64 * head + 1])
            query_heads[head, rows, LANES:] = jnp.where(
                lane == utt, high, jnp.where(lane == utt + 1, middle, jnp.where(lane == utt + 2, low, qmark))
            ).astype(BF)
            delta = jnp.sum(jnp.where(mine, product, 0.0), axis=1, keepdims=True)
            high, middle, low = three_parts(-delta)
            grad_heads[head, rows, LANES:] = jnp.where(
                lane == utt, high, jnp.where(lane == utt + 1, middle, jnp.where(lane == utt + 2, low, 0.0))
            ).astype(BF)
        dq_sum[rows, :] = jnp.zeros((pb, LANES), F32)

    @pl.loop(0, length // bk)
    def _(j):
        key_rows = pl.ds(pl.multiple_of(j * bk, bk), bk)
        key_block = keys[key_rows, :]
        value_block = vals[key_rows, :]

        def body(i, carry):
            dk, dv = carry
            rows = pl.ds(pl.multiple_of(stored_block(i, own, per_part // bq) * bq, bq), bq)
            dq = dq_sum[rows, :]
            for head in range(2):
                query = query_heads[head, rows, :]
                grad = grad_heads[head, rows, :]
                probs = jnp.exp2(lax.dot_general(key_block, query, NT, preferred_element_type=F32))
                pulled = lax.dot_general(value_block, grad, NT, preferred_element_type=F32)
                grad_scores = (probs * pulled).astype(BF)
                dv = dv + jnp.dot(probs.astype(BF), grad[:, :LANES], preferred_element_type=F32)
                dk = dk + jnp.dot(grad_scores, query[:, :LANES], preferred_element_type=F32)
                dq = dq + lax.dot_general(
                    grad_scores, key_heads[head, key_rows, :], TN, preferred_element_type=F32
                )
            dq_sum[rows, :] = dq
            return dk, dv

        zero = jnp.zeros((bk, LANES), F32)
        dk, dv = lax.fori_loop(low_ref[j], high_ref[j], body, (zero, zero))
        at, within = j // (per_part // bk), pl.ds(pl.multiple_of(j % (per_part // bk) * bk, bk), bk)
        out_ref[at, 2, within, :] = dv.astype(BF)
        dk = dk * (1.0 / LOG2E)
        out_ref[at, 1, within, :] = (dk * cos_ref[key_rows, :] - swap_halves(dk) * sin_ref[key_rows, :]).astype(BF)

    @pl.loop(0, length // pb)
    def _(i):
        rows = pl.ds(pl.multiple_of(i * pb, pb), pb)
        at, within = i // (per_part // pb), pl.ds(pl.multiple_of(i % (per_part // pb) * pb, pb), pb)
        dq = dq_sum[rows, :] * HEAD_DIM**-0.5
        out_ref[at, 0, within, :] = (dq * cos_ref[rows, :] - swap_halves(dq) * sin_ref[rows, :]).astype(BF)


def attend_back(
    qkv, pair, grad, ctx, lse, qmark, kmark, cosine, sine, own, low, high, bq, bk, utt, per_part
):
    length = qmark.shape[0]
    in_smem = pl.BlockSpec(memory_space=pltpu.SMEM)
    whole = pl.BlockSpec((length, LANES), lambda i: (0, 0))
    parts = length // per_part
    by_part = pl.BlockSpec((parts, per_part, LANES), lambda i: (0, 0, 0))
    cut = lambda kind: pl.BlockSpec((1, length, LANES), lambda i: (3 * pair + kind, 0, 0))
    wide = pltpu.VMEM((length, 2 * LANES), BF)
    return pl.pallas_call(
        functools.partial(attend_back_kernel, bq=bq, bk=bk, utt=utt, per_part=per_part),
        grid=(1,),
        in_specs=[in_smem] * 3 + [cut(0), cut(1), cut(2)] + [by_part] * 2 + [whole] * 5,
        out_specs=pl.BlockSpec((parts, 3, per_part, LANES), lambda i: (0, 0, 0, 0)),
        out_shape=jax.ShapeDtypeStruct((parts, 3, per_part, LANES), BF),
        scratch_shapes=[
            wide,
            wide,
            pltpu.VMEM((2, length, LANES), BF),
            pltpu.VMEM((2, length, 2 * LANES), BF),
            pltpu.VMEM((2, length, 2 * LANES), BF),
            pltpu.VMEM((length, LANES), F32),
        ],
        compiler_params=pltpu.CompilerParams(vmem_limit_bytes=56 * MIB),
        cost_estimate=cost(66),
        name="attend_back",
    )(own, low, high, qkv, qkv, qkv, grad, ctx, lse, qmark, kmark, cosine, sine)


def frame_marks(lengths, places, utt):
    ends = jnp.cumsum(lengths)
    starts = ends - lengths
    segment = jnp.sum((places[:, None] >= ends[None, :]).astype(jnp.int32), axis=1, dtype=jnp.int32)
    member = segment[:, None] == jnp.arange(utt, dtype=jnp.int32)[None, :]
    offsets = jnp.sum(jnp.where(member, starts[None, :], 0), axis=1, dtype=jnp.int32)
    return segment, member, offsets


def block_ranges(lengths, blocks, size, other):
    ends = jnp.cumsum(lengths)
    starts = ends - lengths
    at_first = blocks * size
    at_last = at_first + (size - 1)
    index = jnp.arange(lengths.shape[0], dtype=jnp.int32)
    seg_first = jnp.sum((at_first[:, None] >= ends[None]).astype(jnp.int32), axis=1)
    seg_last = jnp.sum((at_last[:, None] >= ends[None]).astype(jnp.int32), axis=1)
    low = jnp.sum(jnp.where(index[None] == seg_first[:, None], starts[None], 0), axis=1)
    high = jnp.sum(jnp.where(index[None] == seg_last[:, None], ends[None], 0), axis=1)
    return (low // other).astype(jnp.int32), ((high + other - 1) // other).astype(jnp.int32)


def feed_kernel(
    x_own_ref, cot_own_ref, cot_other_ref, weights_ref, inputs_hbm, heads_hbm,
    out_own_ref, out_other_ref, gin_own_ref, gin_other_ref, grads_ref, inputs_in_hbm, heads_out_hbm,
    x_other_ref, out_sum, gin_sum, local, sems, *, parts,
):
    step = pl.program_id(0)
    last = pl.num_programs(0) - 1
    d, z, core, half = mesh_spot(parts)
    leaves = z // half != core
    there = ((d - core) + z // half, core * half + z % half)
    beside = partner_of(d, z, half, half)

    def copies():
        return in_pieces(inputs_hbm, inputs_in_hbm, sems, 1, there)

    eighth = d // 2 % 4 + 4 * core

    def heads_part(k):
        if k < parts:
            cut = heads_out_hbm.at[eighth, z]
            return remote_copy(cut, cut, sems, PIECES + k, (d, z ^ k))
        size = 1 << (k - parts)
        cut = heads_out_hbm.at[pl.ds(eighth // size * size, size)]
        return remote_copy(cut, cut, sems, PIECES + k, (d ^ (2, 4)[k - parts], z))

    @pl.when(step == 0)
    def _():
        barrier = pltpu.get_barrier_semaphore()
        near = [(d ^ bit, z) for bit in (1, 2, 4)] + [(d, z ^ k) for k in range(1, parts)]
        for device in near:
            pl.semaphore_signal(barrier, inc=1, device_id=device, device_id_type=pl.DeviceIdType.MESH)

        @pl.when(leaves)
        def _():
            pl.semaphore_signal(barrier, inc=1, device_id=there, device_id_type=pl.DeviceIdType.MESH)
            pl.semaphore_wait(barrier, len(near) + 1)

        @pl.when(jnp.logical_not(leaves))
        def _():
            pl.semaphore_wait(barrier, len(near))

        remote_copy(x_own_ref, x_other_ref, sems, 0, beside).start()
        copy = pltpu.make_async_copy(heads_hbm.at[:, eighth], heads_out_hbm.at[eighth, z], local)
        copy.start()
        copy.wait()
        for k in range(1, parts):
            heads_part(k).start()

    @pl.when(step == 1)
    def _():
        @pl.when(leaves)
        def _():
            for copy in copies():
                copy.start()

    @pl.when(step == 2)
    def _():
        for k in range(1, parts):
            heads_part(k).wait()
        heads_part(parts).start()

    @pl.when(step == 4)
    def _():
        heads_part(parts).wait()
        heads_part(parts + 1).start()

    chunk, depth = weights_ref.shape[0] * weights_ref.shape[2], weights_ref.shape[3]
    up = weights_ref[:, 0].reshape(chunk, depth)
    down = weights_ref[:, 1].reshape(chunk, depth)
    root = math.sqrt(2.0 / math.pi)
    gup = gdown = None
    for side, (x_ref, cot_ref) in enumerate(((x_own_ref, cot_own_ref), (x_other_ref, cot_other_ref))):
        if side == 1:

            @pl.when(step == 0)
            def _():
                remote_copy(x_own_ref, x_other_ref, sems, 0, beside).wait()

        x = x_ref[...]
        cot = cot_ref[...]
        before = lax.dot_general(x, up, NT, preferred_element_type=F32)
        grad_act = lax.dot_general(cot, down, NT, preferred_element_type=F32)
        square = before * before
        bend = jnp.tanh(root * before * (1.0 + 0.044715 * square))
        half = 0.5 * (1.0 + bend)
        activated = (before * half).astype(BF)
        slope = half + 0.5 * before * (1.0 - bend * bend) * (root + (3.0 * 0.044715 * root) * square)
        grad_before = (grad_act * slope).astype(BF)
        out = jnp.dot(activated, down, preferred_element_type=F32)
        gin = jnp.dot(grad_before, up, preferred_element_type=F32)
        gd = lax.dot_general(activated, cot, TN, preferred_element_type=F32)
        gu = lax.dot_general(grad_before, x, TN, preferred_element_type=F32)
        gup = gu if side == 0 else gup + gu
        gdown = gd if side == 0 else gdown + gd

        @pl.when(step == 0)
        def _():
            out_sum[side] = out
            gin_sum[side] = gin

        @pl.when(step > 0)
        def _():
            out_sum[side] += out
            gin_sum[side] += gin

    per = weights_ref.shape[2]
    grads_ref[:, :per] = gup.astype(BF).reshape(-1, per, depth)
    grads_ref[:, per : 2 * per] = gdown.astype(BF).reshape(-1, per, depth)
    grads_ref[:, 2 * per :] = jnp.zeros(grads_ref[:, 2 * per :].shape, BF)

    @pl.when(step == last)
    def _():
        out_own_ref[...] = out_sum[0]
        out_other_ref[...] = out_sum[1].astype(BF)
        gin_own_ref[...] = gin_sum[0]
        gin_other_ref[...] = gin_sum[1].astype(BF)

        heads_part(parts + 1).wait()

        @pl.when(leaves)
        def _():
            for copy in copies():
                copy.wait()


def feed(x_own, cot_own, cot_other, weights, inputs, heads, spare, parts):
    frames, depth = x_own.shape
    groups, _, per, _ = weights.shape
    chunk = 256
    whole = pl.BlockSpec((frames, depth), lambda j: (0, 0))
    cut = pl.BlockSpec((chunk // per, 2, per, depth), lambda j: (j, 0, 0, 0))
    grads = pl.BlockSpec((chunk // per, 2 * per + spare, depth), lambda j: (j, 0, 0))
    shape = lambda *s: jax.ShapeDtypeStruct(*s)
    anywhere = pl.BlockSpec(memory_space=pl.ANY)
    return pl.pallas_call(
        functools.partial(feed_kernel, parts=parts),
        grid=(groups * per // chunk,),
        in_specs=[whole] * 3 + [cut] + [anywhere] * 2,
        out_specs=[whole] * 4 + [grads] + [anywhere] * 2,
        out_shape=[
            shape((frames, depth), F32),
            shape((frames, depth), BF),
            shape((frames, depth), F32),
            shape((frames, depth), BF),
            shape((groups, 2 * per + spare, depth), BF),
            shape((frames, depth), BF),
            shape((8, parts) + heads.shape[:1] + heads.shape[2:], BF),
        ],
        scratch_shapes=[
            pltpu.VMEM((frames, depth), BF),
            pltpu.VMEM((2, frames, depth), F32),
            pltpu.VMEM((2, frames, depth), F32),
            pltpu.SemaphoreType.DMA,
            pltpu.SemaphoreType.DMA((2 * (PIECES + parts + 3),)),
        ],
        compiler_params=pltpu.CompilerParams(
            dimension_semantics=("arbitrary",), vmem_limit_bytes=60 * MIB, collective_id=3, has_side_effects=True
        ),
        cost_estimate=cost(84),
        name="feed",
    )(x_own, cot_own, cot_other, weights, inputs, heads)


def spread(segment, table):
    masks = [segment == u for u in range(1, table.shape[0])]
    columns = []
    for k in range(table.shape[1] // LANES):
        cut = table[:, k * LANES : (k + 1) * LANES]
        out = jnp.broadcast_to(cut[0:1], segment.shape)
        for u, mask in enumerate(masks):
            out = jnp.where(mask, cut[u + 1 : u + 2], out)
        columns.append(out)
    return jnp.concatenate(columns, axis=1)


def collect(segment, values, utt):
    rows = []
    for u in range(utt):
        mask = segment == u
        rows.append(
            jnp.concatenate(
                [
                    jnp.sum(jnp.where(mask, values[:, k * LANES : (k + 1) * LANES], 0.0), axis=0, keepdims=True)
                    for k in range(values.shape[1] // LANES)
                ],
                axis=1,
            )
        )
    return jnp.concatenate(rows, axis=0)


def unit_norm(hidden):
    center = hidden - jnp.mean(hidden, axis=-1, keepdims=True)
    inverse = lax.rsqrt(jnp.mean(center * center, axis=-1, keepdims=True) + norm_epsilon)
    return center * inverse, inverse


def pull_norm(unit, inverse, grad, gain):
    pulled = grad * gain
    return (
        pulled
        - jnp.mean(pulled, axis=-1, keepdims=True)
        - unit * jnp.mean(pulled * unit, axis=-1, keepdims=True)
    ) * inverse


def join_kernel(own_ref, *refs, pairs, parts):
    ctx_refs = refs[: pairs * parts]
    w_out_ref, base_ref, base_in_ref, segment_ref, shift_ref, scale_ref, hidden_ref, normed_ref = refs[pairs * parts :]
    own = own_ref[0]
    hidden = jnp.where(own_ref[1] == 1, base_ref[...], base_in_ref[...]).astype(F32)
    for b in range(parts):
        context = jnp.concatenate([ctx_refs[pair * parts + b][...] for pair in range(pairs)], axis=1)
        hidden = hidden + jnp.dot(context, w_out_ref[:, own ^ b].reshape(pairs * LANES, -1), preferred_element_type=F32)
    hidden_ref[...] = hidden
    unit, _ = unit_norm(hidden)
    segment = segment_ref[...]
    normed_ref[...] = (unit * (1.0 + spread(segment, scale_ref[...])) + spread(segment, shift_ref[...])).astype(BF)


def join(own, ctx_blocks, w_out, base, base_in, segment, shift, scale, pairs, parts):
    frames, depth = base.shape
    rows = 256
    row = lambda i, *_: (i, 0)
    wide = pl.BlockSpec((rows, depth), row)
    table = pl.BlockSpec(shift.shape, lambda i, *_: (0, 0))
    return pl.pallas_call(
        functools.partial(join_kernel, pairs=pairs, parts=parts),
        grid_spec=pltpu.PrefetchScalarGridSpec(
            num_scalar_prefetch=1,
            grid=(frames // rows,),
            in_specs=[pl.BlockSpec((rows, LANES), row)] * (pairs * parts)
            + [pl.BlockSpec(w_out.shape, lambda i, *_: (0, 0, 0, 0)), wide, wide, pl.BlockSpec((rows, LANES), row)]
            + [table] * 2,
            out_specs=[wide, wide],
        ),
        out_shape=[jax.ShapeDtypeStruct((frames, depth), F32), jax.ShapeDtypeStruct((frames, depth), BF)],
        compiler_params=pltpu.CompilerParams(vmem_limit_bytes=40 * MIB),
        cost_estimate=cost(8),
        name="join",
    )(own, *ctx_blocks, w_out, base, base_in, segment, shift, scale)


def turn_kernel(
    own_ref, gin_own_ref, gin_in_ref, out_own_ref, out_in_ref, hidden_ref, cot_ref, skips_ref, segment_ref, scale_ref,
    w_out_ref, grad_hidden_ref, low_ref, block_out_ref, sums_ref, *grad_context_refs, pairs, parts, utt,
):
    own = own_ref[0]
    hidden = hidden_ref[...]
    unit, inverse = unit_norm(hidden)
    segment = segment_ref[...]
    block_out_ref[0] = (hidden + out_own_ref[...] + out_in_ref[...].astype(F32)).astype(BF)
    block_out_ref[1] = skips_ref[...]
    grad = gin_own_ref[...] + gin_in_ref[...].astype(F32)
    grad_hidden = cot_ref[...].astype(F32) + pull_norm(unit, inverse, grad, 1.0 + spread(segment, scale_ref[...]))
    grad_hidden_ref[...] = grad_hidden
    low = grad_hidden.astype(BF)
    low_ref[...] = low
    for b in range(parts):
        part = lax.dot_general(low, w_out_ref[:, own ^ b].reshape(pairs * LANES, -1), NT, preferred_element_type=F32).astype(BF)
        for pair in range(pairs):
            grad_context_refs[pair * parts + b][...] = part[:, pair * LANES : (pair + 1) * LANES]
    sums = jnp.concatenate([collect(segment, grad, utt), collect(segment, grad * unit, utt)], axis=0)

    @pl.when(pl.program_id(0) == 0)
    def _():
        sums_ref[...] = sums

    @pl.when(pl.program_id(0) > 0)
    def _():
        sums_ref[...] += sums


def turn(own, gin_own, gin_in, out_own, out_in, hidden, cot, skips, segment, scale, w_out, pairs, parts):
    frames, depth = hidden.shape
    utt = scale.shape[0]
    rows = 256
    row = lambda i, *_: (i, 0)
    wide = pl.BlockSpec((rows, depth), row)
    thin = pl.BlockSpec((rows, LANES), row)
    shape = lambda *s: jax.ShapeDtypeStruct(*s)
    return pl.pallas_call(
        functools.partial(turn_kernel, pairs=pairs, parts=parts, utt=utt),
        grid_spec=pltpu.PrefetchScalarGridSpec(
            num_scalar_prefetch=1,
            grid=(frames // rows,),
            in_specs=[wide] * 7
            + [thin, pl.BlockSpec(scale.shape, lambda i, *_: (0, 0)), pl.BlockSpec(w_out.shape, lambda i, *_: (0, 0, 0, 0))],
            out_specs=[wide] * 2
            + [pl.BlockSpec((2, rows, depth), lambda i, *_: (0, i, 0)), pl.BlockSpec((2 * utt, depth), lambda i, *_: (0, 0))]
            + [thin] * (pairs * parts),
        ),
        out_shape=[
            shape((frames, depth), F32),
            shape((frames, depth), BF),
            shape((2, frames, depth), BF),
            shape((2 * utt, depth), F32),
        ]
        + [shape((frames, LANES), BF)] * (pairs * parts),
        compiler_params=pltpu.CompilerParams(
            dimension_semantics=("arbitrary",), vmem_limit_bytes=48 * MIB
        ),
        cost_estimate=cost(15),
        name="turn",
    )(own, gin_own, gin_in, out_own, out_in, hidden, cot, skips, segment, scale, w_out)


def out_grad_kernel(*refs, pairs, parts, columns, at_row):
    low_ref, ctx_refs, (_, out_hbm, held, landing, local, sems) = refs[0], refs[1:-6], refs[-6:]
    d, z, core, half = mesh_spot(parts)
    part = core * half + z % half
    beside = partner_of(d, z, half, half)
    per = pairs * LANES // (2 * columns)
    greet([beside])
    if per < held.shape[3]:
        held[...] = jnp.zeros_like(held)
    low = low_ref[...]
    for b in range(parts):
        for pair in range(pairs):
            grad = lax.dot_general(ctx_refs[pair * parts + b][...], low, TN, preferred_element_type=F32)
            for k in range(LANES // per):
                spot = pair * (LANES // per) + k
                held[spot % 2, spot // 2, part ^ b, :per, :] = grad[k * per : (k + 1) * per].astype(BF)
    remote(held.at[1 - core], landing, sems, 0, beside).wait()

    @pl.loop(0, columns)
    def _(i):
        held[core, i] = (held[core, i].astype(F32) + landing[i].astype(F32)).astype(BF)

    copies = []
    for i in range(columns):
        copy = pltpu.make_async_copy(
            held.at[core, i], out_hbm.at[i * parts : (i + 1) * parts, at_row:, :], local.at[i]
        )
        copy.start()
        copies.append(copy)
    for copy in copies:
        copy.wait()


def out_grad(low, ctx_blocks, grad_feed, at_row, pairs, parts, columns):
    depth = low.shape[1]
    spare = grad_feed.shape[1] - at_row
    vmem = pl.BlockSpec(memory_space=pltpu.VMEM)
    anywhere = pl.BlockSpec(memory_space=pl.ANY)
    return pl.pallas_call(
        functools.partial(out_grad_kernel, pairs=pairs, parts=parts, columns=columns, at_row=at_row),
        in_specs=[vmem] * (1 + pairs * parts) + [anywhere],
        out_specs=anywhere,
        out_shape=jax.ShapeDtypeStruct(grad_feed.shape, BF),
        scratch_shapes=[
            pltpu.VMEM((2, columns, parts, spare, depth), BF),
            pltpu.VMEM((columns, parts, spare, depth), BF),
            pltpu.SemaphoreType.DMA((columns,)),
            pltpu.SemaphoreType.DMA((2,)),
        ],
        input_output_aliases={1 + pairs * parts: 0},
        compiler_params=pltpu.CompilerParams(
            collective_id=4, has_side_effects=True, vmem_limit_bytes=32 * MIB
        ),
        cost_estimate=cost(9),
        name="out_grad",
    )(low, *ctx_blocks, grad_feed)


class Sender:
    def __init__(self, sems, used=0):
        self.sems, self.used = sems, used
        self.d, self.z = lax.axis_index("dp"), lax.axis_index("tensor")

    def device(self, axis, bit):
        return (self.d ^ bit, self.z) if axis == "dp" else (self.d, self.z ^ bit)

    def side(self, axis, bit):
        return ((self.d if axis == "dp" else self.z) // bit) % 2

    def take(self, count):
        self.used += count
        return self.used - count

    def send(self, source, target, axis, bit):
        return remote(source, target, self.sems, self.take(1), self.device(axis, bit))


def rows_at(start, size):
    return pl.ds(pl.multiple_of(start, 16), size)


def few_rows(size):
    while size > 128:
        size //= 2
    return size


def add_rows(target, start, landing, landing_at, size):
    step = few_rows(size)

    @pl.loop(0, size // step)
    def _(i):
        here = rows_at(start + i * step, step)
        there = landing[rows_at(landing_at + i * step, step), :].astype(F32)
        target[here, :] = (target[here, :].astype(F32) + there).astype(target.dtype)


def sum_tree(sender, buffer, landing, down, turn_round, up, out, offset):
    size = buffer.shape[0] // 2
    starts, begin, kept = [0, size], [0, size], []
    for step in range(len(down[0])):
        kept.append(list(starts))
        size //= 2
        copies = []
        for side in range(2):
            axis, bit = down[side][step]
            upper = sender.side(axis, bit)
            lose = starts[side] + (1 - upper) * size
            copies.append(
                sender.send(buffer.at[rows_at(lose, size), :], landing.at[rows_at(begin[side], size), :], axis, bit)
            )
            starts[side] = starts[side] + upper * size
        yield
        for side in range(2):
            copies[side].wait()
            add_rows(buffer, starts[side], landing, begin[side], size)
            begin[side] += size
    yield from turn_round(starts, size)
    for step in reversed(range(len(down[0]))):
        copies = []
        for side in range(2):
            mine = out.at[rows_at(offset + starts[side], size), :]
            copies.append(sender.send(mine, mine, *up[side][step]))
        yield
        for side in range(2):
            copies[side].wait()
        starts = kept[step]
        size *= 2


def spread_sums(sender, own, held, out, parts):
    half = parts // 2
    slot = (sender.d // 2) * 2 + sender.z // half
    held[0] = own
    group = [("dp", 1)] + [("tensor", 1 << k) for k in range(parts.bit_length() - 2)]
    for at, (axis, bit) in enumerate(group):
        copy = sender.send(held.at[2 * at], held.at[2 * at + 1], axis, bit)
        yield
        copy.wait()
        held[2 * at + 2] = held[2 * at] + held[2 * at + 1]
    out[pl.ds(slot, 1)] = held[pl.ds(2 * len(group), 1)]
    size = 1
    rows_all = out.shape[0]
    for axis, bit in [("tensor", half)] + [("dp", 1 << k) for k in range(1, rows_all.bit_length() - 1)]:
        mine = out.at[pl.ds(slot // size * size, size)]
        copy = sender.send(mine, mine, axis, bit)
        yield
        copy.wait()
        size *= 2


def run_all(running):
    for work in list(running):
        try:
            next(work)
        except StopIteration:
            running.remove(work)


def bits_of(rows_all, parts):
    dp_bits = [1 << k for k in range(1, rows_all.bit_length() - 1)]
    return dp_bits, [1 << k for k in reversed(range(parts.bit_length() - 1))]


def finish_kernel(*refs, pairs, parts, utt, rows_all):
    cut = (pairs - 1) * parts
    prev_hbm, refs = refs[:cut], refs[cut:]
    own_hbm, refs = refs[:pairs], refs[pairs:]
    (
        normed_hbm, weight_hbm, base_hbm, base_in_hbm, grad_hbm, segment_ref, scale_ref,
        grad_base_ref, qkv_ref, sums_ref,
        prev, own, normed, weight, base, grad_hidden, arrived, total, qkv_held, qkv_in, loads, sems,
    ) = refs
    d, z, core, half = mesh_spot(parts)
    part = core * half + z % half
    stays = z // half == core
    frames = normed.shape[1]
    width = pairs * LANES

    there = ((d - core) + z // half, core * half + z % half)
    dp_bits, _ = bits_of(rows_all, parts)
    near = [partner_of(d, z, b, half) for b in range(1, parts)] + [(d, z ^ half)] + [(d ^ bit, z) for bit in dp_bits]
    barrier = pltpu.get_barrier_semaphore()
    for device in near:
        pl.semaphore_signal(barrier, inc=1, device_id=device, device_id_type=pl.DeviceIdType.MESH)

    @pl.when(jnp.logical_not(stays))
    def _():
        pl.semaphore_signal(barrier, inc=1, device_id=there, device_id_type=pl.DeviceIdType.MESH)
        pl.semaphore_wait(barrier, len(near) + 1)

    @pl.when(stays)
    def _():
        pl.semaphore_wait(barrier, len(near))

    sends = []
    order = [b for b in range(1, parts) if b % half] + [b for b in range(1, parts) if b % half == 0]
    for b in order:
        sends.append(
            (b, remote(own_hbm[-1].at[b], arrived.at[b - 1], sems, b - 1, partner_of(d, z, b, half)))
        )

    def load(at, source, target):
        copy = pltpu.make_async_copy(source, target, loads.at[at])
        copy.start()
        return copy

    first = [load(0, normed_hbm, normed)]
    for pair in range(pairs):
        first.append(load(1 + pair, own_hbm[pair], own.at[pair]))
    at = 1 + pairs
    four = pl.ds(core * 4, 4)
    second = [
        load(at, weight_hbm.at[four], weight.at[four]),
        remote(weight_hbm.at[four], weight.at[four], sems, parts - 1, (d ^ 1, z)),
    ]
    for k in range(cut):
        second.append(load(at + 1 + k, prev_hbm[k], prev.at[k]))
    at += 1 + cut
    third = [load(at, grad_hbm, grad_hidden)]

    @pl.when(stays)
    def _():
        pltpu.make_async_copy(base_hbm, base, loads.at[at + 1]).start()

    @pl.when(jnp.logical_not(stays))
    def _():
        pltpu.make_async_copy(base_in_hbm, base, loads.at[at + 1]).start()

    for copy in first:
        copy.wait()
    for kind in range(3):
        for pair in range(pairs):

            def gather(b, carry):
                return carry + lax.dot_general(own[pair, b, kind], normed[b], TN, preferred_element_type=F32)

            grad = lax.fori_loop(0, parts, gather, jnp.zeros((LANES, normed.shape[2]), F32)).astype(BF)
            wide = qkv_held.shape[1]
            for k in range(normed.shape[2] // wide):
                at_row = k * 3 * width + kind * width + pair * LANES
                qkv_held[at_row : at_row + LANES, :] = grad[:, k * wide : (k + 1) * wide]

    sender = Sender(sems, parts)
    down = [
        [("dp", bit) for bit in dp_bits] + [("tensor", half)],
        [("dp", bit) for bit in reversed(dp_bits)] + [("tensor", half)],
    ]

    def go_home(starts, size):
        at_sem = sender.take(2)

        def copies():
            return [
                remote_copy(
                    qkv_held.at[rows_at(starts[side], size), :],
                    qkv_ref.at[rows_at(starts[side], size), :],
                    sems,
                    at_sem + side,
                    there,
                )
                for side in range(2)
            ]

        @pl.when(stays)
        def _():
            for side in range(2):
                here = rows_at(starts[side], size)
                qkv_ref[here, :] = qkv_held[here, :]

        @pl.when(jnp.logical_not(stays))
        def _():
            for copy in copies():
                copy.start()

        yield

        @pl.when(jnp.logical_not(stays))
        def _():
            for copy in copies():
                copy.wait()

        for side in range(2):
            starts[side] = starts[side] + (core - z // half) * size

    up = [line[:-1] + [("dp", 1)] for line in down]
    running = [sum_tree(sender, qkv_held, qkv_in, down, go_home, up, qkv_ref, 0)]
    run_all(running)

    for copy in second:
        copy.wait()
    rows = 256

    def add_block(source, b, pair, fresh):
        weights = jnp.concatenate(
            [weight[:, part ^ b, kind * pairs + pair].reshape(LANES, -1) for kind in range(3)],
            axis=0,
        )

        @pl.loop(0, frames // rows)
        def _(i):
            here = pl.ds(pl.multiple_of(i * rows, rows), rows)
            block = jnp.concatenate([source[kind, here, :] for kind in range(3)], axis=1)
            term = jnp.dot(block, weights, preferred_element_type=F32)
            if fresh:
                total[here, :] = term
            else:
                total[here, :] += term

    add_block(own.at[pairs - 1, 0], 0, pairs - 1, True)
    run_all(running)
    for pair in range(pairs - 1):
        for b in range(parts):
            add_block(prev.at[pair * parts + b], b, pair, False)
            if b % 2:
                run_all(running)
    for b, copy in sorted(sends, key=lambda item: (item[0] % half, item[0])):
        copy.wait()
        add_block(arrived.at[b - 1], b, pairs - 1, False)
        run_all(running)

    for copy in third:
        copy.wait()
    pltpu.make_async_copy(base_hbm, base, loads.at[at + 1]).wait()
    sums_ref[...] = jnp.zeros_like(sums_ref)

    @pl.loop(0, frames // rows)
    def _(i):
        here = pl.ds(pl.multiple_of(i * rows, rows), rows)
        unit, inverse = unit_norm(base[here, :].astype(F32))
        grad = total[here, :]
        segment = segment_ref[here, :]
        pulled = pull_norm(unit, inverse, grad, 1.0 + spread(segment, scale_ref[...]))
        grad_base_ref[here, :] = (grad_hidden[here, :] + pulled).astype(BF)
        sums_ref[...] += jnp.concatenate([collect(segment, grad, utt), collect(segment, grad * unit, utt)], axis=0)

    while running:
        run_all(running)


def finish(
    prev, own, normed_all, weight, base, base_in, grad_hidden, segment, scale, pairs, parts, rows_all
):
    frames, depth = base.shape
    utt = scale.shape[0]
    units = 3 * pairs * LANES
    wide = depth
    while units * depth // wide % (16 * rows_all * 2):
        wide //= 2
    qkv_shape = (units * depth // wide, wide)
    copies = parts + 2 + 5 * rows_all.bit_length() + parts.bit_length()
    anywhere = pl.BlockSpec(memory_space=pl.ANY)
    vmem = pl.BlockSpec(memory_space=pltpu.VMEM)
    shape = lambda *s: jax.ShapeDtypeStruct(*s)
    block = (3, frames, LANES)
    return pl.pallas_call(
        functools.partial(finish_kernel, pairs=pairs, parts=parts, utt=utt, rows_all=rows_all),
        in_specs=[anywhere] * (len(prev) + pairs + 5) + [vmem] * 2,
        out_specs=[vmem] * 3,
        out_shape=[
            shape((frames, depth), BF),
            shape(qkv_shape, BF),
            shape((2 * utt, depth), F32),
        ],
        scratch_shapes=[
            pltpu.VMEM((max(len(prev), 1),) + block, BF),
            pltpu.VMEM((pairs, parts) + block, BF),
            pltpu.VMEM(normed_all.shape, BF),
            pltpu.VMEM(weight.shape, BF),
            pltpu.VMEM((frames, depth), BF),
            pltpu.VMEM((frames, depth), F32),
            pltpu.VMEM((parts - 1,) + block, BF),
            pltpu.VMEM((frames, depth), F32),
            pltpu.VMEM(qkv_shape, BF),
            pltpu.VMEM(qkv_shape, BF),
            pltpu.SemaphoreType.DMA((4 + pairs + len(prev),)),
            pltpu.SemaphoreType.DMA((2 * copies,)),
        ],
        compiler_params=pltpu.CompilerParams(
            collective_id=1, has_side_effects=True, vmem_limit_bytes=56 * MIB
        ),
        cost_estimate=cost(60),
        name="finish",
    )(*prev, *own, normed_all, weight, base, base_in, grad_hidden, segment, scale)


def sums_kernel(
    inputs_hbm, inputs_in_hbm, skips_hbm, skips_in_hbm, grad_ref, sums_ref, skip_out_ref, sums_out_ref, grad_in_hbm,
    frames_in, away, held, first_in, half_in, sums_in, loads, sems, *, rows_all, parts,
):
    d, z, core, half = mesh_spot(parts)
    stays = z // half == core
    leaves = jnp.logical_not(stays)
    dp_bits, z_bits = bits_of(rows_all, parts)
    there = ((d - core) + z // half, core * half + z % half)
    depth = grad_ref.shape[1]
    half_rows, width = held.shape

    for at, (source, source_in) in enumerate(((inputs_hbm, inputs_in_hbm), (skips_hbm, skips_in_hbm))):
        slot = frames_in.at[1 - core if at == 0 else core]

        @pl.when(stays)
        def _():
            pltpu.make_async_copy(source, slot, loads.at[at]).start()

        @pl.when(leaves)
        def _():
            pltpu.make_async_copy(source_in, slot, loads.at[at]).start()

    sender = Sender(sems, PIECES)
    near = [("dp", 1)] + [("dp", bit) for bit in dp_bits] + [("tensor", bit) for bit in z_bits]
    barrier = pltpu.get_barrier_semaphore()
    for axis, bit in near:
        pl.semaphore_signal(
            barrier, inc=1, device_id=sender.device(axis, bit), device_id_type=pl.DeviceIdType.MESH
        )

    @pl.when(leaves)
    def _():
        pl.semaphore_signal(barrier, inc=1, device_id=there, device_id_type=pl.DeviceIdType.MESH)
        pl.semaphore_wait(barrier, len(near) + 1)

    @pl.when(stays)
    def _():
        pl.semaphore_wait(barrier, len(near))

    def start_move(k):
        @pl.when(leaves)
        def _():
            in_pieces(grad_ref, grad_in_hbm, sems, 0, there, [k])[0].start()

    def settle(starts, size):
        for side in range(2):
            skip_out_ref[rows_at(offset + starts[side], size), :] = held[rows_at(starts[side], size), :]
        yield

    offset = core * half_rows

    def skips():
        for slot in range(2):
            pltpu.make_async_copy(inputs_hbm, frames_in.at[slot], loads.at[slot]).wait()
        for slot, target in ((0, away), (1, held)):

            @pl.loop(0, depth // 256)
            def _(i):
                cut = frames_in[slot, :, pl.ds(pl.multiple_of(i * 256, 256), 256)]
                grad = lax.dot_general(cut, grad_ref[...], TN, preferred_element_type=F32).astype(BF)
                for k in range(depth // width):
                    target[rows_at(k * depth + i * 256, 256), :] = grad[:, k * width : (k + 1) * width]

            if slot == 0:
                copy = sender.send(away, first_in, "dp", 1)
                yield
        copy.wait()
        add_rows(held, 0, first_in, 0, half_rows)
        down = [
            [("dp", bit) for bit in dp_bits] + [("tensor", bit) for bit in z_bits],
            [("dp", bit) for bit in reversed(dp_bits)] + [("tensor", bit) for bit in z_bits],
        ]
        yield from sum_tree(sender, held, half_in, down, settle, down, skip_out_ref, offset)
        mine = skip_out_ref.at[rows_at(offset, half_rows), :]
        copy = sender.send(mine, mine, "dp", 1)
        yield
        copy.wait()

    running = [skips(), spread_sums(sender, sums_ref[...], sums_in, sums_out_ref, parts)]
    rounds = 0
    later = 1 + len(dp_bits) + 2 * len(z_bits) + 1
    while running:
        if rounds in (0, 1, later, later + 1):
            start_move(rounds if rounds < 2 else rounds - later + 2)
        rounds += 1
        run_all(running)

    @pl.when(leaves)
    def _():
        for copy in in_pieces(grad_ref, grad_in_hbm, sems, 0, there):
            copy.wait()


def sums(inputs, inputs_in, skips, skips_in, grad_base, utterance_sums, rows_all, parts):
    frames, depth = inputs.shape
    devices = rows_all * parts
    width = min(depth, depth * depth // (16 * devices))
    half_rows = depth * depth // width
    stages = rows_all.bit_length() + parts.bit_length() - 3
    copies = PIECES + 2 + 4 * stages + rows_all.bit_length() + parts.bit_length()
    vmem = pl.BlockSpec(memory_space=pltpu.VMEM)
    anywhere = pl.BlockSpec(memory_space=pl.ANY)
    shape = lambda *s: jax.ShapeDtypeStruct(*s)
    skip_sum, all_sums, grad_base_in = pl.pallas_call(
        functools.partial(sums_kernel, rows_all=rows_all, parts=parts),
        in_specs=[anywhere] * 4 + [vmem] * 2,
        out_specs=[vmem] * 2 + [anywhere],
        out_shape=[
            shape((2 * half_rows, width), BF),
            shape((rows_all,) + utterance_sums.shape, F32),
            shape((frames, depth), BF),
        ],
        scratch_shapes=[pltpu.VMEM((2, frames, depth), BF)]
        + [pltpu.VMEM((half_rows, width), BF)] * 4
        + [
            pltpu.VMEM((2 * parts.bit_length() - 1,) + utterance_sums.shape, F32),
            pltpu.SemaphoreType.DMA((2,)),
            pltpu.SemaphoreType.DMA((2 * copies,)),
        ],
        compiler_params=pltpu.CompilerParams(
            collective_id=0, has_side_effects=True, vmem_limit_bytes=56 * MIB
        ),
        cost_estimate=cost(100),
        name="sums",
    )(inputs, inputs_in, skips, skips_in, grad_base, utterance_sums)
    skip_sum = skip_sum.reshape(2, depth // width, depth, width)
    skip_sum = jnp.transpose(skip_sum, (0, 2, 1, 3)).reshape(2, depth, depth)
    return skip_sum, all_sums, grad_base_in


def front_kernel(
    ends_ref, inputs_ref, skips_ref, w_in_ref, w_res_ref, segment_ref, shift_ref, scale_ref, rate_ref, weight_hbm, w_out_ref,
    base_ref, out_ref, cos_ref, sin_ref, qmark_ref, kmark_ref, weight_in_hbm, w_out_all_ref, away, local, sems,
    *, parts, utt,
):
    d, z, core, half = mesh_spot(parts)
    stays = z // half == core
    leaves = jnp.logical_not(stays)
    there = ((d - core) + z // half, core * half + z % half)
    frames = base_ref.shape[0]
    rows = 256
    chunks = frames // rows

    barrier = pltpu.get_barrier_semaphore()
    near = [partner_of(d, z, b, half) for b in range(1, half + 1)] + [(d ^ bit, z) for bit in (2, 4, 6)]
    near += [(d, z ^ k) for k in range(half, parts)]
    for device in near:
        pl.semaphore_signal(barrier, inc=1, device_id=device, device_id_type=pl.DeviceIdType.MESH)

    @pl.when(leaves)
    def _():
        pl.semaphore_signal(barrier, inc=1, device_id=there, device_id_type=pl.DeviceIdType.MESH)
        pl.semaphore_wait(barrier, len(near) + 1)

    @pl.when(stays)
    def _():
        pl.semaphore_wait(barrier, len(near))

    def here(k):
        return pl.ds(pl.multiple_of(k * rows, rows), rows)

    def copy(kind, k, source, target, device):
        at = kind * chunks + k
        return pltpu.make_async_remote_copy(
            src_ref=source,
            dst_ref=target,
            send_sem=sems.at[2 * at],
            recv_sem=sems.at[2 * at + 1],
            device_id=device,
            device_id_type=pl.DeviceIdType.MESH,
        )

    def moving(k):
        return copy(0, k, away.at[here(k), :], out_ref.at[0, here(k), :], there)

    quarter = weight_hbm.shape[0] // 4
    column = d // 2 % 4

    def weight_part(k):
        cut = pl.ds(pl.multiple_of((column ^ k) * quarter, 16), quarter)
        if k == 0:
            return copy(parts, 0, weight_hbm.at[cut, :], weight_in_hbm.at[cut, :], there)
        own = pl.ds(pl.multiple_of(column * quarter, 16), quarter)
        return copy(parts, k, weight_in_hbm.at[own, :], weight_in_hbm.at[own, :], (d ^ (2 * k), z))

    @pl.when(leaves)
    def _():
        weight_part(0).start()

    @pl.when(stays)
    def _():
        pltpu.make_async_copy(weight_hbm, weight_in_hbm, local).start()

    eighth = d // 2 % 4 + 4 * core
    per = w_out_all_ref.shape[2]
    w_out_all_ref[eighth, z] = w_out_ref[pl.ds(pl.multiple_of(eighth * per, 16), per), :]

    def w_out_part(k):
        if k < parts:
            cut = w_out_all_ref.at[eighth, z]
            return copy(parts, 3 + k, cut, cut, (d, z ^ k))
        size = 1 << (k - parts)
        cut = w_out_all_ref.at[pl.ds(eighth // size * size, size)]
        return copy(parts, 3 + k, cut, cut, (d ^ (2, 4, 1)[k - parts], z))

    for k in range(1, parts):
        w_out_part(k).start()

    def across(b, k):
        return copy(b, k, out_ref.at[0, here(k), :], out_ref.at[b, here(k), :], partner_of(d, z, b, half))

    def beside(b, k):
        return copy(
            half + b, k, out_ref.at[b, here(k), :], out_ref.at[half + b, here(k), :], partner_of(d, z, half, half)
        )

    def spread_own(k):
        for b in range(1, half):
            across(b, k).start()
        beside(0, k).start()

    @pl.loop(0, chunks)
    def _(k):
        at = here(k)
        base = jnp.dot(inputs_ref[at, :], w_in_ref[...], preferred_element_type=F32)
        base = base + jnp.dot(skips_ref[at, :], w_res_ref[...], preferred_element_type=F32)
        base_ref[at, :] = base.astype(BF)
        unit, _ = unit_norm(base)
        segment = segment_ref[at, :]
        normed = (unit * (1.0 + spread(segment, scale_ref[...])) + spread(segment, shift_ref[...])).astype(BF)

        @pl.when(stays)
        def _():
            out_ref[0, at, :] = normed
            spread_own(k)

        @pl.when(leaves)
        def _():
            away[at, :] = normed
            moving(k).start()

    part = core * half + z % half

    @pl.loop(0, parts * chunks)
    def _(i):
        at = here(i)
        place = (part ^ (i // chunks)) * frames + (i % chunks) * rows
        place = place + lax.broadcasted_iota(jnp.int32, (rows, LANES), 0)
        lane = lax.broadcasted_iota(jnp.int32, (rows, LANES), 1)
        segment = jnp.zeros((rows, LANES), jnp.int32)
        start = jnp.zeros((rows, LANES), jnp.int32)
        for u in range(utt - 1):
            past = place >= ends_ref[u]
            segment = jnp.where(past, u + 1, segment)
            start = jnp.where(past, ends_ref[u], start)
        angle = (place - start).astype(F32) * rate_ref[0:1, :]
        cos_ref[at, :] = jnp.cos(angle)
        sin_ref[at, :] = jnp.sin(angle) * rate_ref[1:2, :]
        other = jnp.logical_and(lane < utt, lane != segment)
        qmark_ref[at, :] = jnp.where(other, MASKED, 0.0).astype(BF)
        shown = jnp.where(lane < utt + 3, 1.0, 0.0)
        kmark_ref[at, :] = jnp.where(other, 0.0, shown).astype(BF)

    for k in range(1, parts):
        w_out_part(k).wait()
    w_out_part(parts).start()

    @pl.when(leaves)
    def _():
        weight_part(0).wait()
        for k in range(1, 4):
            weight_part(k).start()

        @pl.loop(0, chunks)
        def _(k):
            moving(k).wait_recv()
            spread_own(k)

    w_out_part(parts).wait()
    w_out_part(parts + 1).start()

    @pl.loop(0, chunks)
    def _(k):
        for b in range(1, half):
            across(b, k).wait_recv()
            beside(b, k).start()

    w_out_part(parts + 1).wait()
    w_out_part(parts + 2).start()

    @pl.loop(0, chunks)
    def _(k):
        for b in range(half):
            beside(b, k).wait_recv()
            beside(b, k).wait_send()
        for b in range(1, half):
            across(b, k).wait_send()

    @pl.when(leaves)
    def _():
        @pl.loop(0, chunks)
        def _(k):
            moving(k).wait_send()

        for k in range(1, 4):
            weight_part(k).wait()

    @pl.when(stays)
    def _():
        pltpu.make_async_copy(weight_hbm, weight_in_hbm, local).wait()

    w_out_part(parts + 2).wait()


def front(ends, inputs, skips, w_in, w_res, segment, shift, scale, rate, weight, w_out, parts):
    frames, depth = inputs.shape
    utt = ends.shape[0]
    vmem = pl.BlockSpec(memory_space=pltpu.VMEM)
    return pl.pallas_call(
        functools.partial(front_kernel, parts=parts, utt=utt),
        in_specs=[pl.BlockSpec(memory_space=pltpu.SMEM)] + [vmem] * 8 + [pl.BlockSpec(memory_space=pl.ANY), vmem],
        out_specs=[vmem] * 6 + [pl.BlockSpec(memory_space=pl.ANY), vmem],
        out_shape=[
            jax.ShapeDtypeStruct((frames, depth), BF),
            jax.ShapeDtypeStruct((parts, frames, depth), BF),
            jax.ShapeDtypeStruct((parts * frames, LANES), F32),
            jax.ShapeDtypeStruct((parts * frames, LANES), F32),
            jax.ShapeDtypeStruct((parts * frames, LANES), BF),
            jax.ShapeDtypeStruct((parts * frames, LANES), BF),
            jax.ShapeDtypeStruct(weight.shape, BF),
            jax.ShapeDtypeStruct((8, parts, w_out.shape[0] // 8, depth), BF),
        ],
        scratch_shapes=[
            pltpu.VMEM((frames, depth), BF),
            pltpu.SemaphoreType.DMA,
            pltpu.SemaphoreType.DMA((2 * (parts * (frames // 256) + 6 + parts),)),
        ],
        compiler_params=pltpu.CompilerParams(
            collective_id=2, has_side_effects=True, vmem_limit_bytes=48 * MIB
        ),
        cost_estimate=cost(75),
        name="front",
    )(ends, inputs, skips, w_in, w_res, segment, shift, scale, rate, weight, w_out)


def dot(a, b, dims=(((1,), (0,)), ((), ()))):
    return lax.dot_general(a, b, dims, preferred_element_type=F32)


def after(value, token):
    return lax.optimization_barrier((value, token))[0]


def on_device(
    inputs, skip_input, lengths, time_steps, w_skip_in, w_skip_res, w_ada, w_qkv, w_out, w_up, w_down, cotangent
):
    parts = lax.axis_size("tensor")
    rows_all = lax.axis_size("dp")
    half = parts // 2
    columns = rows_all // 2
    d = lax.axis_index("dp")
    z = lax.axis_index("tensor")
    core, column = d % 2, d // 2
    stays = z // half == core
    part = core * half + z % half
    inputs, skip_input, cotangent = inputs[0], skip_input[0], cotangent[0]
    frames, depth = inputs.shape
    length = frames * parts
    ws = w_qkv.shape[2]
    pairs = ws // LANES
    utt = lengths.shape[1]
    both = ("dp", "tensor")

    def moved(value):
        pattern = [
            (i * parts + j, ((i // 2) * 2 + j // half) * parts + (i % 2) * half + j % half)
            for i in range(rows_all)
            for j in range(parts)
            if i % 2 != j // half
        ]
        return lax.ppermute(value, both, pattern)

    def partner(value, b):
        pattern = [
            (i * parts + j, (i ^ (b // half)) * parts + (j // half) * half + ((j % half) ^ (b % half)))
            for i in range(rows_all)
            for j in range(parts)
        ]
        return lax.ppermute(value, both, pattern)

    def exchange(blocks):
        return [blocks[0]] + [partner(blocks[b], b) for b in range(1, parts)]

    same_core = [[2 * i + k for i in range(columns)] for k in range(2)]

    other_lengths = partner(lengths, half)
    other_steps = partner(time_steps, half)
    lengths_work = jnp.where(stays, lengths, other_lengths)[0]
    steps_work = jnp.where(stays, time_steps, other_steps)[0]

    time_rate = jnp.exp(
        -math.log(10000.0) * (jnp.arange(w_ada.shape[0] // 2, dtype=F32) / (w_ada.shape[0] // 2))
    )

    def embed(steps):
        phases = steps.astype(F32)[:, None] * time_rate
        return jax.nn.silu(jnp.concatenate([jnp.sin(phases), jnp.cos(phases)], axis=-1)).astype(BF)

    def wide_segment(row_lengths, places):
        segment, _, _ = frame_marks(row_lengths, places, utt)
        return jnp.broadcast_to(segment[:, None], (places.shape[0], LANES))

    spot = jnp.arange(frames, dtype=jnp.int32)
    mods_home = dot(embed(time_steps[0]), w_ada[:, : 2 * depth])
    qkv_rows = jnp.transpose(w_qkv, (0, 2, 1)).reshape(3 * ws, depth)
    rotary_rate = jnp.exp(-math.log(10000.0) * (2.0 * jnp.arange(HEAD_DIM // 2, dtype=F32) / HEAD_DIM))
    sign = jnp.where(jnp.arange(LANES) % HEAD_DIM < HEAD_DIM // 2, -1.0, 1.0).astype(F32)
    base_home, normed_all, cosine, sine, qmark, kmark, w_mine, w_out_all = front(
        jnp.cumsum(lengths_work, dtype=jnp.int32),
        inputs,
        skip_input,
        w_skip_in,
        w_skip_res,
        wide_segment(lengths[0], z * frames + spot),
        mods_home[:, :depth],
        mods_home[:, depth:],
        jnp.stack([jnp.tile(rotary_rate, 4), sign]),
        qkv_rows,
        w_out,
        parts,
    )

    per_q, per_o = 3 * ws // rows_all, ws // rows_all
    units = w_down.shape[0]
    per_u = units // rows_all
    slice_feed = jnp.concatenate(
        [
            jnp.transpose(lax.dynamic_slice_in_dim(w_up, d * per_u, per_u, 1)),
            lax.dynamic_slice_in_dim(w_down, d * per_u, per_u, 0),
        ]
    )
    feed_rows = lax.all_gather(slice_feed, "tensor")
    feed_rows = lax.all_gather(after(feed_rows, base_home), "dp", axis_index_groups=same_core)
    feed_rows = feed_rows.reshape(columns * parts, 2, per_u, depth)

    cotangent = after(cotangent, base_home)
    cot = jnp.where(stays, cotangent, moved(cotangent))
    base_in = moved(after(base_home, cot))

    silu_work = embed(steps_work)
    mods = dot(silu_work, w_ada)
    shift_one, scale_one, shift_two, scale_two = [mods[:, k * depth : (k + 1) * depth] for k in range(4)]
    segment_here = wide_segment(lengths_work, part * frames + spot)

    qkv = project(normed_all.reshape(length, depth), w_mine, cosine, sine, pairs)

    def ranges(size, other):
        per = frames // size
        stored = jnp.arange(length // size, dtype=jnp.int32)
        natural = (part ^ (stored // per)) * per + stored % per
        return block_ranges(lengths_work, natural, size, other)

    own = jnp.stack([part.astype(jnp.int32), stays.astype(jnp.int32)])
    bq, bk = 512, 512
    low, high = ranges(bq, bk)
    low_back, high_back = ranges(bk, bq)
    ctx_pairs, lse_pairs, ctx_mine = [], [], []
    for pair in range(pairs):
        ctx, lse = attend(after(qkv, cot) if pair == pairs - 1 else qkv, pair, qmark, kmark, own, low, high, bq, bk, frames)
        ctx_pairs.append(ctx)
        lse_pairs.append(lse)
        ctx_mine += exchange([ctx[b] for b in range(parts)])
    hidden, ffn_in = join(
        own, ctx_mine, w_out_all, base_home, base_in, segment_here, shift_two, scale_two, pairs, parts
    )

    cot_other = partner(cot, half)
    spare = max(per_o, 16)
    heads = qkv_rows.reshape(3 * pairs, 8, LANES // 8, depth)
    out_own, out_send, gin_own, gin_send, grad_feed, inputs_in, w_heads = feed(
        ffn_in, cot, cot_other, feed_rows, inputs, heads, spare, parts
    )
    grad_hidden, low_grad, block_out, sums_two, *grad_context = turn(
        own, gin_own, partner(gin_send, half), out_own, partner(out_send, half), hidden, cot, skip_input, segment_here,
        scale_two,
        w_out_all, pairs, parts,
    )

    grad_feed = out_grad(low_grad, ctx_mine, grad_feed, 2 * per_u, pairs, parts, columns)
    grad_feed = grad_feed.reshape(columns, parts, 2 * per_u + spare, depth)
    feed_sum = lax.psum_scatter(grad_feed, "dp", scatter_dimension=0, axis_index_groups=same_core)
    grad_feed = lax.psum_scatter(feed_sum, "tensor", scatter_dimension=0)
    feed_shard = grad_feed
    grad_feed = lax.all_gather(grad_feed, "dp")
    grad_up = jnp.transpose(grad_feed[:, :per_u].reshape(units, depth)).astype(F32)
    grad_down = grad_feed[:, per_u : 2 * per_u].reshape(units, depth).astype(F32)
    grad_out = grad_feed[:, 2 * per_u : 2 * per_u + per_o].reshape(ws, depth).astype(F32)

    grad_mine = []
    for pair in range(pairs):
        grad = jnp.stack(exchange(grad_context[pair * parts : (pair + 1) * parts]))
        if pair == pairs - 1 and pairs > 1:
            grad = after(grad, feed_sum)
        grads = attend_back(
            qkv, pair, grad, ctx_pairs[pair], lse_pairs[pair], qmark, kmark, cosine, sine, own,
            low_back, high_back, bq, bk, utt, frames,
        )
        grad_mine.append(grads)

    returned = []
    for grads in grad_mine[:-1]:
        returned += exchange([grads[b] for b in range(parts)])
    block_out_in, skips_in = moved(block_out)
    grad_base, grad_qkv, sums_one = finish(
        returned, after(grad_mine, feed_shard), normed_all, w_heads, base_home, base_in, grad_hidden, segment_here, scale_one,
        pairs, parts, rows_all,
    )
    silu_rows = jnp.pad(silu_work.astype(F32) * (1.0 / parts), ((0, 0), (0, depth - silu_work.shape[1])))
    skip_sum, all_sums, grad_base_in = sums(
        inputs, inputs_in, skip_input, skips_in, grad_base, jnp.concatenate([sums_one, sums_two, silu_rows]),
        rows_all, parts,
    )
    grad_qkv = grad_qkv.reshape(-1, 3, ws, grad_qkv.shape[1])
    grad_qkv = jnp.transpose(grad_qkv, (1, 0, 3, 2)).reshape(3, depth, ws).astype(F32)
    grad_skip = skip_sum.astype(F32)
    grad_base_home = jnp.where(stays, grad_base, grad_base_in)
    grad_inputs = dot(grad_base_home, w_skip_in, NT)
    grad_skips = dot(grad_base_home, w_skip_res, NT)
    block_out = jnp.where(stays, block_out[0], block_out_in).astype(F32)

    all_sums = all_sums.reshape(rows_all, 5, utt, depth)
    silu_all = all_sums[:, 4, :, : w_ada.shape[0]].reshape(rows_all * utt, w_ada.shape[0])
    all_sums = jnp.concatenate([all_sums[:, k] for k in range(4)], axis=-1).reshape(rows_all * utt, 4 * depth)
    grad_ada = jnp.einsum("ut,um->tm", silu_all, all_sums, precision=lax.Precision.HIGHEST)

    return (
        block_out[None],
        grad_inputs[None],
        grad_skips[None],
        grad_skip[0],
        grad_skip[1],
        grad_ada,
        grad_qkv,
        grad_out,
        grad_up,
        grad_down,
    )


def solution(mesh):
    placed = (
        P("dp", "tensor", None),
        P("dp", "tensor", None),
        P("dp", None),
        P("dp", None),
        P(),
        P(),
        P(),
        P(None, None, "tensor"),
        P("tensor", None),
        P(None, "tensor"),
        P("tensor", None),
        P("dp", "tensor", None),
    )
    return jax.shard_map(
        on_device,
        mesh=mesh,
        in_specs=placed,
        out_specs=(
            P("dp", "tensor", None),
            P("dp", "tensor", None),
            P("dp", "tensor", None),
            P(),
            P(),
            P(),
            P(None, None, "tensor"),
            P("tensor", None),
            P(None, "tensor"),
            P("tensor", None),
        ),
        check_vma=False,
    )
```

time: 1340 us -> 867 us (0.65); the launches traced: 1350 us -> 858 us
  waiting for transfers between devices: 277 us -> 28.2 us
  Pallas kernels: 551 us -> 714 us
  starting transfers between devices: 166 us -> 25.1 us
  local copies, waits for them, and re-layouts: 129 us -> 46.2 us
  other arithmetic: 91.6 us -> 15 us
  matrix products: 87.6 us -> 14.4 us
  blocking collectives: 34.1 us -> 0 us
    pallas_call x2 -> x7, Pallas kernels: 264 us -> 460 us  [the longest x1 128 us: front(): pl.pallas_call(functools.partial(front_kernel, parts=parts, utt=utt), in_...]
    ppermute x28 -> x20, starting transfers between devices: 150 us -> 21 us  [partner(): return lax.ppermute(value, both, pattern)]
    all_gather x5 -> x3, waiting for transfers between devices: 95.3 us -> 0.01 us  [the longest x1 0.01 us: on_device(): feed_rows = lax.all_gather(slice_feed, 'tensor')]
    psum x2 -> x0, waiting for transfers between devices: 87.1 us -> none  [the longest x1 54.8 us: on_device(): grad_qkv = lax.psum(grad_qkv, 'dp').astype(F32).reshape(depth, 3, ws)]
    dot_general x13 -> x4, matrix products: 62.9 us -> 9.41 us  [dot(): return lax.dot_general(a, b, dims, preferred_element_type=F32)]
    ppermute x28 -> x20, waiting for transfers between devices: 72 us -> 28.1 us  [partner(): return lax.ppermute(value, both, pattern)]
    all_gather x1 -> x0, blocking collectives: 34.1 us -> none  [on_device(): steps_all = lax.all_gather(time_steps[0], 'dp')]
    slice x13 -> x11, local copies, waits for them, and re-layouts: 34.7 us -> 4.79 us  [the longest x1 2.69 us: on_device(): grad_down = grad_feed[:, per_u:2 * per_u].reshape(units, depth).astype(F32)]
  transfers between devices with their start and end apart: 45 -> 28, of which waited for: 19 -> 7; matrix products, arithmetic and copies ran while one was open for 18% -> 5% of each run, Pallas kernels for 35% -> 67%
where the time goes in v2:
time: 867 us; the launch traced here: 858 us
  Pallas kernels  714 us (82%)
  local copies, waits for them, and re-layouts  46.2 us (5%)
  waiting for transfers between devices  28.2 us (3%)
  starting transfers between devices  25.1 us (3%)
  between operations  15.2 us (2%)
  other arithmetic  15 us (2%)
  matrix products  14.4 us (2%)
    pallas_call x2, Pallas kernels, attend_back(): pl.pallas_call(functools.partial(attend_back_kernel, bq=bq, bk=bk, utt=ut...  151 us
    pallas_call x1, Pallas kernels, front(): pl.pallas_call(functools.partial(front_kernel, parts=parts, utt=utt), in_...  128 us
    pallas_call x1, Pallas kernels, feed(): pl.pallas_call(functools.partial(feed_kernel, parts=parts), grid=(groups...  115 us
    pallas_call x1, Pallas kernels, sums(): pl.pallas_call(functools.partial(sums_kernel, rows_all=rows_all, parts=pa...  110 us
    pallas_call x2, Pallas kernels, attend(): pl.pallas_call(functools.partial(attend_kernel, bq=bq, bk=bk, per_part=pe...  91.8 us
    pallas_call x1, Pallas kernels, finish(): pl.pallas_call(functools.partial(finish_kernel, pairs=pairs, parts=parts,...  78.6 us
    ppermute x20, waiting for transfers between devices, partner(): return lax.ppermute(value, both, pattern)  28.1 us
    ppermute x20, starting transfers between devices, partner(): return lax.ppermute(value, both, pattern)  21 us
  transfers between devices with their start and end apart: 28, of which 7 were waited for; matrix products, arithmetic and copies ran while one was open for 5% of the time, Pallas kernels for 67%

profile of v2, /device:TPU:0, one launch (start us, length us, event | category | flops | bytes accessed | tf_op | source)
XLA Modules:
  0.0 858.2 jit_solution(8700955687725659156)
XLA Ops:
  7.8 0.9 copy-done
  9.0 1.0 constant_dynamic-slice_fusion
  10.0 0.8 pad_maximum_fusion.2
  11.2 2.8 copy.56
  15.0 127.7 %front.1 = (bf16[1024,1024]{1,0:T(8,128)(2,1)}, bf16[4,1024,1024]{2,1,0:T(8,128)(2,1)}, f32[4096,128]{1,0:T(8,128)}, f32[4096,128]{1,0:T(8,128)}, bf16[4096,128]...) custom-call(s32[4]{0:T(128)S(1)} %bitcast.101, ...), custom_call_target="tpu_custom_call" | custom-call | flops 82500001792 | tf_op jit(solution)/shard_map/front/pallas_call | solution.py:1362
  142.7 1.1 copy-done.44
  143.8 1.0 copy-done.48
  144.8 1.0 copy-done.50
  146.0 2.2 collective-permute-start.4
  148.5 1.6 copy-done.43
  150.1 1.4 copy-done.45
  151.5 11.9 %project.1.q_ref.k_ref.v_ref = bf16[6,4096,128]{2,1,0:T(8,128)(2,1)S(1)} custom-call(bf16[4096,1024]{1,0:T(8,128)(2,1)} %bitcast.133, bf16[768,1024]{1,0:T(8,128)(2,1)S(1)} %copy-done.45, f32[4096,128]{1,0:T(8,128)S(1)} %copy-done.42, f32[4096,128]{1,0:T(8,128)S(1)} %copy-done.43), custom_call_target="tpu_custom_call" | custom-call | flops 12099999744 | tf_op jit(solution)/shard_map/project/pallas_call | solution.py:105
  163.5 2.6 copy-done.39
  166.1 45.9 %attend.2 = (bf16[4,1024,128]{2,1,0:T(8,128)(2,1)S(1)}, f32[4096,128]{1,0:T(8,128)S(1)}) custom-call(s32[2]{0:T(128)S(1)} %pad_add_fusion.own_ref, s32[8]{0:T(128)S(1)} %get-tuple-element.140.low_ref, s32[8]{0:T(128)S(1)} %get-tuple-element.139.high_ref, bf16[6,4096,128]{2,1,0:T(8,128)(2,1)} %copy-done.39, bf16[6,4096,128]{2,1,0:T(8,128)(2,1)} %copy-done.39, ...), custom_call_target="tpu_custom_call" | custom-call | flops 40699998208 | tf_op jit(solution)/shard_map/attend/pallas_call | solution.py:179
  212.1 3.2 collective-permute-start.3
  215.3 1.5 collective-permute-start.1
  217.5 2.9 collective-permute-start.10
  220.4 0.8 collective-permute-start.8
  221.2 45.9 %attend.3 = (bf16[4,1024,128]{2,1,0:T(8,128)(2,1)S(1)}, f32[4096,128]{1,0:T(8,128)S(1)}) custom-call(s32[2]{0:T(128)S(1)} %pad_add_fusion.own_ref, s32[8]{0:T(128)S(1)} %get-tuple-element.140.low_ref, s32[8]{0:T(128)S(1)} %get-tuple-element.139.high_ref, bf16[6,4096,128]{2,1,0:T(8,128)(2,1)} %copy-done.39, bf16[6,4096,128]{2,1,0:T(8,128)(2,1)} %copy-done.39, ...), custom_call_target="tpu_custom_call" | custom-call | flops 40699998208 | tf_op jit(solution)/shard_map/attend/pallas_call | solution.py:179
  267.1 1.3 copy-done.46
  268.5 1.4 collective-permute-start.7
  269.9 1.5 collective-permute-start.5
  271.6 0.6 fusion.31
  272.2 4.4 collective-permute-done.7.refs_7_.refs_8_
  276.6 6.2 collective-permute-done.5.refs_5_.refs_6_
  283.0 6.3 join.1
  289.4 1.3 copy-done.41
  290.7 114.6 %feed.1 = (f32[1024,1024]{1,0:T(8,128)}, bf16[1024,1024]{1,0:T(8,128)(2,1)}, f32[1024,1024]{1,0:T(8,128)}, bf16[1024,1024]{1,0:T(8,128)(2,1)}, bf16[16,288,1024]...) custom-call(bf16[1024,1024]{1,0:T(8,128)(2,1)} %copy-done.41, ...), custom_call_target="tpu_custom_call" | custom-call | flops 92400001024 | tf_op jit(solution)/shard_map/feed/pallas_call | solution.py:484
  405.9 3.9 collective-permute-done.11.gin_in_ref
  409.8 3.0 collective-permute-done.12.out_in_ref
  412.8 1.3 copy-done.69
  414.2 16.9 %turn.1 = (f32[1024,1024]{1,0:T(8,128)}, bf16[1024,1024]{1,0:T(8,128)(2,1)S(1)}, bf16[2,1024,1024]{2,1,0:T(8,128)(2,1)}, f32[8,1024]{1,0:T(8,128)S(1)}, bf16[102...) custom-call(s32[2]{0:T(128)S(1)} %pad_add_fusion.own_ref, ...), custom_call_target="tpu_custom_call" | custom-call | flops 16499999744 | tf_op jit(solution)/shard_map/turn/pallas_call | solution.py:631
  431.2 5.5 out_grad.1
  436.8 3.7 copy-done.3
  440.6 0.8 copy-done.37
  441.4 3.9 collective-permute-start.14
  445.5 0.6 convert_multiply_fusion
  446.1 1.9 collective-permute-start.20
  448.1 4.3 collective-permute-done.14
  452.7 0.9 collective-permute-start.13
  453.6 4.0 collective-permute-done.16
  457.6 1.1 pad_maximum_fusion.do_ref
  458.7 75.5 %attend_back.2.refs_4_ = bf16[4,3,1024,128]{3,2,1,0:T(8,128)(2,1)} custom-call(s32[2]{0:T(128)} %copy-done.38, s32[8]{0:T(128)} %copy-done.10, s32[8]{0:T(128)} %copy-done.9, bf16[6,4096,128]{2,1,0:T(8,128)(2,1)} %copy-done.39, bf16[6,4096,128]{2,1,0:T(8,128)(2,1)} %copy-done.39, bf16[6,4096,128]{2,1,0:T(8,128)(2,1)} %copy-done.39, ...), custom_call_target="tpu_custom_call" | custom-call | flops 72600002560 | tf_op jit(solution)/shard_map/attend_back/pallas_call | solution.py:308
  534.2 3.3 slice_bitcast_fusion.1
  537.5 2.6 collective-permute-start.19
  540.5 1.1 pad_maximum_fusion.1.do_ref
  541.6 3.1 slice_bitcast_fusion
  544.8 75.3 %attend_back.3.refs_5_ = bf16[4,3,1024,128]{3,2,1,0:T(8,128)(2,1)} custom-call(s32[2]{0:T(128)} %copy-done.38, s32[8]{0:T(128)} %copy-done.10, s32[8]{0:T(128)} %copy-done.9, bf16[6,4096,128]{2,1,0:T(8,128)(2,1)} %copy-done.39, bf16[6,4096,128]{2,1,0:T(8,128)(2,1)} %copy-done.39, bf16[6,4096,128]{2,1,0:T(8,128)(2,1)} %copy-done.39, ...), custom_call_target="tpu_custom_call" | custom-call | flops 72600002560 | tf_op jit(solution)/shard_map/attend_back/pallas_call | solution.py:308
  620.2 2.2 collective-permute-done.17.refs_1_
  622.4 78.6 %finish.1 = (bf16[1024,1024]{1,0:T(8,128)(2,1)}, bf16[768,1024]{1,0:T(8,128)(2,1)}, f32[8,1024]{1,0:T(8,128)}) custom-call(bf16[3,1024,128]{2,1,0:T(8,128)(2,1)} %get-tuple-element.113.refs_0_, bf16[3,1024,128]{2,1,0:T(8,128)(2,1)} %collective-permute-done.17.refs_1_, bf16[3,1024,128]{2,1,0:T(8,128)(2,1)} %collective-permute-done.18.refs_2_, ...), custom_call_target="tpu_custom_call" | custom-call | flops 65999998976 | tf_op jit(solution)/shard_map/finish/pallas_call | solution.py:1012
  701.0 3.1 copy.65
  704.1 0.6 select_maximum_fusion.sums_ref
  704.7 110.0 %sums.1 = (bf16[2048,1024]{1,0:T(8,128)(2,1)}, f32[8,20,1024]{2,1,0:T(8,128)}, bf16[1024,1024]{1,0:T(8,128)(2,1)}) custom-call(bf16[1024,1024]{1,0:T(8,128)(2,1)} %bitcast.129, bf16[1024,1024]{1,0:T(8,128)(2,1)} %get-tuple-element.95.inputs_in_hbm, bf16[1024,1024]{1,0:T(8,128)(2,1)} %bitcast.132, bf16[1024,1024]{1,0:T(8,128)(2,1)} %get-tuple-element.108.skips_in_hbm, ...), custom_call_target="tpu_custom_call" | custom-call | flops 109999996928 | tf_op jit(solution)/shard_map/sums/pallas_call | solution.py:1147
  814.7 1.5 copy.59
  817.0 5.0 fusion.3
  822.0 4.7 fusion.29
  826.8 4.4 convolution_bitcast_fusion
  831.2 4.4 convolution_bitcast_fusion.1
  835.6 1.1 slice.134
  836.7 1.1 bitcast_convert_fusion.2
  837.8 2.7 fusion.28
  840.5 2.6 bitcast_convert_fusion
  843.1 2.6 bitcast_convert_fusion.1
  845.7 5.5 copy.66
  (220 shorter events, 6.2 us)
Async XLA Ops:
  7.2 138.6 %all-gather.8.cloned.1.call-start = ((), (), s32[]{:S(2)}) async-start(), calls=%async_computation.4 | async-start | bytes 2621440 | tf_op jit(solution)/shard_map/all_gather | solution.py:1485
  7.2 7.1 collective-permute-start.9
  7.8 6.4 collective-permute-start
  10.8 279.9 %all-gather.10.cloned.1.call-start = ((), (), s32[]{:S(2)}) async-start(), calls=%async_computation.5 | async-start | bytes 10485760 | tf_op jit(solution)/shard_map/all_gather | solution.py:1486
  14.5 202.3 %copy-start.59 = (f32[4,128]{1,0:T(4,128)}, f32[4,128]{1,0:T(4,128)S(1)}, u32[]{:S(2)}) copy-start(f32[4,128]{1,0:T(4,128)S(1)} %get-tuple-element.131) | copy-start | bytes 6148
  14.5 202.3 %copy-start.61 = (f32[4,128]{1,0:T(4,128)}, f32[4,128]{1,0:T(4,128)S(1)}, u32[]{:S(2)}) copy-start(f32[4,128]{1,0:T(4,128)S(1)} %get-tuple-element.132) | copy-start | bytes 6148
  145.8 398.9 %reduce-scatter.7.cloned.1.call-start = ((), (), s32[]{:S(2)}) async-start(), calls=%async_computation.6 | async-start | bytes 11796480
  146.0 268.1 %copy-start.38 = (s32[2]{0:T(128)}, s32[2]{0:T(128)S(1)}, u32[]{:S(2)}) copy-start(s32[2]{0:T(128)S(1)} %pad_add_fusion.own_ref) | copy-start | bytes 28
  146.0 71.2 %collective-permute-start.4 = (bf16[1024,1024]{1,0:T(8,128)(2,1)}, bf16[1024,1024]{1,0:T(8,128)(2,1)}, u32[]{:S(2)}, u32[]{:S(2)}) collective-permute-start(bf16[1024,1024]{1,0:T(8,128)(2,1)} %bitcast.110), channel_id=1, source_target_pairs={{2,4},{3,5},{4,2},{5,3},{10,12},{11,13},{12,10},{13,11},{18,20},{1... | collective-permute-start | bytes 6291464 | tf_op jit(solution)/shard_map/ppermute | solution.py:1424
  148.5 72.7 %copy-start.9 = (s32[8]{0:T(128)}, s32[8]{0:T(128)S(1)}, u32[]{:S(2)}) copy-start(s32[8]{0:T(128)S(1)} %get-tuple-element.139.high_ref) | copy-start | bytes 100
  148.5 72.7 %copy-start.10 = (s32[8]{0:T(128)}, s32[8]{0:T(128)S(1)}, u32[]{:S(2)}) copy-start(s32[8]{0:T(128)S(1)} %get-tuple-element.140.low_ref) | copy-start | bytes 100
  151.5 14.6 %copy-start.49 = (bf16[4096,128]{1,0:T(8,128)(2,1)S(1)}, bf16[4096,128]{1,0:T(8,128)(2,1)}, u32[]{:S(2)}) copy-start(bf16[4096,128]{1,0:T(8,128)(2,1)} %copy-done.48) | copy-start | bytes 3145732
  151.5 14.6 %copy-start.51 = (bf16[4096,128]{1,0:T(8,128)(2,1)S(1)}, bf16[4096,128]{1,0:T(8,128)(2,1)}, u32[]{:S(2)}) copy-start(bf16[4096,128]{1,0:T(8,128)(2,1)} %copy-done.50) | copy-start | bytes 3145732
  212.1 56.4 %collective-permute-start.3 = (bf16[1024,128]{1,0:T(8,128)(2,1)S(1)}, bf16[1024,128]{1,0:T(8,128)(2,1)S(1)}, u32[]{:S(2)}, u32[]{:S(2)}) collective-permute-start(bf16[1024,128]{1,0:T(8,128)(2,1)S(1)} %get-tuple-element.118), channel_id=1, source_target_pairs={{0,5},{1,4},{2,7},{3,6},{4,1},{5,0},{6,3},{7,2},{8,13},{9,12},{10,... | collective-permute-start | bytes 786440 | tf_op jit(solution)/shard_map/ppermute | solution.py:1432
  215.3 54.6 %collective-permute-start.2 = (bf16[1024,128]{1,0:T(8,128)(2,1)S(1)}, bf16[1024,128]{1,0:T(8,128)(2,1)S(1)}, u32[]{:S(2)}, u32[]{:S(2)}) collective-permute-start(bf16[1024,128]{1,0:T(8,128)(2,1)S(1)} %get-tuple-element.119), channel_id=1, source_target_pairs={{0,4},{1,5},{2,6},{3,7},{4,0},{5,1},{6,2},{7,3},{8,12},{9,13},{10,... | collective-permute-start | bytes 786440 | tf_op jit(solution)/shard_map/ppermute | solution.py:1432
  215.3 54.6 %collective-permute-start.1 = (bf16[1024,128]{1,0:T(8,128)(2,1)S(1)}, bf16[1024,128]{1,0:T(8,128)(2,1)S(1)}, u32[]{:S(2)}, u32[]{:S(2)}) collective-permute-start(bf16[1024,128]{1,0:T(8,128)(2,1)S(1)} %get-tuple-element.120), channel_id=1, source_target_pairs={{0,1},{1,0},{2,3},{3,2},{4,5},{5,4},{6,7},{7,6},{8,9},{9,8},{10,11... | collective-permute-start | bytes 786440 | tf_op jit(solution)/shard_map/ppermute | solution.py:1432
  217.5 49.6 %copy-start.56 = (bf16[1024,1024]{1,0:T(8,128)(2,1)}, bf16[1024,1024]{1,0:T(8,128)(2,1)S(1)}, u32[]{:S(2)}) copy-start(bf16[1024,1024]{1,0:T(8,128)(2,1)S(1)} %broadcast_select_fusion.1.cot_own_ref.cot_ref) | copy-start | bytes 6291460
  217.5 73.3 %collective-permute-start.10 = (bf16[1024,1024]{1,0:T(8,128)(2,1)S(1)}, bf16[1024,1024]{1,0:T(8,128)(2,1)}, u32[]{:S(2)}, u32[]{:S(2)}) collective-permute-start(bf16[1024,1024]{1,0:T(8,128)(2,1)S(1)} %broadcast_select_fusion.1.cot_own_ref.cot_ref), channel_id=1, source_target_pairs={{0,4},{1,5},{2,6},{3,7},{4,0},{5,1},{6,2},{7,3},{8,12},{9,13},{10,... | collective-permute-start | bytes 6291464 | tf_op jit(solution)/shard_map/ppermute | solution.py:1432
  220.4 62.5 %collective-permute-start.8 = (bf16[1024,1024]{1,0:T(8,128)(2,1)S(1)}, bf16[1024,1024]{1,0:T(8,128)(2,1)S(1)}, u32[]{:S(2)}, u32[]{:S(2)}) collective-permute-start(bf16[1024,1024]{1,0:T(8,128)(2,1)S(1)} %copy-done.11), channel_id=1, source_target_pairs={{2,4},{3,5},{4,2},{5,3},{10,12},{11,13},{12,10},{13,11},{18,20},{1... | collective-permute-start | bytes 6291464 | tf_op jit(solution)/shard_map/ppermute | solution.py:1424
  268.4 20.9 %copy-start.4 = (bf16[4,1024,128]{2,1,0:T(8,128)(2,1)}, bf16[4,1024,128]{2,1,0:T(8,128)(2,1)S(1)}, u32[]{:S(2)}) copy-start(bf16[4,1024,128]{2,1,0:T(8,128)(2,1)S(1)} %get-tuple-element.66.ctx_ref) | copy-start | bytes 3145732
  268.4 14.6 %copy-start.40 = (bf16[8,4,32,1024]{3,2,1,0:T(8,128)(2,1)S(1)}, bf16[8,4,32,1024]{3,2,1,0:T(8,128)(2,1)}, u32[]{:S(2)}) copy-start(bf16[8,4,32,1024]{3,2,1,0:T(8,128)(2,1)} %get-tuple-element.67.refs_8_.w_out_ref) | copy-start | bytes 6291460
  268.5 20.8 %copy-start.14 = (bf16[1024,128]{1,0:T(8,128)(2,1)}, bf16[1024,128]{1,0:T(8,128)(2,1)S(1)}, u32[]{:S(2)}) copy-start(bf16[1024,128]{1,0:T(8,128)(2,1)S(1)} %collective-permute-done.3.refs_3_.refs_4_) | copy-start | bytes 786436
  268.5 8.0 collective-permute-start.7
  269.9 19.5 %copy-start.16 = (bf16[1024,128]{1,0:T(8,128)(2,1)}, bf16[1024,128]{1,0:T(8,128)(2,1)S(1)}, u32[]{:S(2)}) copy-start(bf16[1024,128]{1,0:T(8,128)(2,1)S(1)} %collective-permute-done.2.refs_2_.refs_3_) | copy-start | bytes 786436
  269.9 6.7 collective-permute-start.6
  269.9 19.4 %copy-start.18 = (bf16[1024,128]{1,0:T(8,128)(2,1)}, bf16[1024,128]{1,0:T(8,128)(2,1)S(1)}, u32[]{:S(2)}) copy-start(bf16[1024,128]{1,0:T(8,128)(2,1)S(1)} %collective-permute-done.1.refs_1_.refs_2_) | copy-start | bytes 786436
  269.9 12.9 %collective-permute-start.5 = (bf16[1024,128]{1,0:T(8,128)(2,1)S(1)}, bf16[1024,128]{1,0:T(8,128)(2,1)S(1)}, u32[]{:S(2)}, u32[]{:S(2)}) collective-permute-start(bf16[1024,128]{1,0:T(8,128)(2,1)S(1)} %get-tuple-element.116), channel_id=1, source_target_pairs={{0,1},{1,0},{2,3},{3,2},{4,5},{5,4},{6,7},{7,6},{8,9},{9,8},{10,11... | collective-permute-start | bytes 786440 | tf_op jit(solution)/shard_map/ppermute | solution.py:1432
  276.6 12.8 %copy-start.22 = (bf16[1024,128]{1,0:T(8,128)(2,1)}, bf16[1024,128]{1,0:T(8,128)(2,1)S(1)}, u32[]{:S(2)}) copy-start(bf16[1024,128]{1,0:T(8,128)(2,1)S(1)} %collective-permute-done.7.refs_7_.refs_8_) | copy-start | bytes 786436
  276.6 12.8 %copy-start.26 = (bf16[1024,128]{1,0:T(8,128)(2,1)}, bf16[1024,128]{1,0:T(8,128)(2,1)S(1)}, u32[]{:S(2)}) copy-start(bf16[1024,128]{1,0:T(8,128)(2,1)S(1)} %collective-permute-done.6.refs_6_.refs_7_) | copy-start | bytes 786436
  282.8 6.6 copy-start.30
  282.8 6.6 copy-start.12
  283.0 131.1 %copy-start.6 = (s32[1024,128]{1,0:T(8,128)}, s32[1024,128]{1,0:T(8,128)S(1)}, u32[]{:S(2)}) copy-start(s32[1024,128]{1,0:T(8,128)S(1)} %broadcast_in_dim.48.refs_11_.segment_ref) | copy-start | bytes 1572868
  405.3 4.4 collective-permute-start.11
  405.4 7.4 collective-permute-start.12
  414.1 17.0 %copy-start.2 = (bf16[16,288,1024]{2,1,0:T(8,128)(2,1)S(1)}, bf16[16,288,1024]{2,1,0:T(8,128)(2,1)}, u32[]{:S(2)}) copy-start(bf16[16,288,1024]{2,1,0:T(8,128)(2,1)} %get-tuple-element.87.refs_9_) | copy-start | bytes 28311556
  414.1 17.0 %copy-start.15 = (bf16[1024,128]{1,0:T(8,128)(2,1)S(1)}, bf16[1024,128]{1,0:T(8,128)(2,1)}, u32[]{:S(2)}) copy-start(bf16[1024,128]{1,0:T(8,128)(2,1)} %copy-done.14) | copy-start | bytes 786436
  414.1 17.0 %copy-start.17 = (bf16[1024,128]{1,0:T(8,128)(2,1)S(1)}, bf16[1024,128]{1,0:T(8,128)(2,1)}, u32[]{:S(2)}) copy-start(bf16[1024,128]{1,0:T(8,128)(2,1)} %copy-done.16) | copy-start | bytes 786436
  414.1 17.0 %copy-start.19 = (bf16[1024,128]{1,0:T(8,128)(2,1)S(1)}, bf16[1024,128]{1,0:T(8,128)(2,1)}, u32[]{:S(2)}) copy-start(bf16[1024,128]{1,0:T(8,128)(2,1)} %copy-done.18) | copy-start | bytes 786436
  414.1 17.0 %copy-start.23 = (bf16[1024,128]{1,0:T(8,128)(2,1)S(1)}, bf16[1024,128]{1,0:T(8,128)(2,1)}, u32[]{:S(2)}) copy-start(bf16[1024,128]{1,0:T(8,128)(2,1)} %copy-done.22) | copy-start | bytes 786436
  414.1 17.0 %copy-start.27 = (bf16[1024,128]{1,0:T(8,128)(2,1)S(1)}, bf16[1024,128]{1,0:T(8,128)(2,1)}, u32[]{:S(2)}) copy-start(bf16[1024,128]{1,0:T(8,128)(2,1)} %copy-done.26) | copy-start | bytes 786436
  414.1 17.0 %copy-start.31 = (bf16[1024,128]{1,0:T(8,128)(2,1)S(1)}, bf16[1024,128]{1,0:T(8,128)(2,1)}, u32[]{:S(2)}) copy-start(bf16[1024,128]{1,0:T(8,128)(2,1)} %copy-done.30) | copy-start | bytes 786436
  431.0 5.6 copy-start.7
  431.0 5.6 copy-start.20
  431.1 5.6 copy-start.24
  431.1 5.6 copy-start.28
  431.1 5.6 copy-start.32
  431.1 5.6 copy-start.34
  431.1 5.6 copy-start.36
  440.5 7.6 copy-start.25
  440.5 11.9 %copy-start.21 = (bf16[1024,128]{1,0:T(8,128)(2,1)S(1)}, bf16[1024,128]{1,0:T(8,128)(2,1)}, u32[]{:S(2)}) copy-start(bf16[1024,128]{1,0:T(8,128)(2,1)} %copy-done.20) | copy-start | bytes 786436
  440.5 17.1 %copy-start.8 = (bf16[1024,128]{1,0:T(8,128)(2,1)S(1)}, bf16[1024,128]{1,0:T(8,128)(2,1)}, u32[]{:S(2)}) copy-start(bf16[1024,128]{1,0:T(8,128)(2,1)} %copy-done.7) | copy-start | bytes 786436
  440.5 264.2 %reduce-scatter.5.cloned.1.call-start = ((), (), s32[]{:S(2)}) async-start(), calls=%async_computation.2 | async-start | bytes 2949120 | tf_op jit(solution)/shard_map/reduce_scatter | solution.py:1535
  441.4 11.0 %collective-permute-start.14 = (bf16[1024,128]{1,0:T(8,128)(2,1)S(1)}, bf16[1024,128]{1,0:T(8,128)(2,1)S(1)}, u32[]{:S(2)}, u32[]{:S(2)}) collective-permute-start(bf16[1024,128]{1,0:T(8,128)(2,1)S(1)} %copy-done.37), channel_id=1, source_target_pairs={{0,1},{1,0},{2,3},{3,2},{4,5},{5,4},{6,7},{7,6},{8,9},{9,8},{10,11... | collective-permute-start | bytes 786440 | tf_op jit(solution)/shard_map/ppermute | solution.py:1432
  445.3 7.4 collective-permute-start.15
  445.3 12.3 %collective-permute-start.16 = (bf16[1024,128]{1,0:T(8,128)(2,1)S(1)}, bf16[1024,128]{1,0:T(8,128)(2,1)S(1)}, u32[]{:S(2)}, u32[]{:S(2)}) collective-permute-start(bf16[1024,128]{1,0:T(8,128)(2,1)S(1)} %copy-done.33), channel_id=1, source_target_pairs={{0,5},{1,4},{2,7},{3,6},{4,1},{5,0},{6,3},{7,2},{8,13},{9,12},{10,... | collective-permute-start | bytes 786440 | tf_op jit(solution)/shard_map/ppermute | solution.py:1432
  446.1 93.9 %collective-permute-start.20 = (bf16[1024,128]{1,0:T(8,128)(2,1)S(1)}, bf16[1024,128]{1,0:T(8,128)(2,1)S(1)}, u32[]{:S(2)}, u32[]{:S(2)}) collective-permute-start(bf16[1024,128]{1,0:T(8,128)(2,1)S(1)} %copy-done.29), channel_id=1, source_target_pairs={{0,1},{1,0},{2,3},{3,2},{4,5},{5,4},{6,7},{7,6},{8,9},{9,8},{10,11... | collective-permute-start | bytes 786440 | tf_op jit(solution)/shard_map/ppermute | solution.py:1432
  448.1 92.0 %collective-permute-start.21 = (bf16[1024,128]{1,0:T(8,128)(2,1)S(1)}, bf16[1024,128]{1,0:T(8,128)(2,1)S(1)}, u32[]{:S(2)}, u32[]{:S(2)}) collective-permute-start(bf16[1024,128]{1,0:T(8,128)(2,1)S(1)} %copy-done.25), channel_id=1, source_target_pairs={{0,4},{1,5},{2,6},{3,7},{4,0},{5,1},{6,2},{7,3},{8,12},{9,13},{10,... | collective-permute-start | bytes 786440 | tf_op jit(solution)/shard_map/ppermute | solution.py:1432
  452.4 88.1 %collective-permute-start.22 = (bf16[1024,128]{1,0:T(8,128)(2,1)S(1)}, bf16[1024,128]{1,0:T(8,128)(2,1)S(1)}, u32[]{:S(2)}, u32[]{:S(2)}) collective-permute-start(bf16[1024,128]{1,0:T(8,128)(2,1)S(1)} %copy-done.21), channel_id=1, source_target_pairs={{0,5},{1,4},{2,7},{3,6},{4,1},{5,0},{6,3},{7,2},{8,13},{9,12},{10,... | collective-permute-start | bytes 786440 | tf_op jit(solution)/shard_map/ppermute | solution.py:1432
  452.7 89.0 %collective-permute-start.13 = (bf16[2,1024,1024]{2,1,0:T(8,128)(2,1)}, bf16[2,1024,1024]{2,1,0:T(8,128)(2,1)S(1)}, u32[]{:S(2)}, u32[]{:S(2)}) collective-permute-start(bf16[2,1024,1024]{2,1,0:T(8,128)(2,1)} %get-tuple-element.76), channel_id=1, source_target_pairs={{2,4},{3,5},{4,2},{5,3},{10,12},{11,13},{12,10},{13,11},{18,20},{1... | collective-permute-start | bytes 12582920 | tf_op jit(solution)/shard_map/ppermute | solution.py:1424
  534.2 7.5 copy-start.57
  537.5 82.7 %collective-permute-start.19 = (bf16[3,1024,128]{2,1,0:T(8,128)(2,1)}, bf16[3,1024,128]{2,1,0:T(8,128)(2,1)}, u32[]{:S(2)}, u32[]{:S(2)}) collective-permute-start(bf16[3,1024,128]{2,1,0:T(8,128)(2,1)} %get-tuple-element.110), channel_id=1, source_target_pairs={{0,5},{1,4},{2,7},{3,6},{4,1},{5,0},{6,3},{7,2},{8,13},{9,12},{10,... | collective-permute-start | bytes 2359304 | tf_op jit(solution)/shard_map/ppermute | solution.py:1432
  540.0 80.1 %collective-permute-start.18 = (bf16[3,1024,128]{2,1,0:T(8,128)(2,1)S(1)}, bf16[3,1024,128]{2,1,0:T(8,128)(2,1)}, u32[]{:S(2)}, u32[]{:S(2)}) collective-permute-start(bf16[3,1024,128]{2,1,0:T(8,128)(2,1)S(1)} %get-tuple-element.111), channel_id=1, source_target_pairs={{0,4},{1,5},{2,6},{3,7},{4,0},{5,1},{6,2},{7,3},{8,12},{9,13},{10,... | collective-permute-start | bytes 2359304 | tf_op jit(solution)/shard_map/ppermute | solution.py:1432
  540.1 82.3 %collective-permute-start.17 = (bf16[3,1024,128]{2,1,0:T(8,128)(2,1)S(1)}, bf16[3,1024,128]{2,1,0:T(8,128)(2,1)}, u32[]{:S(2)}, u32[]{:S(2)}) collective-permute-start(bf16[3,1024,128]{2,1,0:T(8,128)(2,1)S(1)} %get-tuple-element.112), channel_id=1, source_target_pairs={{0,1},{1,0},{2,3},{3,2},{4,5},{5,4},{6,7},{7,6},{8,9},{9,8},{10,11... | collective-permute-start | bytes 2359304 | tf_op jit(solution)/shard_map/ppermute | solution.py:1432
  544.8 290.8 %all-gather.6.cloned.1.call-start = ((), (), s32[]{:S(2)}) async-start(), calls=%async_computation.3 | async-start | bytes 5308416 | tf_op jit(solution)/shard_map/all_gather | solution.py:1537
  (36 other events, 123.6 us)
Sparse Core Ops, SparseCore 0:
  11.0 76.4 all-gather.7
  146.0 87.4 all-gather.9
  440.7 96.3 reduce-scatter.6
  544.9 72.1 reduce-scatter.4
  704.9 50.1 all-gather.5

commit v3 on v2

--- a/solution.py
+++ b/solution.py
@@ -157,15 +157,17 @@
         for head in range(2):
             peak, total = carry[head]
             scores = lax.dot_general(queries[head], block, NT, preferred_element_type=F32)
-            higher = jnp.maximum(peak, jnp.max(scores, axis=1, keepdims=True))
-            weights = jnp.exp2(scores - higher).astype(BF)
+            cuts = [scores[:, k * LANES : (k + 1) * LANES] for k in range(bk // LANES)]
+            tallest = functools.reduce(jnp.maximum, cuts)
+            higher = jnp.maximum(peak, jnp.max(tallest, axis=1, keepdims=True))
+            weights = jnp.concatenate([jnp.exp2(cut - higher).astype(BF) for cut in cuts], axis=1)
             total = total * jnp.exp2(peak - higher) + jnp.dot(
                 weights, vals[head, rows, :], preferred_element_type=F32
             )
             new.append((higher, total))
         return tuple(new)
 
-    init = (jnp.full((bq, 1), -3e38, F32), jnp.zeros((bq, LANES), F32))
+    init = (jnp.full((bq, LANES), -3e38, F32), jnp.zeros((bq, LANES), F32))
     (peak_a, sum_a), (peak_b, sum_b) = lax.fori_loop(low_ref[step], high_ref[step], body, (init, init))
     weight_sum = pltpu.roll(jnp.where(first, sum_b, sum_a), 64, 1)
     ctx_ref[0] = (jnp.where(first, sum_a, sum_b) / weight_sum).astype(BF)
@@ -201,7 +203,7 @@
         compiler_params=pltpu.CompilerParams(
             dimension_semantics=("arbitrary",), vmem_limit_bytes=48 * MIB
         ),
-        cost_estimate=cost(37),
+        cost_estimate=cost(35),
         name="attend",
     )(own, low, high, qkv, qkv, qkv, qmark, kmark)
 
@@ -348,19 +350,14 @@
 
 
 def feed_kernel(
-    x_own_ref, cot_own_ref, cot_other_ref, weights_ref, inputs_hbm, heads_hbm,
-    out_own_ref, out_other_ref, gin_own_ref, gin_other_ref, grads_ref, inputs_in_hbm, heads_out_hbm,
+    x_own_ref, cot_own_ref, cot_other_ref, weights_ref, heads_hbm,
+    out_own_ref, out_other_ref, gin_own_ref, gin_other_ref, grads_ref, heads_out_hbm,
     x_other_ref, out_sum, gin_sum, local, sems, *, parts,
 ):
     step = pl.program_id(0)
     last = pl.num_programs(0) - 1
     d, z, core, half = mesh_spot(parts)
-    leaves = z // half != core
-    there = ((d - core) + z // half, core * half + z % half)
     beside = partner_of(d, z, half, half)
-
-    def copies():
-        return in_pieces(inputs_hbm, inputs_in_hbm, sems, 1, there)
 
     eighth = d // 2 % 4 + 4 * core
 
@@ -374,33 +371,13 @@
 
     @pl.when(step == 0)
     def _():
-        barrier = pltpu.get_barrier_semaphore()
-        near = [(d ^ bit, z) for bit in (1, 2, 4)] + [(d, z ^ k) for k in range(1, parts)]
-        for device in near:
-            pl.semaphore_signal(barrier, inc=1, device_id=device, device_id_type=pl.DeviceIdType.MESH)
-
-        @pl.when(leaves)
-        def _():
-            pl.semaphore_signal(barrier, inc=1, device_id=there, device_id_type=pl.DeviceIdType.MESH)
-            pl.semaphore_wait(barrier, len(near) + 1)
-
-        @pl.when(jnp.logical_not(leaves))
-        def _():
-            pl.semaphore_wait(barrier, len(near))
-
+        greet([(d ^ bit, z) for bit in (1, 2, 4)] + [(d, z ^ k) for k in range(1, parts)])
         remote_copy(x_own_ref, x_other_ref, sems, 0, beside).start()
         copy = pltpu.make_async_copy(heads_hbm.at[:, eighth], heads_out_hbm.at[eighth, z], local)
         copy.start()
         copy.wait()
         for k in range(1, parts):
             heads_part(k).start()
-
-    @pl.when(step == 1)
-    def _():
-        @pl.when(leaves)
-        def _():
-            for copy in copies():
-                copy.start()
 
     @pl.when(step == 2)
     def _():
@@ -466,13 +443,8 @@
 
         heads_part(parts + 1).wait()
 
-        @pl.when(leaves)
-        def _():
-            for copy in copies():
-                copy.wait()
-
-
-def feed(x_own, cot_own, cot_other, weights, inputs, heads, spare, parts):
+
+def feed(x_own, cot_own, cot_other, weights, heads, spare, parts):
     frames, depth = x_own.shape
     groups, _, per, _ = weights.shape
     chunk = 256
@@ -484,15 +456,14 @@
     return pl.pallas_call(
         functools.partial(feed_kernel, parts=parts),
         grid=(groups * per // chunk,),
-        in_specs=[whole] * 3 + [cut] + [anywhere] * 2,
-        out_specs=[whole] * 4 + [grads] + [anywhere] * 2,
+        in_specs=[whole] * 3 + [cut, anywhere],
+        out_specs=[whole] * 4 + [grads, anywhere],
         out_shape=[
             shape((frames, depth), F32),
             shape((frames, depth), BF),
             shape((frames, depth), F32),
             shape((frames, depth), BF),
             shape((groups, 2 * per + spare, depth), BF),
-            shape((frames, depth), BF),
             shape((8, parts) + heads.shape[:1] + heads.shape[2:], BF),
         ],
         scratch_shapes=[
@@ -507,7 +478,7 @@
         ),
         cost_estimate=cost(84),
         name="feed",
-    )(x_own, cot_own, cot_other, weights, inputs, heads)
+    )(x_own, cot_own, cot_other, weights, heads)
 
 
 def spread(segment, table):
@@ -553,41 +524,96 @@
     ) * inverse
 
 
-def join_kernel(own_ref, *refs, pairs, parts):
-    ctx_refs = refs[: pairs * parts]
-    w_out_ref, base_ref, base_in_ref, segment_ref, shift_ref, scale_ref, hidden_ref, normed_ref = refs[pairs * parts :]
-    own = own_ref[0]
-    hidden = jnp.where(own_ref[1] == 1, base_ref[...], base_in_ref[...]).astype(F32)
+def join_kernel(*refs, pairs, parts):
+    ctx_refs, refs = refs[: (pairs - 1) * parts], refs[(pairs - 1) * parts :]
+    (
+        last_hbm, w_out_ref, base_ref, base_in_ref, segment_ref, shift_ref, scale_ref,
+        hidden_ref, normed_ref, last_out_hbm, last, local, sems,
+    ) = refs
+    step = pl.program_id(0)
+    steps = pl.num_programs(0)
+    d, z, core, half = mesh_spot(parts)
+    part = core * half + z % half
+    stays = z // half == core
+    rows = hidden_ref.shape[0]
+
+    def chunk(b, k):
+        here = pl.ds(pl.multiple_of(k * rows, rows), rows)
+        return remote_copy(
+            last_hbm.at[b, here, :], last.at[b, here, :], sems, k * parts + b, partner_of(d, z, b, half)
+        )
+
+    own = pltpu.make_async_copy(last_hbm.at[0], last.at[0], local)
+
+    @pl.when(step == 0)
+    def _():
+        own.start()
+        greet([partner_of(d, z, b, half) for b in range(1, parts)])
+
+        @pl.loop(0, steps)
+        def _(k):
+            for b in range(1, parts):
+                chunk(b, k).start()
+
+    hidden = jnp.where(stays, base_ref[...], base_in_ref[...]).astype(F32)
     for b in range(parts):
-        context = jnp.concatenate([ctx_refs[pair * parts + b][...] for pair in range(pairs)], axis=1)
-        hidden = hidden + jnp.dot(context, w_out_ref[:, own ^ b].reshape(pairs * LANES, -1), preferred_element_type=F32)
+        for pair in range(pairs - 1):
+            weights = w_out_ref[:, part ^ b].reshape(pairs * LANES, -1)[pair * LANES : (pair + 1) * LANES]
+            hidden = hidden + jnp.dot(ctx_refs[pair * parts + b][...], weights, preferred_element_type=F32)
+
+    @pl.when(step == 0)
+    def _():
+        own.wait()
+
+    for b in range(1, parts):
+        chunk(b, step).wait()
+    here = pl.ds(pl.multiple_of(step * rows, rows), rows)
+    for b in range(parts):
+        weights = w_out_ref[:, part ^ b].reshape(pairs * LANES, -1)[(pairs - 1) * LANES :]
+        hidden = hidden + jnp.dot(last[b, here, :], weights, preferred_element_type=F32)
     hidden_ref[...] = hidden
     unit, _ = unit_norm(hidden)
     segment = segment_ref[...]
     normed_ref[...] = (unit * (1.0 + spread(segment, scale_ref[...])) + spread(segment, shift_ref[...])).astype(BF)
 
-
-def join(own, ctx_blocks, w_out, base, base_in, segment, shift, scale, pairs, parts):
+    @pl.when(step == steps - 1)
+    def _():
+        copy = pltpu.make_async_copy(last, last_out_hbm, local)
+        copy.start()
+        copy.wait()
+
+
+def join(ctx_blocks, last, w_out, base, base_in, segment, shift, scale, pairs, parts):
     frames, depth = base.shape
     rows = 256
-    row = lambda i, *_: (i, 0)
+    row = lambda i: (i, 0)
     wide = pl.BlockSpec((rows, depth), row)
-    table = pl.BlockSpec(shift.shape, lambda i, *_: (0, 0))
+    thin = pl.BlockSpec((rows, LANES), row)
+    table = pl.BlockSpec(shift.shape, lambda i: (0, 0))
+    anywhere = pl.BlockSpec(memory_space=pl.ANY)
     return pl.pallas_call(
         functools.partial(join_kernel, pairs=pairs, parts=parts),
-        grid_spec=pltpu.PrefetchScalarGridSpec(
-            num_scalar_prefetch=1,
-            grid=(frames // rows,),
-            in_specs=[pl.BlockSpec((rows, LANES), row)] * (pairs * parts)
-            + [pl.BlockSpec(w_out.shape, lambda i, *_: (0, 0, 0, 0)), wide, wide, pl.BlockSpec((rows, LANES), row)]
-            + [table] * 2,
-            out_specs=[wide, wide],
+        grid=(frames // rows,),
+        in_specs=[thin] * len(ctx_blocks)
+        + [anywhere, pl.BlockSpec(w_out.shape, lambda i: (0, 0, 0, 0)), wide, wide, thin]
+        + [table] * 2,
+        out_specs=[wide, wide, anywhere],
+        out_shape=[
+            jax.ShapeDtypeStruct((frames, depth), F32),
+            jax.ShapeDtypeStruct((frames, depth), BF),
+            jax.ShapeDtypeStruct(last.shape, BF),
+        ],
+        scratch_shapes=[
+            pltpu.VMEM(last.shape, BF),
+            pltpu.SemaphoreType.DMA,
+            pltpu.SemaphoreType.DMA((2 * parts * (frames // rows),)),
+        ],
+        compiler_params=pltpu.CompilerParams(
+            dimension_semantics=("arbitrary",), vmem_limit_bytes=40 * MIB, collective_id=5, has_side_effects=True
         ),
-        out_shape=[jax.ShapeDtypeStruct((frames, depth), F32), jax.ShapeDtypeStruct((frames, depth), BF)],
-        compiler_params=pltpu.CompilerParams(vmem_limit_bytes=40 * MIB),
-        cost_estimate=cost(8),
+        cost_estimate=cost(18),
         name="join",
-    )(own, *ctx_blocks, w_out, base, base_in, segment, shift, scale)
+    )(*ctx_blocks, last, w_out, base, base_in, segment, shift, scale)
 
 
 def turn_kernel(
@@ -655,7 +681,7 @@
 
 
 def out_grad_kernel(*refs, pairs, parts, columns, at_row):
-    low_ref, ctx_refs, (_, out_hbm, held, landing, local, sems) = refs[0], refs[1:-6], refs[-6:]
+    low_ref, ctx_refs, (last_ref, _, out_hbm, held, landing, local, sems) = refs[0], refs[1:-7], refs[-7:]
     d, z, core, half = mesh_spot(parts)
     part = core * half + z % half
     beside = partner_of(d, z, half, half)
@@ -666,7 +692,8 @@
     low = low_ref[...]
     for b in range(parts):
         for pair in range(pairs):
-            grad = lax.dot_general(ctx_refs[pair * parts + b][...], low, TN, preferred_element_type=F32)
+            ctx = last_ref[b] if pair == pairs - 1 else ctx_refs[pair * parts + b][...]
+            grad = lax.dot_general(ctx, low, TN, preferred_element_type=F32)
             for k in range(LANES // per):
                 spot = pair * (LANES // per) + k
                 held[spot % 2, spot // 2, part ^ b, :per, :] = grad[k * per : (k + 1) * per].astype(BF)
@@ -687,14 +714,14 @@
         copy.wait()
 
 
-def out_grad(low, ctx_blocks, grad_feed, at_row, pairs, parts, columns):
+def out_grad(low, ctx_blocks, last, grad_feed, at_row, pairs, parts, columns):
     depth = low.shape[1]
     spare = grad_feed.shape[1] - at_row
     vmem = pl.BlockSpec(memory_space=pltpu.VMEM)
     anywhere = pl.BlockSpec(memory_space=pl.ANY)
     return pl.pallas_call(
         functools.partial(out_grad_kernel, pairs=pairs, parts=parts, columns=columns, at_row=at_row),
-        in_specs=[vmem] * (1 + pairs * parts) + [anywhere],
+        in_specs=[vmem] * (2 + len(ctx_blocks)) + [anywhere],
         out_specs=anywhere,
         out_shape=jax.ShapeDtypeStruct(grad_feed.shape, BF),
         scratch_shapes=[
@@ -703,13 +730,13 @@
             pltpu.SemaphoreType.DMA((columns,)),
             pltpu.SemaphoreType.DMA((2,)),
         ],
-        input_output_aliases={1 + pairs * parts: 0},
+        input_output_aliases={2 + len(ctx_blocks): 0},
         compiler_params=pltpu.CompilerParams(
             collective_id=4, has_side_effects=True, vmem_limit_bytes=32 * MIB
         ),
         cost_estimate=cost(9),
         name="out_grad",
-    )(low, *ctx_blocks, grad_feed)
+    )(low, *ctx_blocks, last, grad_feed)
 
 
 class Sender:
@@ -823,8 +850,8 @@
     prev_hbm, refs = refs[:cut], refs[cut:]
     own_hbm, refs = refs[:pairs], refs[pairs:]
     (
-        normed_hbm, weight_hbm, base_hbm, base_in_hbm, grad_hbm, segment_ref, scale_ref,
-        grad_base_ref, qkv_ref, sums_ref,
+        normed_hbm, weight_hbm, base_hbm, base_in_hbm, grad_hbm, inputs_hbm, segment_ref, scale_ref,
+        grad_base_ref, qkv_ref, sums_ref, inputs_in_hbm,
         prev, own, normed, weight, base, grad_hidden, arrived, total, qkv_held, qkv_in, loads, sems,
     ) = refs
     d, z, core, half = mesh_spot(parts)
@@ -855,6 +882,11 @@
         sends.append(
             (b, remote(own_hbm[-1].at[b], arrived.at[b - 1], sems, b - 1, partner_of(d, z, b, half)))
         )
+
+    @pl.when(jnp.logical_not(stays))
+    def _():
+        for copy in in_pieces(inputs_hbm, inputs_in_hbm, sems, parts, there):
+            copy.start()
 
     def load(at, source, target):
         copy = pltpu.make_async_copy(source, target, loads.at[at])
@@ -897,7 +929,7 @@
                 at_row = k * 3 * width + kind * width + pair * LANES
                 qkv_held[at_row : at_row + LANES, :] = grad[:, k * wide : (k + 1) * wide]
 
-    sender = Sender(sems, parts)
+    sender = Sender(sems, parts + PIECES)
     down = [
         [("dp", bit) for bit in dp_bits] + [("tensor", half)],
         [("dp", bit) for bit in reversed(dp_bits)] + [("tensor", half)],
@@ -993,9 +1025,14 @@
     while running:
         run_all(running)
 
+    @pl.when(jnp.logical_not(stays))
+    def _():
+        for copy in in_pieces(inputs_hbm, inputs_in_hbm, sems, parts, there):
+            copy.wait()
+
 
 def finish(
-    prev, own, normed_all, weight, base, base_in, grad_hidden, segment, scale, pairs, parts, rows_all
+    prev, own, normed_all, weight, base, base_in, grad_hidden, inputs, segment, scale, pairs, parts, rows_all
 ):
     frames, depth = base.shape
     utt = scale.shape[0]
@@ -1004,19 +1041,20 @@
     while units * depth // wide % (16 * rows_all * 2):
         wide //= 2
     qkv_shape = (units * depth // wide, wide)
-    copies = parts + 2 + 5 * rows_all.bit_length() + parts.bit_length()
+    copies = parts + 2 + PIECES + 5 * rows_all.bit_length() + parts.bit_length()
     anywhere = pl.BlockSpec(memory_space=pl.ANY)
     vmem = pl.BlockSpec(memory_space=pltpu.VMEM)
     shape = lambda *s: jax.ShapeDtypeStruct(*s)
     block = (3, frames, LANES)
     return pl.pallas_call(
         functools.partial(finish_kernel, pairs=pairs, parts=parts, utt=utt, rows_all=rows_all),
-        in_specs=[anywhere] * (len(prev) + pairs + 5) + [vmem] * 2,
-        out_specs=[vmem] * 3,
+        in_specs=[anywhere] * (len(prev) + pairs + 6) + [vmem] * 2,
+        out_specs=[vmem] * 3 + [anywhere],
         out_shape=[
             shape((frames, depth), BF),
             shape(qkv_shape, BF),
             shape((2 * utt, depth), F32),
+            shape((frames, depth), BF),
         ],
         scratch_shapes=[
             pltpu.VMEM((max(len(prev), 1),) + block, BF),
@@ -1037,7 +1075,7 @@
         ),
         cost_estimate=cost(60),
         name="finish",
-    )(*prev, *own, normed_all, weight, base, base_in, grad_hidden, segment, scale)
+    )(*prev, *own, normed_all, weight, base, base_in, grad_hidden, inputs, segment, scale)
 
 
 def sums_kernel(
@@ -1504,24 +1542,28 @@
         return block_ranges(lengths_work, natural, size, other)
 
     own = jnp.stack([part.astype(jnp.int32), stays.astype(jnp.int32)])
+    wide = min(frames, 1024)
+    low, high = ranges(wide, wide)
     bq, bk = 512, 512
-    low, high = ranges(bq, bk)
     low_back, high_back = ranges(bk, bq)
     ctx_pairs, lse_pairs, ctx_mine = [], [], []
     for pair in range(pairs):
-        ctx, lse = attend(after(qkv, cot) if pair == pairs - 1 else qkv, pair, qmark, kmark, own, low, high, bq, bk, frames)
+        ctx, lse = attend(
+            after(qkv, cot) if pair == pairs - 1 else qkv, pair, qmark, kmark, own, low, high, wide, wide, frames
+        )
         ctx_pairs.append(ctx)
         lse_pairs.append(lse)
-        ctx_mine += exchange([ctx[b] for b in range(parts)])
-    hidden, ffn_in = join(
-        own, ctx_mine, w_out_all, base_home, base_in, segment_here, shift_two, scale_two, pairs, parts
+        if pair < pairs - 1:
+            ctx_mine += exchange([ctx[b] for b in range(parts)])
+    hidden, ffn_in, ctx_last = join(
+        ctx_mine, ctx_pairs[-1], w_out_all, base_home, base_in, segment_here, shift_two, scale_two, pairs, parts
     )
 
     cot_other = partner(cot, half)
     spare = max(per_o, 16)
     heads = qkv_rows.reshape(3 * pairs, 8, LANES // 8, depth)
-    out_own, out_send, gin_own, gin_send, grad_feed, inputs_in, w_heads = feed(
-        ffn_in, cot, cot_other, feed_rows, inputs, heads, spare, parts
+    out_own, out_send, gin_own, gin_send, grad_feed, w_heads = feed(
+        ffn_in, cot, cot_other, feed_rows, heads, spare, parts
     )
     grad_hidden, low_grad, block_out, sums_two, *grad_context = turn(
         own, gin_own, partner(gin_send, half), out_own, partner(out_send, half), hidden, cot, skip_input, segment_here,
@@ -1529,7 +1571,7 @@
         w_out_all, pairs, parts,
     )
 
-    grad_feed = out_grad(low_grad, ctx_mine, grad_feed, 2 * per_u, pairs, parts, columns)
+    grad_feed = out_grad(low_grad, ctx_mine, ctx_last, grad_feed, 2 * per_u, pairs, parts, columns)
     grad_feed = grad_feed.reshape(columns, parts, 2 * per_u + spare, depth)
     feed_sum = lax.psum_scatter(grad_feed, "dp", scatter_dimension=0, axis_index_groups=same_core)
     grad_feed = lax.psum_scatter(feed_sum, "tensor", scatter_dimension=0)
@@ -1554,8 +1596,8 @@
     for grads in grad_mine[:-1]:
         returned += exchange([grads[b] for b in range(parts)])
     block_out_in, skips_in = moved(block_out)
-    grad_base, grad_qkv, sums_one = finish(
-        returned, after(grad_mine, feed_shard), normed_all, w_heads, base_home, base_in, grad_hidden, segment_here, scale_one,
+    grad_base, grad_qkv, sums_one, inputs_in = finish(
+        returned, after(grad_mine, feed_shard), normed_all, w_heads, base_home, base_in, grad_hidden, inputs, segment_here, scale_one,
         pairs, parts, rows_all,
     )
     silu_rows = jnp.pad(silu_work.astype(F32) * (1.0 / parts), ((0, 0), (0, depth - silu_work.shape[1])))

time: 867 us -> 866 us (level)
  Pallas kernels: 714 us -> 727 us
  waiting for transfers between devices: 28.2 us -> 16.9 us
    pallas_call x1, Pallas kernels: 78.6 us -> 104 us  [finish(): pl.pallas_call(functools.partial(finish_kernel, pairs=pairs, parts=parts,...]
    pallas_call x1, Pallas kernels: 115 us -> 92.6 us  [feed(): pl.pallas_call(functools.partial(feed_kernel, parts=parts), grid=(groups...]
    pallas_call x1, Pallas kernels: 6.32 us -> 25.7 us  [join(): pl.pallas_call(functools.partial(join_kernel, pairs=pairs, parts=parts),...]
    pallas_call x2, Pallas kernels: 91.8 us -> 78.1 us  [attend(): pl.pallas_call(functools.partial(attend_kernel, bq=bq, bk=bk, per_part=pe...]
    ppermute x20 -> x17, waiting for transfers between devices: 28.1 us -> 16.8 us  [partner(): return lax.ppermute(value, both, pattern)]
    ppermute x20 -> x17, starting transfers between devices: 21 us -> 16.4 us  [partner(): return lax.ppermute(value, both, pattern)]
    unnamed x145 -> x137, local copies, waits for them, and re-layouts: 18.6 us -> 19.9 us
  transfers between devices with their start and end apart: 28 -> 25, of which waited for: 7 -> 5; matrix products, arithmetic and copies ran while one was open for 5% -> 5% of each run, Pallas kernels for 67% -> 71%
where the time goes in v3:
time: 866 us; the launch traced here: 858 us
  Pallas kernels  727 us (84%)
  local copies, waits for them, and re-layouts  47.4 us (5%)
  starting transfers between devices  20.7 us (2%)
  waiting for transfers between devices  16.9 us (2%)
  other arithmetic  16.2 us (2%)
  between operations  15.2 us (2%)
  matrix products  14.4 us (2%)
    pallas_call x2, Pallas kernels, attend_back(): pl.pallas_call(functools.partial(attend_back_kernel, bq=bq, bk=bk, utt=ut...  151 us
    pallas_call x1, Pallas kernels, front(): pl.pallas_call(functools.partial(front_kernel, parts=parts, utt=utt), in_...  128 us
    pallas_call x1, Pallas kernels, sums(): pl.pallas_call(functools.partial(sums_kernel, rows_all=rows_all, parts=pa...  114 us
    pallas_call x1, Pallas kernels, finish(): pl.pallas_call(functools.partial(finish_kernel, pairs=pairs, parts=parts,...  104 us
    pallas_call x1, Pallas kernels, feed(): pl.pallas_call(functools.partial(feed_kernel, parts=parts), grid=(groups...  92.6 us
    pallas_call x2, Pallas kernels, attend(): pl.pallas_call(functools.partial(attend_kernel, bq=bq, bk=bk, per_part=pe...  78.1 us
    pallas_call x1, Pallas kernels, join(): pl.pallas_call(functools.partial(join_kernel, pairs=pairs, parts=parts),...  25.7 us
    unnamed x137, local copies, waits for them, and re-layouts  19.9 us
  transfers between devices with their start and end apart: 25, of which 5 were waited for; matrix products, arithmetic and copies ran while one was open for 5% of the time, Pallas kernels for 71%

profile of v3, /device:TPU:0, one launch (start us, length us, event | category | flops | bytes accessed | tf_op | source)
XLA Modules:
  0.0 857.8 jit_solution(2972715567956644211)
XLA Ops:
  7.2 0.5 collective-permute-start.6
  7.8 0.9 copy-done
  9.0 1.0 constant_dynamic-slice_fusion
  10.0 0.8 pad_maximum_fusion.2
  11.3 2.8 copy.56
  15.0 127.8 %front.1 = (bf16[1024,1024]{1,0:T(8,128)(2,1)}, bf16[4,1024,1024]{2,1,0:T(8,128)(2,1)}, f32[4096,128]{1,0:T(8,128)}, f32[4096,128]{1,0:T(8,128)}, bf16[4096,128]...) custom-call(s32[4]{0:T(128)S(1)} %bitcast.93, ...), custom_call_target="tpu_custom_call" | custom-call | flops 82500001792 | tf_op jit(solution)/shard_map/front/pallas_call | solution.py:1400
  142.8 1.1 copy-done.35
  143.9 1.0 copy-done.42
  144.9 1.0 copy-done.44
  146.0 2.1 collective-permute-start.4
  148.7 1.6 copy-done.34
  150.3 1.4 copy-done.36
  151.7 11.9 %project.1.q_ref.k_ref.v_ref = bf16[6,4096,128]{2,1,0:T(8,128)(2,1)S(1)} custom-call(bf16[4096,1024]{1,0:T(8,128)(2,1)} %bitcast.127, bf16[768,1024]{1,0:T(8,128)(2,1)S(1)} %copy-done.36, f32[4096,128]{1,0:T(8,128)S(1)} %copy-done.33, f32[4096,128]{1,0:T(8,128)S(1)} %copy-done.34), custom_call_target="tpu_custom_call" | custom-call | flops 12099999744 | tf_op jit(solution)/shard_map/project/pallas_call | solution.py:105
  163.6 2.6 copy-done.30
  166.3 39.0 %attend.2 = (bf16[4,1024,128]{2,1,0:T(8,128)(2,1)S(1)}, f32[4096,128]{1,0:T(8,128)S(1)}) custom-call(s32[2]{0:T(128)S(1)} %pad_add_fusion.own_ref, s32[4]{0:T(128)S(1)} %get-tuple-element.142.low_ref, s32[4]{0:T(128)S(1)} %get-tuple-element.141.high_ref, bf16[6,4096,128]{2,1,0:T(8,128)(2,1)} %copy-done.30, bf16[6,4096,128]{2,1,0:T(8,128)(2,1)} %copy-done.30, ...), custom_call_target="tpu_custom_call" | custom-call | flops 38499999744 | tf_op jit(solution)/shard_map/attend/pallas_call | solution.py:181
  205.4 3.3 collective-permute-start.3
  208.8 1.5 collective-permute-start.1
  210.8 0.6 fusion.31
  211.7 2.6 collective-permute-start.7
  214.3 1.1 collective-permute-start.5
  215.4 39.0 %attend.3 = (bf16[4,1024,128]{2,1,0:T(8,128)(2,1)S(1)}, f32[4096,128]{1,0:T(8,128)S(1)}) custom-call(s32[2]{0:T(128)S(1)} %pad_add_fusion.own_ref, s32[4]{0:T(128)S(1)} %get-tuple-element.142.low_ref, s32[4]{0:T(128)S(1)} %get-tuple-element.141.high_ref, bf16[6,4096,128]{2,1,0:T(8,128)(2,1)} %copy-done.30, bf16[6,4096,128]{2,1,0:T(8,128)(2,1)} %copy-done.30, ...), custom_call_target="tpu_custom_call" | custom-call | flops 38499999744 | tf_op jit(solution)/shard_map/attend/pallas_call | solution.py:181
  254.5 1.3 copy-done.40
  256.1 25.7 %join.1 = (f32[1024,1024]{1,0:T(8,128)}, bf16[1024,1024]{1,0:T(8,128)(2,1)S(1)}, bf16[4,1024,128]{2,1,0:T(8,128)(2,1)S(1)}) custom-call(bf16[1024,128]{1,0:T(8,128)(2,1)S(1)} %get-tuple-element.121.refs_0_.refs_1_, bf16[1024,128]{1,0:T(8,128)(2,1)S(1)} %collective-permute-done.1.refs_1_.refs_2_, ...), custom_call_target="tpu_custom_call" | custom-call | flops 19800000512 | tf_op jit(solution)/shard_map/join/pallas_call | solution.py:594
  281.8 1.3 copy-done.38
  283.1 92.6 %feed.1 = (f32[1024,1024]{1,0:T(8,128)}, bf16[1024,1024]{1,0:T(8,128)(2,1)}, f32[1024,1024]{1,0:T(8,128)}, bf16[1024,1024]{1,0:T(8,128)(2,1)}, bf16[16,288,1024]...) custom-call(bf16[1024,1024]{1,0:T(8,128)(2,1)} %copy-done.38, bf16[1024,1024]{1,0:T(8,128)(2,1)} %copy-done.50, ...), custom_call_target="tpu_custom_call" | custom-call | flops 92400001024 | tf_op jit(solution)/shard_map/feed/pallas_call | solution.py:456
  375.8 0.5 collective-permute-start.9
  376.3 3.9 collective-permute-done.8.gin_in_ref
  380.2 3.0 collective-permute-done.9.out_in_ref
  383.2 1.3 copy-done.65
  384.6 16.9 %turn.1 = (f32[1024,1024]{1,0:T(8,128)}, bf16[1024,1024]{1,0:T(8,128)(2,1)S(1)}, bf16[2,1024,1024]{2,1,0:T(8,128)(2,1)}, f32[8,1024]{1,0:T(8,128)S(1)}, bf16[102...) custom-call(s32[2]{0:T(128)S(1)} %pad_add_fusion.own_ref, ...), custom_call_target="tpu_custom_call" | custom-call | flops 16499999744 | tf_op jit(solution)/shard_map/turn/pallas_call | solution.py:657
  401.6 1.7 copy-done.32
  403.3 5.4 out_grad.1
  408.8 3.7 copy-done.3
  412.6 0.5 copy-done.7
  413.4 2.2 collective-permute-start.11
  415.8 0.6 convert_multiply_fusion
  416.4 0.6 and_select_fusion
  417.0 1.9 collective-permute-start.17
  419.0 3.7 collective-permute-done.11
  423.0 0.9 collective-permute-start.10
  423.9 4.0 collective-permute-done.13
  427.9 1.1 pad_maximum_fusion.do_ref
  429.0 75.4 %attend_back.2.refs_4_ = bf16[4,3,1024,128]{3,2,1,0:T(8,128)(2,1)} custom-call(s32[2]{0:T(128)} %copy-done.29, s32[8]{0:T(128)} %get-tuple-element.140.low_ref, s32[8]{0:T(128)} %get-tuple-element.139.high_ref, bf16[6,4096,128]{2,1,0:T(8,128)(2,1)} %copy-done.30, bf16[6,4096,128]{2,1,0:T(8,128)(2,1)} %copy-done.30, bf16[6,4096,128]{2,1,0:T(8,128)(2,1)} %copy-done.30, ...), custom_call_target="tpu_custom_call" | custom-call | flops 72600002560 | tf_op jit(solution)/shard_map/attend_back/pallas_call | solution.py:310
  504.4 3.3 slice_bitcast_fusion.1
  507.7 2.7 collective-permute-start.16
  510.9 1.1 pad_maximum_fusion.1.do_ref
  512.0 3.1 slice_bitcast_fusion
  515.2 75.3 %attend_back.3.refs_5_ = bf16[4,3,1024,128]{3,2,1,0:T(8,128)(2,1)} custom-call(s32[2]{0:T(128)} %copy-done.29, s32[8]{0:T(128)} %get-tuple-element.140.low_ref, s32[8]{0:T(128)} %get-tuple-element.139.high_ref, bf16[6,4096,128]{2,1,0:T(8,128)(2,1)} %copy-done.30, bf16[6,4096,128]{2,1,0:T(8,128)(2,1)} %copy-done.30, bf16[6,4096,128]{2,1,0:T(8,128)(2,1)} %copy-done.30, ...), custom_call_target="tpu_custom_call" | custom-call | flops 72600002560 | tf_op jit(solution)/shard_map/attend_back/pallas_call | solution.py:310
  590.5 2.2 collective-permute-done.14.refs_1_
  592.7 104.1 %finish.1 = (bf16[1024,1024]{1,0:T(8,128)(2,1)}, bf16[768,1024]{1,0:T(8,128)(2,1)}, f32[8,1024]{1,0:T(8,128)}, bf16[1024,1024]{1,0:T(8,128)(2,1)}) custom-call(bf16[3,1024,128]{2,1,0:T(8,128)(2,1)} %get-tuple-element.117.refs_0_, bf16[3,1024,128]{2,1,0:T(8,128)(2,1)} %collective-permute-done.14.refs_1_, ...), custom_call_target="tpu_custom_call" | custom-call | flops 65999998976 | tf_op jit(solution)/shard_map/finish/pallas_call | solution.py:1049
  696.8 3.1 copy.65
  699.9 0.6 select_maximum_fusion.sums_ref
  700.6 113.8 %sums.1 = (bf16[2048,1024]{1,0:T(8,128)(2,1)}, f32[8,20,1024]{2,1,0:T(8,128)}, bf16[1024,1024]{1,0:T(8,128)(2,1)}) custom-call(bf16[1024,1024]{1,0:T(8,128)(2,1)} %bitcast.123, bf16[1024,1024]{1,0:T(8,128)(2,1)} %get-tuple-element.97.inputs_in_hbm, bf16[1024,1024]{1,0:T(8,128)(2,1)} %bitcast.126, bf16[1024,1024]{1,0:T(8,128)(2,1)} %get-tuple-element.112.skips_in_hbm, ...), custom_call_target="tpu_custom_call" | custom-call | flops 109999996928 | tf_op jit(solution)/shard_map/sums/pallas_call | solution.py:1185
  814.3 1.5 copy.59
  816.6 5.0 fusion.3
  821.6 4.7 fusion.29
  826.4 4.4 convolution_bitcast_fusion
  830.8 4.4 convolution_bitcast_fusion.1
  835.2 1.1 slice.118
  836.3 1.1 bitcast_convert_fusion.2
  837.4 2.7 fusion.28
  840.1 2.6 bitcast_convert_fusion
  842.7 2.6 bitcast_convert_fusion.1
  845.3 5.5 copy.66
  (211 shorter events, 5.7 us)
Async XLA Ops:
  7.2 138.6 %all-gather.8.cloned.1.call-start = ((), (), s32[]{:S(2)}) async-start(), calls=%async_computation.4 | async-start | bytes 2621440 | tf_op jit(solution)/shard_map/all_gather | solution.py:1523
  7.2 7.1 collective-permute-start.6
  7.8 6.4 collective-permute-start
  10.8 272.3 %all-gather.10.cloned.1.call-start = ((), (), s32[]{:S(2)}) async-start(), calls=%async_computation.5 | async-start | bytes 10485760 | tf_op jit(solution)/shard_map/all_gather | solution.py:1524
  14.3 196.0 %copy-start.6 = (s32[4,1]{0,1:T(1,128)}, s32[4,1]{0,1:T(1,128)S(1)}, u32[]{:S(2)}) copy-start(s32[4,1]{0,1:T(1,128)S(1)} %reduce-window.13) | copy-start | bytes 52
  14.5 195.9 %copy-start.53 = (f32[4,128]{1,0:T(4,128)}, f32[4,128]{1,0:T(4,128)S(1)}, u32[]{:S(2)}) copy-start(f32[4,128]{1,0:T(4,128)S(1)} %get-tuple-element.131) | copy-start | bytes 6148
  14.5 195.9 %copy-start.55 = (f32[4,128]{1,0:T(4,128)}, f32[4,128]{1,0:T(4,128)S(1)}, u32[]{:S(2)}) copy-start(f32[4,128]{1,0:T(4,128)S(1)} %get-tuple-element.132) | copy-start | bytes 6148
  145.9 369.2 %reduce-scatter.7.cloned.1.call-start = ((), (), s32[]{:S(2)}) async-start(), calls=%async_computation.6 | async-start | bytes 11796480
  146.0 238.5 %copy-start.29 = (s32[2]{0:T(128)}, s32[2]{0:T(128)S(1)}, u32[]{:S(2)}) copy-start(s32[2]{0:T(128)S(1)} %pad_add_fusion.own_ref) | copy-start | bytes 28
  146.0 65.4 %collective-permute-start.4 = (bf16[1024,1024]{1,0:T(8,128)(2,1)}, bf16[1024,1024]{1,0:T(8,128)(2,1)}, u32[]{:S(2)}, u32[]{:S(2)}) collective-permute-start(bf16[1024,1024]{1,0:T(8,128)(2,1)} %bitcast.104), channel_id=1, source_target_pairs={{2,4},{3,5},{4,2},{5,3},{10,12},{11,13},{12,10},{13,11},{18,20},{1... | collective-permute-start | bytes 6291464 | tf_op jit(solution)/shard_map/ppermute | solution.py:1462
  148.5 15.1 %copy-start.60 = (s32[4]{0:T(128)}, s32[4]{0:T(128)S(1)}, u32[]{:S(2)}) copy-start(s32[4]{0:T(128)S(1)} %fusion.21) | copy-start | bytes 52
  151.7 14.5 %copy-start.43 = (bf16[4096,128]{1,0:T(8,128)(2,1)S(1)}, bf16[4096,128]{1,0:T(8,128)(2,1)}, u32[]{:S(2)}) copy-start(bf16[4096,128]{1,0:T(8,128)(2,1)} %copy-done.42) | copy-start | bytes 3145732
  151.7 14.5 %copy-start.45 = (bf16[4096,128]{1,0:T(8,128)(2,1)S(1)}, bf16[4096,128]{1,0:T(8,128)(2,1)}, u32[]{:S(2)}) copy-start(bf16[4096,128]{1,0:T(8,128)(2,1)} %copy-done.44) | copy-start | bytes 3145732
  205.3 5.5 copy-start.4
  205.3 5.5 copy-start.41
  205.3 5.1 copy-start.48
  205.3 6.1 copy-start.49
  205.4 50.4 %collective-permute-start.3 = (bf16[1024,128]{1,0:T(8,128)(2,1)S(1)}, bf16[1024,128]{1,0:T(8,128)(2,1)S(1)}, u32[]{:S(2)}, u32[]{:S(2)}) collective-permute-start(bf16[1024,128]{1,0:T(8,128)(2,1)S(1)} %get-tuple-element.118), channel_id=1, source_target_pairs={{0,5},{1,4},{2,7},{3,6},{4,1},{5,0},{6,3},{7,2},{8,13},{9,12},{10,... | collective-permute-start | bytes 786440 | tf_op jit(solution)/shard_map/ppermute | solution.py:1470
  208.8 47.0 %collective-permute-start.2 = (bf16[1024,128]{1,0:T(8,128)(2,1)S(1)}, bf16[1024,128]{1,0:T(8,128)(2,1)S(1)}, u32[]{:S(2)}, u32[]{:S(2)}) collective-permute-start(bf16[1024,128]{1,0:T(8,128)(2,1)S(1)} %get-tuple-element.119), channel_id=1, source_target_pairs={{0,4},{1,5},{2,6},{3,7},{4,0},{5,1},{6,2},{7,3},{8,12},{9,13},{10,... | collective-permute-start | bytes 786440 | tf_op jit(solution)/shard_map/ppermute | solution.py:1470
  208.8 47.0 %collective-permute-start.1 = (bf16[1024,128]{1,0:T(8,128)(2,1)S(1)}, bf16[1024,128]{1,0:T(8,128)(2,1)S(1)}, u32[]{:S(2)}, u32[]{:S(2)}) collective-permute-start(bf16[1024,128]{1,0:T(8,128)(2,1)S(1)} %get-tuple-element.120), channel_id=1, source_target_pairs={{0,1},{1,0},{2,3},{3,2},{4,5},{5,4},{6,7},{7,6},{8,9},{9,8},{10,11... | collective-permute-start | bytes 786440 | tf_op jit(solution)/shard_map/ppermute | solution.py:1470
  211.7 42.8 %copy-start.50 = (bf16[1024,1024]{1,0:T(8,128)(2,1)}, bf16[1024,1024]{1,0:T(8,128)(2,1)S(1)}, u32[]{:S(2)}) copy-start(bf16[1024,1024]{1,0:T(8,128)(2,1)S(1)} %broadcast_select_fusion.1.cot_own_ref.cot_ref) | copy-start | bytes 6291460
  211.7 44.4 %copy-start.37 = (bf16[8,4,32,1024]{3,2,1,0:T(8,128)(2,1)S(1)}, bf16[8,4,32,1024]{3,2,1,0:T(8,128)(2,1)}, u32[]{:S(2)}) copy-start(bf16[8,4,32,1024]{3,2,1,0:T(8,128)(2,1)} %get-tuple-element.68.refs_5_.w_out_ref) | copy-start | bytes 6291460
  211.7 71.4 %collective-permute-start.7 = (bf16[1024,1024]{1,0:T(8,128)(2,1)S(1)}, bf16[1024,1024]{1,0:T(8,128)(2,1)}, u32[]{:S(2)}, u32[]{:S(2)}) collective-permute-start(bf16[1024,1024]{1,0:T(8,128)(2,1)S(1)} %broadcast_select_fusion.1.cot_own_ref.cot_ref), channel_id=1, source_target_pairs={{0,4},{1,5},{2,6},{3,7},{4,0},{5,1},{6,2},{7,3},{8,12},{9,13},{10,... | collective-permute-start | bytes 6291464 | tf_op jit(solution)/shard_map/ppermute | solution.py:1470
  214.3 41.5 %collective-permute-start.5 = (bf16[1024,1024]{1,0:T(8,128)(2,1)S(1)}, bf16[1024,1024]{1,0:T(8,128)(2,1)S(1)}, u32[]{:S(2)}, u32[]{:S(2)}) collective-permute-start(bf16[1024,1024]{1,0:T(8,128)(2,1)S(1)} %copy-done.8), channel_id=1, source_target_pairs={{2,4},{3,5},{4,2},{5,3},{10,12},{11,13},{12,10},{13,11},{18,20},{1... | collective-permute-start | bytes 6291464 | tf_op jit(solution)/shard_map/ppermute | solution.py:1462
  255.8 26.0 %copy-start.39 = (bf16[4,1024,128]{2,1,0:T(8,128)(2,1)}, bf16[4,1024,128]{2,1,0:T(8,128)(2,1)S(1)}, u32[]{:S(2)}) copy-start(bf16[4,1024,128]{2,1,0:T(8,128)(2,1)S(1)} %get-tuple-element.67.refs_4_.ctx_ref) | copy-start | bytes 3145732
  255.8 26.0 %copy-start.15 = (bf16[1024,128]{1,0:T(8,128)(2,1)}, bf16[1024,128]{1,0:T(8,128)(2,1)S(1)}, u32[]{:S(2)}) copy-start(bf16[1024,128]{1,0:T(8,128)(2,1)S(1)} %collective-permute-done.3.refs_3_.refs_4_) | copy-start | bytes 786436
  255.8 26.0 %copy-start.19 = (bf16[1024,128]{1,0:T(8,128)(2,1)}, bf16[1024,128]{1,0:T(8,128)(2,1)S(1)}, u32[]{:S(2)}) copy-start(bf16[1024,128]{1,0:T(8,128)(2,1)S(1)} %collective-permute-done.2.refs_2_.refs_3_) | copy-start | bytes 786436
  255.8 26.0 %copy-start.21 = (bf16[1024,128]{1,0:T(8,128)(2,1)}, bf16[1024,128]{1,0:T(8,128)(2,1)S(1)}, u32[]{:S(2)}) copy-start(bf16[1024,128]{1,0:T(8,128)(2,1)S(1)} %collective-permute-done.1.refs_1_.refs_2_) | copy-start | bytes 786436
  255.8 25.9 %copy-start.9 = (bf16[1024,1024]{1,0:T(8,128)(2,1)}, bf16[1024,1024]{1,0:T(8,128)(2,1)S(1)}, u32[]{:S(2)}) copy-start(bf16[1024,1024]{1,0:T(8,128)(2,1)S(1)} %collective-permute-done.5.refs_7_.refs_9_) | copy-start | bytes 6291460
  256.0 128.5 %copy-start.5 = (s32[1024,128]{1,0:T(8,128)}, s32[1024,128]{1,0:T(8,128)S(1)}, u32[]{:S(2)}) copy-start(s32[1024,128]{1,0:T(8,128)S(1)} %broadcast_in_dim.56.refs_8_.segment_ref.refs_12_) | copy-start | bytes 1572868
  283.1 92.7 %copy-start.31 = (bf16[4,1024,128]{2,1,0:T(8,128)(2,1)}, bf16[4,1024,128]{2,1,0:T(8,128)(2,1)S(1)}, u32[]{:S(2)}) copy-start(bf16[4,1024,128]{2,1,0:T(8,128)(2,1)S(1)} %get-tuple-element.88.refs_5_) | copy-start | bytes 3145732
  375.8 4.4 collective-permute-start.8
  375.8 7.4 collective-permute-start.9
  384.5 17.0 %copy-start.2 = (bf16[16,288,1024]{2,1,0:T(8,128)(2,1)S(1)}, bf16[16,288,1024]{2,1,0:T(8,128)(2,1)}, u32[]{:S(2)}) copy-start(bf16[16,288,1024]{2,1,0:T(8,128)(2,1)} %get-tuple-element.89.refs_6_) | copy-start | bytes 28311556
  384.5 17.0 %copy-start.16 = (bf16[1024,128]{1,0:T(8,128)(2,1)S(1)}, bf16[1024,128]{1,0:T(8,128)(2,1)}, u32[]{:S(2)}) copy-start(bf16[1024,128]{1,0:T(8,128)(2,1)} %copy-done.15) | copy-start | bytes 786436
  384.5 17.0 %copy-start.20 = (bf16[1024,128]{1,0:T(8,128)(2,1)S(1)}, bf16[1024,128]{1,0:T(8,128)(2,1)}, u32[]{:S(2)}) copy-start(bf16[1024,128]{1,0:T(8,128)(2,1)} %copy-done.19) | copy-start | bytes 786436
  384.5 17.0 %copy-start.22 = (bf16[1024,128]{1,0:T(8,128)(2,1)S(1)}, bf16[1024,128]{1,0:T(8,128)(2,1)}, u32[]{:S(2)}) copy-start(bf16[1024,128]{1,0:T(8,128)(2,1)} %copy-done.21) | copy-start | bytes 786436
  401.5 7.3 copy-start.11
  401.5 7.3 copy-start.13
  401.5 7.3 copy-start.17
  401.5 7.3 copy-start.23
  401.5 7.3 copy-start.25
  401.5 7.3 copy-start.27
  412.5 4.5 copy-start.18
  412.5 6.4 copy-start.14
  412.5 10.2 %copy-start.12 = (bf16[1024,128]{1,0:T(8,128)(2,1)S(1)}, bf16[1024,128]{1,0:T(8,128)(2,1)}, u32[]{:S(2)}) copy-start(bf16[1024,128]{1,0:T(8,128)(2,1)} %copy-done.11) | copy-start | bytes 786436
  412.6 288.0 %reduce-scatter.5.cloned.1.call-start = ((), (), s32[]{:S(2)}) async-start(), calls=%async_computation.2 | async-start | bytes 2949120 | tf_op jit(solution)/shard_map/reduce_scatter | solution.py:1577
  413.4 9.3 %collective-permute-start.11 = (bf16[1024,128]{1,0:T(8,128)(2,1)S(1)}, bf16[1024,128]{1,0:T(8,128)(2,1)S(1)}, u32[]{:S(2)}, u32[]{:S(2)}) collective-permute-start(bf16[1024,128]{1,0:T(8,128)(2,1)S(1)} %copy-done.28), channel_id=1, source_target_pairs={{0,1},{1,0},{2,3},{3,2},{4,5},{5,4},{6,7},{7,6},{8,9},{9,8},{10,11... | collective-permute-start | bytes 786440 | tf_op jit(solution)/shard_map/ppermute | solution.py:1470
  415.6 7.4 collective-permute-start.12
  415.6 12.3 %collective-permute-start.13 = (bf16[1024,128]{1,0:T(8,128)(2,1)S(1)}, bf16[1024,128]{1,0:T(8,128)(2,1)S(1)}, u32[]{:S(2)}, u32[]{:S(2)}) collective-permute-start(bf16[1024,128]{1,0:T(8,128)(2,1)S(1)} %copy-done.24), channel_id=1, source_target_pairs={{0,5},{1,4},{2,7},{3,6},{4,1},{5,0},{6,3},{7,2},{8,13},{9,12},{10,... | collective-permute-start | bytes 786440 | tf_op jit(solution)/shard_map/ppermute | solution.py:1470
  417.0 93.4 %collective-permute-start.17 = (bf16[1024,128]{1,0:T(8,128)(2,1)S(1)}, bf16[1024,128]{1,0:T(8,128)(2,1)S(1)}, u32[]{:S(2)}, u32[]{:S(2)}) collective-permute-start(bf16[1024,128]{1,0:T(8,128)(2,1)S(1)} %copy-done.18), channel_id=1, source_target_pairs={{0,1},{1,0},{2,3},{3,2},{4,5},{5,4},{6,7},{7,6},{8,9},{9,8},{10,11... | collective-permute-start | bytes 786440 | tf_op jit(solution)/shard_map/ppermute | solution.py:1470
  419.0 91.5 %collective-permute-start.18 = (bf16[1024,128]{1,0:T(8,128)(2,1)S(1)}, bf16[1024,128]{1,0:T(8,128)(2,1)S(1)}, u32[]{:S(2)}, u32[]{:S(2)}) collective-permute-start(bf16[1024,128]{1,0:T(8,128)(2,1)S(1)} %copy-done.14), channel_id=1, source_target_pairs={{0,4},{1,5},{2,6},{3,7},{4,0},{5,1},{6,2},{7,3},{8,12},{9,13},{10,... | collective-permute-start | bytes 786440 | tf_op jit(solution)/shard_map/ppermute | solution.py:1470
  422.7 88.2 %collective-permute-start.19 = (bf16[1024,128]{1,0:T(8,128)(2,1)S(1)}, bf16[1024,128]{1,0:T(8,128)(2,1)S(1)}, u32[]{:S(2)}, u32[]{:S(2)}) collective-permute-start(bf16[1024,128]{1,0:T(8,128)(2,1)S(1)} %copy-done.12), channel_id=1, source_target_pairs={{0,5},{1,4},{2,7},{3,6},{4,1},{5,0},{6,3},{7,2},{8,13},{9,12},{10,... | collective-permute-start | bytes 786440 | tf_op jit(solution)/shard_map/ppermute | solution.py:1470
  423.0 89.0 %collective-permute-start.10 = (bf16[2,1024,1024]{2,1,0:T(8,128)(2,1)}, bf16[2,1024,1024]{2,1,0:T(8,128)(2,1)S(1)}, u32[]{:S(2)}, u32[]{:S(2)}) collective-permute-start(bf16[2,1024,1024]{2,1,0:T(8,128)(2,1)} %get-tuple-element.77), channel_id=1, source_target_pairs={{2,4},{3,5},{4,2},{5,3},{10,12},{11,13},{12,10},{13,11},{18,20},{1... | collective-permute-start | bytes 12582920 | tf_op jit(solution)/shard_map/ppermute | solution.py:1462
  504.4 7.6 copy-start.51
  507.7 82.8 %collective-permute-start.16 = (bf16[3,1024,128]{2,1,0:T(8,128)(2,1)}, bf16[3,1024,128]{2,1,0:T(8,128)(2,1)}, u32[]{:S(2)}, u32[]{:S(2)}) collective-permute-start(bf16[3,1024,128]{2,1,0:T(8,128)(2,1)} %get-tuple-element.114), channel_id=1, source_target_pairs={{0,5},{1,4},{2,7},{3,6},{4,1},{5,0},{6,3},{7,2},{8,13},{9,12},{10,... | collective-permute-start | bytes 2359304 | tf_op jit(solution)/shard_map/ppermute | solution.py:1470
  510.4 80.1 %collective-permute-start.15 = (bf16[3,1024,128]{2,1,0:T(8,128)(2,1)S(1)}, bf16[3,1024,128]{2,1,0:T(8,128)(2,1)}, u32[]{:S(2)}, u32[]{:S(2)}) collective-permute-start(bf16[3,1024,128]{2,1,0:T(8,128)(2,1)S(1)} %get-tuple-element.115), channel_id=1, source_target_pairs={{0,4},{1,5},{2,6},{3,7},{4,0},{5,1},{6,2},{7,3},{8,12},{9,13},{10,... | collective-permute-start | bytes 2359304 | tf_op jit(solution)/shard_map/ppermute | solution.py:1470
  510.4 82.3 %collective-permute-start.14 = (bf16[3,1024,128]{2,1,0:T(8,128)(2,1)S(1)}, bf16[3,1024,128]{2,1,0:T(8,128)(2,1)}, u32[]{:S(2)}, u32[]{:S(2)}) collective-permute-start(bf16[3,1024,128]{2,1,0:T(8,128)(2,1)S(1)} %get-tuple-element.116), channel_id=1, source_target_pairs={{0,1},{1,0},{2,3},{3,2},{4,5},{5,4},{6,7},{7,6},{8,9},{9,8},{10,11... | collective-permute-start | bytes 2359304 | tf_op jit(solution)/shard_map/ppermute | solution.py:1470
  515.1 320.1 %all-gather.6.cloned.1.call-start = ((), (), s32[]{:S(2)}) async-start(), calls=%async_computation.3 | async-start | bytes 5308416 | tf_op jit(solution)/shard_map/all_gather | solution.py:1579
  816.6 5.0 copy-start.46
  821.6 4.7 copy-start.62
  821.6 4.7 copy-start.66
  821.6 4.8 copy-start.67
  845.3 5.5 copy-start.1
  (29 other events, 69.1 us)
Sparse Core Ops, SparseCore 0:
  11.0 76.3 all-gather.7
  146.0 87.4 all-gather.9
  412.7 94.2 reduce-scatter.6
  515.3 74.5 reduce-scatter.4
  700.7 54.3 all-gather.5

commit v4 on v3

--- a/solution.py
+++ b/solution.py
@@ -379,13 +379,13 @@
         for k in range(1, parts):
             heads_part(k).start()
 
-    @pl.when(step == 2)
+    @pl.when(step == 1)
     def _():
         for k in range(1, parts):
             heads_part(k).wait()
         heads_part(parts).start()
 
-    @pl.when(step == 4)
+    @pl.when(step == 2)
     def _():
         heads_part(parts).wait()
         heads_part(parts + 1).start()
@@ -419,15 +419,17 @@
         gup = gu if side == 0 else gup + gu
         gdown = gd if side == 0 else gdown + gd
 
+        out_to, gin_to = (out_own_ref, gin_own_ref) if side == 0 else (out_sum, gin_sum)
+
         @pl.when(step == 0)
         def _():
-            out_sum[side] = out
-            gin_sum[side] = gin
+            out_to[...] = out
+            gin_to[...] = gin
 
         @pl.when(step > 0)
         def _():
-            out_sum[side] += out
-            gin_sum[side] += gin
+            out_to[...] += out
+            gin_to[...] += gin
 
     per = weights_ref.shape[2]
     grads_ref[:, :per] = gup.astype(BF).reshape(-1, per, depth)
@@ -436,10 +438,8 @@
 
     @pl.when(step == last)
     def _():
-        out_own_ref[...] = out_sum[0]
-        out_other_ref[...] = out_sum[1].astype(BF)
-        gin_own_ref[...] = gin_sum[0]
-        gin_other_ref[...] = gin_sum[1].astype(BF)
+        out_other_ref[...] = out_sum[...].astype(BF)
+        gin_other_ref[...] = gin_sum[...].astype(BF)
 
         heads_part(parts + 1).wait()
 
@@ -447,8 +447,8 @@
 def feed(x_own, cot_own, cot_other, weights, heads, spare, parts):
     frames, depth = x_own.shape
     groups, _, per, _ = weights.shape
-    chunk = 256
-    whole = pl.BlockSpec((frames, depth), lambda j: (0, 0))
+    chunk = 512
+    whole = pl.BlockSpec((frames, depth), lambda j: (0, 0), pipeline_mode=pl.Buffered(1))
     cut = pl.BlockSpec((chunk // per, 2, per, depth), lambda j: (j, 0, 0, 0))
     grads = pl.BlockSpec((chunk // per, 2 * per + spare, depth), lambda j: (j, 0, 0))
     shape = lambda *s: jax.ShapeDtypeStruct(*s)
@@ -468,8 +468,8 @@
         ],
         scratch_shapes=[
             pltpu.VMEM((frames, depth), BF),
-            pltpu.VMEM((2, frames, depth), F32),
-            pltpu.VMEM((2, frames, depth), F32),
+            pltpu.VMEM((frames, depth), F32),
+            pltpu.VMEM((frames, depth), F32),
             pltpu.SemaphoreType.DMA,
             pltpu.SemaphoreType.DMA((2 * (PIECES + parts + 3),)),
         ],
@@ -811,6 +811,22 @@
         size *= 2
 
 
+def gather_rows(sender, own_hbm, out, semaphore):
+    columns = out.shape[0] // 2
+    slot = sender.d // 2 + columns * (sender.d % 2)
+    copy = pltpu.make_async_copy(own_hbm, out.at[slot], semaphore)
+    copy.start()
+    yield
+    copy.wait()
+    size = 1
+    while size < 2 * columns:
+        cut = out.at[pl.ds(slot // size * size, size)]
+        copy = sender.send(cut, cut, "dp", 2 * size if size < columns else 1)
+        yield
+        copy.wait()
+        size *= 2
+
+
 def spread_sums(sender, own, held, out, parts):
     half = parts // 2
     slot = (sender.d // 2) * 2 + sender.z // half
@@ -850,8 +866,8 @@
     prev_hbm, refs = refs[:cut], refs[cut:]
     own_hbm, refs = refs[:pairs], refs[pairs:]
     (
-        normed_hbm, weight_hbm, base_hbm, base_in_hbm, grad_hbm, inputs_hbm, segment_ref, scale_ref,
-        grad_base_ref, qkv_ref, sums_ref, inputs_in_hbm,
+        normed_hbm, weight_hbm, base_hbm, base_in_hbm, grad_hbm, inputs_hbm, shard_hbm, segment_ref, scale_ref,
+        grad_base_ref, qkv_ref, sums_ref, shards_ref, inputs_in_hbm,
         prev, own, normed, weight, base, grad_hidden, arrived, total, qkv_held, qkv_in, loads, sems,
     ) = refs
     d, z, core, half = mesh_spot(parts)
@@ -915,8 +931,12 @@
     def _():
         pltpu.make_async_copy(base_in_hbm, base, loads.at[at + 1]).start()
 
+    sender = Sender(sems, parts + PIECES)
+    running = [gather_rows(sender, shard_hbm, shards_ref, loads.at[len(own_hbm) + cut + 4])]
+    run_all(running)
     for copy in first:
         copy.wait()
+    run_all(running)
     for kind in range(3):
         for pair in range(pairs):
 
@@ -929,7 +949,6 @@
                 at_row = k * 3 * width + kind * width + pair * LANES
                 qkv_held[at_row : at_row + LANES, :] = grad[:, k * wide : (k + 1) * wide]
 
-    sender = Sender(sems, parts + PIECES)
     down = [
         [("dp", bit) for bit in dp_bits] + [("tensor", half)],
         [("dp", bit) for bit in reversed(dp_bits)] + [("tensor", half)],
@@ -972,7 +991,7 @@
             starts[side] = starts[side] + (core - z // half) * size
 
     up = [line[:-1] + [("dp", 1)] for line in down]
-    running = [sum_tree(sender, qkv_held, qkv_in, down, go_home, up, qkv_ref, 0)]
+    running.append(sum_tree(sender, qkv_held, qkv_in, down, go_home, up, qkv_ref, 0))
     run_all(running)
 
     for copy in second:
@@ -1032,7 +1051,7 @@
 
 
 def finish(
-    prev, own, normed_all, weight, base, base_in, grad_hidden, inputs, segment, scale, pairs, parts, rows_all
+    prev, own, normed_all, weight, base, base_in, grad_hidden, inputs, shard, segment, scale, pairs, parts, rows_all
 ):
     frames, depth = base.shape
     utt = scale.shape[0]
@@ -1041,19 +1060,20 @@
     while units * depth // wide % (16 * rows_all * 2):
         wide //= 2
     qkv_shape = (units * depth // wide, wide)
-    copies = parts + 2 + PIECES + 5 * rows_all.bit_length() + parts.bit_length()
+    copies = parts + 2 + PIECES + 6 * rows_all.bit_length() + parts.bit_length()
     anywhere = pl.BlockSpec(memory_space=pl.ANY)
     vmem = pl.BlockSpec(memory_space=pltpu.VMEM)
     shape = lambda *s: jax.ShapeDtypeStruct(*s)
     block = (3, frames, LANES)
     return pl.pallas_call(
         functools.partial(finish_kernel, pairs=pairs, parts=parts, utt=utt, rows_all=rows_all),
-        in_specs=[anywhere] * (len(prev) + pairs + 6) + [vmem] * 2,
-        out_specs=[vmem] * 3 + [anywhere],
+        in_specs=[anywhere] * (len(prev) + pairs + 7) + [vmem] * 2,
+        out_specs=[vmem] * 4 + [anywhere],
         out_shape=[
             shape((frames, depth), BF),
             shape(qkv_shape, BF),
             shape((2 * utt, depth), F32),
+            shape((rows_all,) + shard.shape, BF),
             shape((frames, depth), BF),
         ],
         scratch_shapes=[
@@ -1067,7 +1087,7 @@
             pltpu.VMEM((frames, depth), F32),
             pltpu.VMEM(qkv_shape, BF),
             pltpu.VMEM(qkv_shape, BF),
-            pltpu.SemaphoreType.DMA((4 + pairs + len(prev),)),
+            pltpu.SemaphoreType.DMA((5 + pairs + len(prev),)),
             pltpu.SemaphoreType.DMA((2 * copies,)),
         ],
         compiler_params=pltpu.CompilerParams(
@@ -1075,7 +1095,7 @@
         ),
         cost_estimate=cost(60),
         name="finish",
-    )(*prev, *own, normed_all, weight, base, base_in, grad_hidden, inputs, segment, scale)
+    )(*prev, *own, normed_all, weight, base, base_in, grad_hidden, inputs, shard, segment, scale)
 
 
 def sums_kernel(
@@ -1209,6 +1229,31 @@
     return skip_sum, all_sums, grad_base_in
 
 
+def spread_out_kernel(shard_ref, up_ref, down_ref):
+    per = down_ref.shape[0]
+    rows = shard_ref[0].astype(F32)
+    up_ref[...] = rows[:per].T
+    down_ref[...] = rows[per : 2 * per]
+
+
+def spread_out(shards, per):
+    count, _, depth = shards.shape
+    units = count * per
+    if per % LANES:
+        up = jnp.transpose(shards[:, :per].reshape(units, depth)).astype(F32)
+        return up, shards[:, per : 2 * per].reshape(units, depth).astype(F32)
+    return pl.pallas_call(
+        spread_out_kernel,
+        grid=(count,),
+        in_specs=[pl.BlockSpec((1,) + shards.shape[1:], lambda i: (i, 0, 0))],
+        out_specs=[pl.BlockSpec((depth, per), lambda i: (0, i)), pl.BlockSpec((per, depth), lambda i: (i, 0))],
+        out_shape=[jax.ShapeDtypeStruct((depth, units), F32), jax.ShapeDtypeStruct((units, depth), F32)],
+        compiler_params=pltpu.CompilerParams(vmem_limit_bytes=24 * MIB),
+        cost_estimate=cost(4),
+        name="spread_out",
+    )(shards)
+
+
 def front_kernel(
     ends_ref, inputs_ref, skips_ref, w_in_ref, w_res_ref, segment_ref, shift_ref, scale_ref, rate_ref, weight_hbm, w_out_ref,
     base_ref, out_ref, cos_ref, sin_ref, qmark_ref, kmark_ref, weight_in_hbm, w_out_all_ref, away, local, sems,
@@ -1574,12 +1619,7 @@
     grad_feed = out_grad(low_grad, ctx_mine, ctx_last, grad_feed, 2 * per_u, pairs, parts, columns)
     grad_feed = grad_feed.reshape(columns, parts, 2 * per_u + spare, depth)
     feed_sum = lax.psum_scatter(grad_feed, "dp", scatter_dimension=0, axis_index_groups=same_core)
-    grad_feed = lax.psum_scatter(feed_sum, "tensor", scatter_dimension=0)
-    feed_shard = grad_feed
-    grad_feed = lax.all_gather(grad_feed, "dp")
-    grad_up = jnp.transpose(grad_feed[:, :per_u].reshape(units, depth)).astype(F32)
-    grad_down = grad_feed[:, per_u : 2 * per_u].reshape(units, depth).astype(F32)
-    grad_out = grad_feed[:, 2 * per_u : 2 * per_u + per_o].reshape(ws, depth).astype(F32)
+    feed_shard = lax.psum_scatter(feed_sum, "tensor", scatter_dimension=0)
 
     grad_mine = []
     for pair in range(pairs):
@@ -1596,10 +1636,13 @@
     for grads in grad_mine[:-1]:
         returned += exchange([grads[b] for b in range(parts)])
     block_out_in, skips_in = moved(block_out)
-    grad_base, grad_qkv, sums_one, inputs_in = finish(
-        returned, after(grad_mine, feed_shard), normed_all, w_heads, base_home, base_in, grad_hidden, inputs, segment_here, scale_one,
-        pairs, parts, rows_all,
+    grad_base, grad_qkv, sums_one, shards, inputs_in = finish(
+        returned, grad_mine, normed_all, w_heads, base_home, base_in, grad_hidden, inputs, feed_shard.reshape(-1, depth), segment_here,
+        scale_one, pairs, parts, rows_all,
     )
+    shards = jnp.transpose(shards.reshape((2, columns) + shards.shape[1:]), (1, 0, 2, 3))
+    grad_up, grad_down = spread_out(shards.reshape((rows_all,) + shards.shape[2:]), per_u)
+    grad_out = shards[:, :, 2 * per_u : 2 * per_u + per_o].reshape(ws, depth).astype(F32)
     silu_rows = jnp.pad(silu_work.astype(F32) * (1.0 / parts), ((0, 0), (0, depth - silu_work.shape[1])))
     skip_sum, all_sums, grad_base_in = sums(
         inputs, inputs_in, skip_input, skips_in, grad_base, jnp.concatenate([sums_one, sums_two, silu_rows]),

time: 866 us -> 856 us (0.988)
    pallas_call x2, Pallas kernels: 151 us -> 164 us  [attend_back(): pl.pallas_call(functools.partial(attend_back_kernel, bq=bq, bk=bk, utt=ut...]
    pallas_call x1, Pallas kernels: 114 us -> 105 us  [sums(): pl.pallas_call(functools.partial(sums_kernel, rows_all=rows_all, parts=pa...]
    unnamed x137 -> x139, local copies, waits for them, and re-layouts: 19.9 us -> 19.9 us
  transfers between devices with their start and end apart: 25 -> 24, of which waited for: 5 -> 4; matrix products, arithmetic and copies ran while one was open for 5% -> 2% of each run, Pallas kernels for 71% -> 48%
where the time goes in v4:
time: 856 us; the launch traced here: 845 us
  Pallas kernels  729 us (85%)
  local copies, waits for them, and re-layouts  39.9 us (5%)
  starting transfers between devices  20.3 us (2%)
  between operations  15.2 us (2%)
  waiting for transfers between devices  14.8 us (2%)
  matrix products  14.4 us (2%)
  other arithmetic  11.8 us (1%)
    pallas_call x2, Pallas kernels, attend_back(): pl.pallas_call(functools.partial(attend_back_kernel, bq=bq, bk=bk, utt=ut...  164 us
    pallas_call x1, Pallas kernels, front(): pl.pallas_call(functools.partial(front_kernel, parts=parts, utt=utt), in_...  128 us
    pallas_call x1, Pallas kernels, sums(): pl.pallas_call(functools.partial(sums_kernel, rows_all=rows_all, parts=pa...  105 us
    pallas_call x1, Pallas kernels, finish(): pl.pallas_call(functools.partial(finish_kernel, pairs=pairs, parts=parts,...  102 us
    pallas_call x1, Pallas kernels, feed(): pl.pallas_call(functools.partial(feed_kernel, parts=parts), grid=(groups...  87.6 us
    pallas_call x2, Pallas kernels, attend(): pl.pallas_call(functools.partial(attend_kernel, bq=bq, bk=bk, per_part=pe...  78.1 us
    pallas_call x1, Pallas kernels, join(): pl.pallas_call(functools.partial(join_kernel, pairs=pairs, parts=parts),...  25.8 us
    unnamed x139, local copies, waits for them, and re-layouts  19.9 us
  transfers between devices with their start and end apart: 24, of which 4 were waited for; matrix products, arithmetic and copies ran while one was open for 2% of the time, Pallas kernels for 48%

profile of v4, /device:TPU:0, one launch (start us, length us, event | category | flops | bytes accessed | tf_op | source)
XLA Modules:
  0.0 845.4 jit_solution(16149407945949675327)
XLA Ops:
  7.2 0.5 collective-permute-start.6
  7.8 0.9 copy-done
  9.0 1.0 constant_dynamic-slice_fusion
  10.0 0.8 pad_maximum_fusion.2
  11.3 2.8 copy.56
  14.5 0.2 fusion.1
  15.0 127.8 %front.1 = (bf16[1024,1024]{1,0:T(8,128)(2,1)}, bf16[4,1024,1024]{2,1,0:T(8,128)(2,1)}, f32[4096,128]{1,0:T(8,128)}, f32[4096,128]{1,0:T(8,128)}, bf16[4096,128]...) custom-call(s32[4]{0:T(128)S(1)} %bitcast.94, ...), custom_call_target="tpu_custom_call" | custom-call | flops 82500001792 | tf_op jit(solution)/shard_map/front/pallas_call | solution.py:1445
  142.8 1.1 copy-done.35
  143.9 1.0 copy-done.42
  144.9 1.0 copy-done.44
  146.0 2.1 collective-permute-start.4
  148.7 1.6 copy-done.34
  150.3 1.4 copy-done.36
  151.7 11.9 %project.1.q_ref.k_ref.v_ref = bf16[6,4096,128]{2,1,0:T(8,128)(2,1)S(1)} custom-call(bf16[4096,1024]{1,0:T(8,128)(2,1)} %bitcast.131, bf16[768,1024]{1,0:T(8,128)(2,1)S(1)} %copy-done.36, f32[4096,128]{1,0:T(8,128)S(1)} %copy-done.33, f32[4096,128]{1,0:T(8,128)S(1)} %copy-done.34), custom_call_target="tpu_custom_call" | custom-call | flops 12099999744 | tf_op jit(solution)/shard_map/project/pallas_call | solution.py:105
  163.6 2.6 copy-done.30
  166.3 39.0 %attend.2 = (bf16[4,1024,128]{2,1,0:T(8,128)(2,1)S(1)}, f32[4096,128]{1,0:T(8,128)S(1)}) custom-call(s32[2]{0:T(128)S(1)} %pad_add_fusion.own_ref, s32[4]{0:T(128)S(1)} %get-tuple-element.144.low_ref, s32[4]{0:T(128)S(1)} %get-tuple-element.143.high_ref, bf16[6,4096,128]{2,1,0:T(8,128)(2,1)} %copy-done.30, bf16[6,4096,128]{2,1,0:T(8,128)(2,1)} %copy-done.30, ...), custom_call_target="tpu_custom_call" | custom-call | flops 38499999744 | tf_op jit(solution)/shard_map/attend/pallas_call | solution.py:181
  205.4 3.3 collective-permute-start.3
  208.8 1.5 collective-permute-start.1
  210.4 0.4 fusion.26
  210.8 0.6 fusion.31
  211.4 0.2 broadcast_select_fusion.1.cot_own_ref.cot_ref
  211.7 2.6 collective-permute-start.7
  214.3 1.0 collective-permute-start.5
  215.3 39.0 %attend.3 = (bf16[4,1024,128]{2,1,0:T(8,128)(2,1)S(1)}, f32[4096,128]{1,0:T(8,128)S(1)}) custom-call(s32[2]{0:T(128)S(1)} %pad_add_fusion.own_ref, s32[4]{0:T(128)S(1)} %get-tuple-element.144.low_ref, s32[4]{0:T(128)S(1)} %get-tuple-element.143.high_ref, bf16[6,4096,128]{2,1,0:T(8,128)(2,1)} %copy-done.30, bf16[6,4096,128]{2,1,0:T(8,128)(2,1)} %copy-done.30, ...), custom_call_target="tpu_custom_call" | custom-call | flops 38499999744 | tf_op jit(solution)/shard_map/attend/pallas_call | solution.py:181
  254.3 1.3 copy-done.40
  255.9 25.8 %join.1 = (f32[1024,1024]{1,0:T(8,128)}, bf16[1024,1024]{1,0:T(8,128)(2,1)S(1)}, bf16[4,1024,128]{2,1,0:T(8,128)(2,1)S(1)}) custom-call(bf16[1024,128]{1,0:T(8,128)(2,1)S(1)} %get-tuple-element.123.refs_0_.refs_1_, bf16[1024,128]{1,0:T(8,128)(2,1)S(1)} %collective-permute-done.1.refs_1_.refs_2_, ...), custom_call_target="tpu_custom_call" | custom-call | flops 19800000512 | tf_op jit(solution)/shard_map/join/pallas_call | solution.py:594
  281.8 1.3 copy-done.38
  283.1 87.6 %feed.1 = (f32[1024,1024]{1,0:T(8,128)}, bf16[1024,1024]{1,0:T(8,128)(2,1)}, f32[1024,1024]{1,0:T(8,128)}, bf16[1024,1024]{1,0:T(8,128)(2,1)}, bf16[16,288,1024]...) custom-call(bf16[1024,1024]{1,0:T(8,128)(2,1)} %copy-done.38, bf16[1024,1024]{1,0:T(8,128)(2,1)} %copy-done.49, ...), custom_call_target="tpu_custom_call" | custom-call | flops 92400001024 | tf_op jit(solution)/shard_map/feed/pallas_call | solution.py:456
  370.8 0.5 collective-permute-start.9
  371.3 3.9 collective-permute-done.8.gin_in_ref
  375.2 3.0 collective-permute-done.9.out_in_ref
  378.2 1.3 copy-done.64
  379.5 16.6 %turn.1 = (f32[1024,1024]{1,0:T(8,128)}, bf16[1024,1024]{1,0:T(8,128)(2,1)S(1)}, bf16[2,1024,1024]{2,1,0:T(8,128)(2,1)}, f32[8,1024]{1,0:T(8,128)S(1)}, bf16[102...) custom-call(s32[2]{0:T(128)S(1)} %pad_add_fusion.own_ref, ...), custom_call_target="tpu_custom_call" | custom-call | flops 16499999744 | tf_op jit(solution)/shard_map/turn/pallas_call | solution.py:657
  396.3 1.7 copy-done.32
  398.0 5.5 out_grad.1
  403.5 3.7 copy-done.3
  407.3 0.5 copy-done.7
  408.1 2.7 collective-permute-start.11
  411.0 0.6 convert_multiply_fusion
  411.6 0.6 and_select_fusion
  412.2 1.9 collective-permute-start.17
  414.1 3.7 collective-permute-done.11
  418.1 0.9 collective-permute-start.10
  419.0 4.1 collective-permute-done.13
  423.1 1.1 pad_maximum_fusion.do_ref
  424.2 82.2 %attend_back.2.refs_4_ = bf16[4,3,1024,128]{3,2,1,0:T(8,128)(2,1)} custom-call(s32[2]{0:T(128)} %copy-done.29, s32[8]{0:T(128)} %get-tuple-element.142.low_ref, s32[8]{0:T(128)} %get-tuple-element.141.high_ref, bf16[6,4096,128]{2,1,0:T(8,128)(2,1)} %copy-done.30, bf16[6,4096,128]{2,1,0:T(8,128)(2,1)} %copy-done.30, bf16[6,4096,128]{2,1,0:T(8,128)(2,1)} %copy-done.30, ...), custom_call_target="tpu_custom_call" | custom-call | flops 72600002560 | tf_op jit(solution)/shard_map/attend_back/pallas_call | solution.py:310
  506.3 3.3 slice_bitcast_fusion.1
  509.7 2.1 collective-permute-start.16
  511.8 0.5 collective-permute-start.14
  512.2 1.1 pad_maximum_fusion.1.do_ref
  513.4 3.1 slice_bitcast_fusion
  516.5 81.6 %attend_back.3.refs_5_ = bf16[4,3,1024,128]{3,2,1,0:T(8,128)(2,1)} custom-call(s32[2]{0:T(128)} %copy-done.29, s32[8]{0:T(128)} %get-tuple-element.142.low_ref, s32[8]{0:T(128)} %get-tuple-element.141.high_ref, bf16[6,4096,128]{2,1,0:T(8,128)(2,1)} %copy-done.30, bf16[6,4096,128]{2,1,0:T(8,128)(2,1)} %copy-done.30, bf16[6,4096,128]{2,1,0:T(8,128)(2,1)} %copy-done.30, ...), custom_call_target="tpu_custom_call" | custom-call | flops 72600002560 | tf_op jit(solution)/shard_map/attend_back/pallas_call | solution.py:310
  598.2 102.5 %finish.1 = (bf16[1024,1024]{1,0:T(8,128)(2,1)}, bf16[768,1024]{1,0:T(8,128)(2,1)}, f32[8,1024]{1,0:T(8,128)}, bf16[8,288,1024]{2,1,0:T(8,128)(2,1)}, bf16[1024,1024]{1,0:T(8,128)(2,1)}) custom-call(bf16[3,1024,128]{2,1,0:T(8,128)(2,1)} %get-tuple-element.119.refs_0_, bf16[3,1024,128]{2,1,0:T(8,128)(2,1)} %collective-permute-done.14.refs_1_, ...), custom_call_target="tpu_custom_call" | custom-call | flops 65999998976 | tf_op jit(solution)/shard_map/finish/pallas_call | solution.py:1068
  700.7 1.4 select_maximum_fusion.sums_ref
  702.1 104.9 %sums.1 = (bf16[2048,1024]{1,0:T(8,128)(2,1)}, f32[8,20,1024]{2,1,0:T(8,128)}, bf16[1024,1024]{1,0:T(8,128)(2,1)}) custom-call(bf16[1024,1024]{1,0:T(8,128)(2,1)} %bitcast.126, bf16[1024,1024]{1,0:T(8,128)(2,1)} %get-tuple-element.96.inputs_in_hbm, bf16[1024,1024]{1,0:T(8,128)(2,1)} %bitcast.129, bf16[1024,1024]{1,0:T(8,128)(2,1)} %get-tuple-element.114.skips_in_hbm, ...), custom_call_target="tpu_custom_call" | custom-call | flops 109999996928 | tf_op jit(solution)/shard_map/sums/pallas_call | solution.py:1205
  807.0 1.7 copy.59
  808.8 4.4 convolution_bitcast_fusion
  813.2 4.4 convolution_bitcast_fusion.1
  817.6 2.1 copy.65
  820.3 6.8 fusion.29
  827.2 0.5 copy.70
  827.7 1.1 bitcast_convert_fusion
  828.9 4.6 spread_out.1
  833.5 5.0 fusion.3
  (209 shorter events, 4.3 us)
Async XLA Ops:
  7.2 138.6 %all-gather.5.cloned.1.call-start = ((), (), s32[]{:S(2)}) async-start(), calls=%async_computation.3 | async-start | bytes 2621440 | tf_op jit(solution)/shard_map/all_gather | solution.py:1568
  7.2 7.1 collective-permute-start.6
  7.8 6.4 collective-permute-start
  10.8 272.3 %all-gather.7.cloned.1.call-start = ((), (), s32[]{:S(2)}) async-start(), calls=%async_computation.4 | async-start | bytes 10485760 | tf_op jit(solution)/shard_map/all_gather | solution.py:1569
  14.3 196.0 %copy-start.6 = (s32[4,1]{0,1:T(1,128)}, s32[4,1]{0,1:T(1,128)S(1)}, u32[]{:S(2)}) copy-start(s32[4,1]{0,1:T(1,128)S(1)} %reduce-window.13) | copy-start | bytes 52
  14.5 195.9 %copy-start.52 = (f32[4,128]{1,0:T(4,128)}, f32[4,128]{1,0:T(4,128)S(1)}, u32[]{:S(2)}) copy-start(f32[4,128]{1,0:T(4,128)S(1)} %get-tuple-element.133) | copy-start | bytes 6148
  14.5 195.9 %copy-start.54 = (f32[4,128]{1,0:T(4,128)}, f32[4,128]{1,0:T(4,128)S(1)}, u32[]{:S(2)}) copy-start(f32[4,128]{1,0:T(4,128)S(1)} %get-tuple-element.134) | copy-start | bytes 6148
  145.9 370.6 %reduce-scatter.7.cloned.1.call-start = ((), (), s32[]{:S(2)}) async-start(), calls=%async_computation.5 | async-start | bytes 11796480
  146.0 233.5 %copy-start.29 = (s32[2]{0:T(128)}, s32[2]{0:T(128)S(1)}, u32[]{:S(2)}) copy-start(s32[2]{0:T(128)S(1)} %pad_add_fusion.own_ref) | copy-start | bytes 28
  146.0 65.4 %collective-permute-start.4 = (bf16[1024,1024]{1,0:T(8,128)(2,1)}, bf16[1024,1024]{1,0:T(8,128)(2,1)}, u32[]{:S(2)}, u32[]{:S(2)}) collective-permute-start(bf16[1024,1024]{1,0:T(8,128)(2,1)} %bitcast.107), channel_id=1, source_target_pairs={{2,4},{3,5},{4,2},{5,3},{10,12},{11,13},{12,10},{13,11},{18,20},{1... | collective-permute-start | bytes 6291464 | tf_op jit(solution)/shard_map/ppermute | solution.py:1507
  148.5 15.1 %copy-start.59 = (s32[4]{0:T(128)}, s32[4]{0:T(128)S(1)}, u32[]{:S(2)}) copy-start(s32[4]{0:T(128)S(1)} %fusion.21) | copy-start | bytes 52
  151.7 14.5 %copy-start.43 = (bf16[4096,128]{1,0:T(8,128)(2,1)S(1)}, bf16[4096,128]{1,0:T(8,128)(2,1)}, u32[]{:S(2)}) copy-start(bf16[4096,128]{1,0:T(8,128)(2,1)} %copy-done.42) | copy-start | bytes 3145732
  151.7 14.5 %copy-start.45 = (bf16[4096,128]{1,0:T(8,128)(2,1)S(1)}, bf16[4096,128]{1,0:T(8,128)(2,1)}, u32[]{:S(2)}) copy-start(bf16[4096,128]{1,0:T(8,128)(2,1)} %copy-done.44) | copy-start | bytes 3145732
  205.3 5.5 copy-start.4
  205.3 5.5 copy-start.41
  205.3 5.1 copy-start.47
  205.3 6.1 copy-start.48
  205.4 50.2 %collective-permute-start.3 = (bf16[1024,128]{1,0:T(8,128)(2,1)S(1)}, bf16[1024,128]{1,0:T(8,128)(2,1)S(1)}, u32[]{:S(2)}, u32[]{:S(2)}) collective-permute-start(bf16[1024,128]{1,0:T(8,128)(2,1)S(1)} %get-tuple-element.120), channel_id=1, source_target_pairs={{0,5},{1,4},{2,7},{3,6},{4,1},{5,0},{6,3},{7,2},{8,13},{9,12},{10,... | collective-permute-start | bytes 786440 | tf_op jit(solution)/shard_map/ppermute | solution.py:1515
  208.8 46.9 %collective-permute-start.2 = (bf16[1024,128]{1,0:T(8,128)(2,1)S(1)}, bf16[1024,128]{1,0:T(8,128)(2,1)S(1)}, u32[]{:S(2)}, u32[]{:S(2)}) collective-permute-start(bf16[1024,128]{1,0:T(8,128)(2,1)S(1)} %get-tuple-element.121), channel_id=1, source_target_pairs={{0,4},{1,5},{2,6},{3,7},{4,0},{5,1},{6,2},{7,3},{8,12},{9,13},{10,... | collective-permute-start | bytes 786440 | tf_op jit(solution)/shard_map/ppermute | solution.py:1515
  208.8 46.9 %collective-permute-start.1 = (bf16[1024,128]{1,0:T(8,128)(2,1)S(1)}, bf16[1024,128]{1,0:T(8,128)(2,1)S(1)}, u32[]{:S(2)}, u32[]{:S(2)}) collective-permute-start(bf16[1024,128]{1,0:T(8,128)(2,1)S(1)} %get-tuple-element.122), channel_id=1, source_target_pairs={{0,1},{1,0},{2,3},{3,2},{4,5},{5,4},{6,7},{7,6},{8,9},{9,8},{10,11... | collective-permute-start | bytes 786440 | tf_op jit(solution)/shard_map/ppermute | solution.py:1515
  211.7 42.7 %copy-start.49 = (bf16[1024,1024]{1,0:T(8,128)(2,1)}, bf16[1024,1024]{1,0:T(8,128)(2,1)S(1)}, u32[]{:S(2)}) copy-start(bf16[1024,1024]{1,0:T(8,128)(2,1)S(1)} %broadcast_select_fusion.1.cot_own_ref.cot_ref) | copy-start | bytes 6291460
  211.7 44.3 %copy-start.37 = (bf16[8,4,32,1024]{3,2,1,0:T(8,128)(2,1)S(1)}, bf16[8,4,32,1024]{3,2,1,0:T(8,128)(2,1)}, u32[]{:S(2)}) copy-start(bf16[8,4,32,1024]{3,2,1,0:T(8,128)(2,1)} %get-tuple-element.69.refs_5_.w_out_ref) | copy-start | bytes 6291460
  211.7 71.4 %collective-permute-start.7 = (bf16[1024,1024]{1,0:T(8,128)(2,1)S(1)}, bf16[1024,1024]{1,0:T(8,128)(2,1)}, u32[]{:S(2)}, u32[]{:S(2)}) collective-permute-start(bf16[1024,1024]{1,0:T(8,128)(2,1)S(1)} %broadcast_select_fusion.1.cot_own_ref.cot_ref), channel_id=1, source_target_pairs={{0,4},{1,5},{2,6},{3,7},{4,0},{5,1},{6,2},{7,3},{8,12},{9,13},{10,... | collective-permute-start | bytes 6291464 | tf_op jit(solution)/shard_map/ppermute | solution.py:1515
  214.3 41.4 %collective-permute-start.5 = (bf16[1024,1024]{1,0:T(8,128)(2,1)S(1)}, bf16[1024,1024]{1,0:T(8,128)(2,1)S(1)}, u32[]{:S(2)}, u32[]{:S(2)}) collective-permute-start(bf16[1024,1024]{1,0:T(8,128)(2,1)S(1)} %copy-done.8), channel_id=1, source_target_pairs={{2,4},{3,5},{4,2},{5,3},{10,12},{11,13},{12,10},{13,11},{18,20},{1... | collective-permute-start | bytes 6291464 | tf_op jit(solution)/shard_map/ppermute | solution.py:1507
  255.7 26.1 %copy-start.39 = (bf16[4,1024,128]{2,1,0:T(8,128)(2,1)}, bf16[4,1024,128]{2,1,0:T(8,128)(2,1)S(1)}, u32[]{:S(2)}) copy-start(bf16[4,1024,128]{2,1,0:T(8,128)(2,1)S(1)} %get-tuple-element.68.refs_4_.ctx_ref) | copy-start | bytes 3145732
  255.7 26.1 %copy-start.15 = (bf16[1024,128]{1,0:T(8,128)(2,1)}, bf16[1024,128]{1,0:T(8,128)(2,1)S(1)}, u32[]{:S(2)}) copy-start(bf16[1024,128]{1,0:T(8,128)(2,1)S(1)} %collective-permute-done.3.refs_3_.refs_4_) | copy-start | bytes 786436
  255.7 26.1 %copy-start.19 = (bf16[1024,128]{1,0:T(8,128)(2,1)}, bf16[1024,128]{1,0:T(8,128)(2,1)S(1)}, u32[]{:S(2)}) copy-start(bf16[1024,128]{1,0:T(8,128)(2,1)S(1)} %collective-permute-done.2.refs_2_.refs_3_) | copy-start | bytes 786436
  255.7 26.1 %copy-start.21 = (bf16[1024,128]{1,0:T(8,128)(2,1)}, bf16[1024,128]{1,0:T(8,128)(2,1)S(1)}, u32[]{:S(2)}) copy-start(bf16[1024,128]{1,0:T(8,128)(2,1)S(1)} %collective-permute-done.1.refs_1_.refs_2_) | copy-start | bytes 786436
  255.7 26.1 %copy-start.9 = (bf16[1024,1024]{1,0:T(8,128)(2,1)}, bf16[1024,1024]{1,0:T(8,128)(2,1)S(1)}, u32[]{:S(2)}) copy-start(bf16[1024,1024]{1,0:T(8,128)(2,1)S(1)} %collective-permute-done.5.refs_7_.refs_9_) | copy-start | bytes 6291460
  255.9 123.6 %copy-start.5 = (s32[1024,128]{1,0:T(8,128)}, s32[1024,128]{1,0:T(8,128)S(1)}, u32[]{:S(2)}) copy-start(s32[1024,128]{1,0:T(8,128)S(1)} %broadcast_in_dim.56.refs_8_.segment_ref.refs_13_) | copy-start | bytes 1572868
  283.1 87.6 %copy-start.31 = (bf16[4,1024,128]{2,1,0:T(8,128)(2,1)}, bf16[4,1024,128]{2,1,0:T(8,128)(2,1)S(1)}, u32[]{:S(2)}) copy-start(bf16[4,1024,128]{2,1,0:T(8,128)(2,1)S(1)} %get-tuple-element.89.refs_5_) | copy-start | bytes 3145732
  370.7 4.4 collective-permute-start.8
  370.8 7.4 collective-permute-start.9
  379.5 16.7 %copy-start.2 = (bf16[16,288,1024]{2,1,0:T(8,128)(2,1)S(1)}, bf16[16,288,1024]{2,1,0:T(8,128)(2,1)}, u32[]{:S(2)}) copy-start(bf16[16,288,1024]{2,1,0:T(8,128)(2,1)} %get-tuple-element.90.refs_6_) | copy-start | bytes 28311556
  379.5 16.7 %copy-start.16 = (bf16[1024,128]{1,0:T(8,128)(2,1)S(1)}, bf16[1024,128]{1,0:T(8,128)(2,1)}, u32[]{:S(2)}) copy-start(bf16[1024,128]{1,0:T(8,128)(2,1)} %copy-done.15) | copy-start | bytes 786436
  379.5 16.7 %copy-start.20 = (bf16[1024,128]{1,0:T(8,128)(2,1)S(1)}, bf16[1024,128]{1,0:T(8,128)(2,1)}, u32[]{:S(2)}) copy-start(bf16[1024,128]{1,0:T(8,128)(2,1)} %copy-done.19) | copy-start | bytes 786436
  379.5 16.7 %copy-start.22 = (bf16[1024,128]{1,0:T(8,128)(2,1)S(1)}, bf16[1024,128]{1,0:T(8,128)(2,1)}, u32[]{:S(2)}) copy-start(bf16[1024,128]{1,0:T(8,128)(2,1)} %copy-done.21) | copy-start | bytes 786436
  396.2 7.3 copy-start.11
  396.2 7.3 copy-start.13
  396.2 7.3 copy-start.17
  396.2 7.3 copy-start.23
  396.2 7.3 copy-start.25
  396.2 7.3 copy-start.27
  407.2 5.0 copy-start.18
  407.2 6.9 copy-start.14
  407.2 10.6 %copy-start.12 = (bf16[1024,128]{1,0:T(8,128)(2,1)S(1)}, bf16[1024,128]{1,0:T(8,128)(2,1)}, u32[]{:S(2)}) copy-start(bf16[1024,128]{1,0:T(8,128)(2,1)} %copy-done.11) | copy-start | bytes 786436
  407.3 190.9 %reduce-scatter.5.cloned.1.call-start = ((), (), s32[]{:S(2)}) async-start(), calls=%async_computation.2 | async-start | bytes 2949120 | tf_op jit(solution)/shard_map/reduce_scatter | solution.py:1622
  408.1 9.8 %collective-permute-start.11 = (bf16[1024,128]{1,0:T(8,128)(2,1)S(1)}, bf16[1024,128]{1,0:T(8,128)(2,1)S(1)}, u32[]{:S(2)}, u32[]{:S(2)}) collective-permute-start(bf16[1024,128]{1,0:T(8,128)(2,1)S(1)} %copy-done.28), channel_id=1, source_target_pairs={{0,1},{1,0},{2,3},{3,2},{4,5},{5,4},{6,7},{7,6},{8,9},{9,8},{10,11... | collective-permute-start | bytes 786440 | tf_op jit(solution)/shard_map/ppermute | solution.py:1515
  410.8 7.3 collective-permute-start.12
  410.8 12.3 %collective-permute-start.13 = (bf16[1024,128]{1,0:T(8,128)(2,1)S(1)}, bf16[1024,128]{1,0:T(8,128)(2,1)S(1)}, u32[]{:S(2)}, u32[]{:S(2)}) collective-permute-start(bf16[1024,128]{1,0:T(8,128)(2,1)S(1)} %copy-done.24), channel_id=1, source_target_pairs={{0,5},{1,4},{2,7},{3,6},{4,1},{5,0},{6,3},{7,2},{8,13},{9,12},{10,... | collective-permute-start | bytes 786440 | tf_op jit(solution)/shard_map/ppermute | solution.py:1515
  412.2 99.6 %collective-permute-start.17 = (bf16[1024,128]{1,0:T(8,128)(2,1)S(1)}, bf16[1024,128]{1,0:T(8,128)(2,1)S(1)}, u32[]{:S(2)}, u32[]{:S(2)}) collective-permute-start(bf16[1024,128]{1,0:T(8,128)(2,1)S(1)} %copy-done.18), channel_id=1, source_target_pairs={{0,1},{1,0},{2,3},{3,2},{4,5},{5,4},{6,7},{7,6},{8,9},{9,8},{10,11... | collective-permute-start | bytes 786440 | tf_op jit(solution)/shard_map/ppermute | solution.py:1515
  414.1 97.6 %collective-permute-start.18 = (bf16[1024,128]{1,0:T(8,128)(2,1)S(1)}, bf16[1024,128]{1,0:T(8,128)(2,1)S(1)}, u32[]{:S(2)}, u32[]{:S(2)}) collective-permute-start(bf16[1024,128]{1,0:T(8,128)(2,1)S(1)} %copy-done.14), channel_id=1, source_target_pairs={{0,4},{1,5},{2,6},{3,7},{4,0},{5,1},{6,2},{7,3},{8,12},{9,13},{10,... | collective-permute-start | bytes 786440 | tf_op jit(solution)/shard_map/ppermute | solution.py:1515
  417.9 94.4 %collective-permute-start.19 = (bf16[1024,128]{1,0:T(8,128)(2,1)S(1)}, bf16[1024,128]{1,0:T(8,128)(2,1)S(1)}, u32[]{:S(2)}, u32[]{:S(2)}) collective-permute-start(bf16[1024,128]{1,0:T(8,128)(2,1)S(1)} %copy-done.12), channel_id=1, source_target_pairs={{0,5},{1,4},{2,7},{3,6},{4,1},{5,0},{6,3},{7,2},{8,13},{9,12},{10,... | collective-permute-start | bytes 786440 | tf_op jit(solution)/shard_map/ppermute | solution.py:1515
  418.1 95.3 %collective-permute-start.10 = (bf16[2,1024,1024]{2,1,0:T(8,128)(2,1)}, bf16[2,1024,1024]{2,1,0:T(8,128)(2,1)S(1)}, u32[]{:S(2)}, u32[]{:S(2)}) collective-permute-start(bf16[2,1024,1024]{2,1,0:T(8,128)(2,1)} %get-tuple-element.78), channel_id=1, source_target_pairs={{2,4},{3,5},{4,2},{5,3},{10,12},{11,13},{12,10},{13,11},{18,20},{1... | collective-permute-start | bytes 12582920 | tf_op jit(solution)/shard_map/ppermute | solution.py:1507
  506.3 7.0 copy-start.51
  509.7 88.4 %collective-permute-start.16 = (bf16[3,1024,128]{2,1,0:T(8,128)(2,1)}, bf16[3,1024,128]{2,1,0:T(8,128)(2,1)}, u32[]{:S(2)}, u32[]{:S(2)}) collective-permute-start(bf16[3,1024,128]{2,1,0:T(8,128)(2,1)} %get-tuple-element.116), channel_id=1, source_target_pairs={{0,5},{1,4},{2,7},{3,6},{4,1},{5,0},{6,3},{7,2},{8,13},{9,12},{10,... | collective-permute-start | bytes 2359304 | tf_op jit(solution)/shard_map/ppermute | solution.py:1515
  511.8 86.4 %collective-permute-start.15 = (bf16[3,1024,128]{2,1,0:T(8,128)(2,1)S(1)}, bf16[3,1024,128]{2,1,0:T(8,128)(2,1)}, u32[]{:S(2)}, u32[]{:S(2)}) collective-permute-start(bf16[3,1024,128]{2,1,0:T(8,128)(2,1)S(1)} %get-tuple-element.117), channel_id=1, source_target_pairs={{0,4},{1,5},{2,6},{3,7},{4,0},{5,1},{6,2},{7,3},{8,12},{9,13},{10,... | collective-permute-start | bytes 2359304 | tf_op jit(solution)/shard_map/ppermute | solution.py:1515
  511.8 86.4 %collective-permute-start.14 = (bf16[3,1024,128]{2,1,0:T(8,128)(2,1)S(1)}, bf16[3,1024,128]{2,1,0:T(8,128)(2,1)}, u32[]{:S(2)}, u32[]{:S(2)}) collective-permute-start(bf16[3,1024,128]{2,1,0:T(8,128)(2,1)S(1)} %get-tuple-element.118), channel_id=1, source_target_pairs={{0,1},{1,0},{2,3},{3,2},{4,5},{5,4},{6,7},{7,6},{8,9},{9,8},{10,11... | collective-permute-start | bytes 2359304 | tf_op jit(solution)/shard_map/ppermute | solution.py:1515
  598.2 102.5 %copy-start.56 = (f32[4,256]{1,0:T(4,128)S(1)}, f32[4,256]{1,0:T(4,128)}, u32[]{:S(2)}) copy-start(f32[4,256]{1,0:T(4,128)} %convert_multiply_fusion) | copy-start | bytes 12292
  702.1 106.6 %copy-start.65 = (bf16[1024,1024]{1,0:T(8,128)(2,1)S(1)}, bf16[1024,1024]{1,0:T(8,128)(2,1)}, u32[]{:S(2)}) copy-start(bf16[1024,1024]{1,0:T(8,128)(2,1)} %get-tuple-element.95.grad_ref) | copy-start | bytes 6291460
  808.8 4.4 copy-start.66
  820.3 6.9 slice-start
  820.3 6.8 slice-start.1
  828.9 9.6 %copy-start.1 = (bf16[1024,1024]{1,0:T(8,128)(2,1)S(1)}, bf16[1024,1024]{1,0:T(8,128)(2,1)}, u32[]{:S(2)}) copy-start(bf16[1024,1024]{1,0:T(8,128)(2,1)} %param.21) | copy-start | bytes 6291460
  (29 other events, 71.1 us)
Sparse Core Ops, SparseCore 0:
  11.0 76.3 all-gather.4
  146.0 87.4 all-gather.6
  407.4 95.8 reduce-scatter.6
  516.6 67.5 reduce-scatter.4

commit v5 on v4

--- a/solution.py
+++ b/solution.py
@@ -634,7 +634,7 @@
     for b in range(parts):
         part = lax.dot_general(low, w_out_ref[:, own ^ b].reshape(pairs * LANES, -1), NT, preferred_element_type=F32).astype(BF)
         for pair in range(pairs):
-            grad_context_refs[pair * parts + b][...] = part[:, pair * LANES : (pair + 1) * LANES]
+            grad_context_refs[b][pair] = part[:, pair * LANES : (pair + 1) * LANES]
     sums = jnp.concatenate([collect(segment, grad, utt), collect(segment, grad * unit, utt)], axis=0)
 
     @pl.when(pl.program_id(0) == 0)
@@ -663,7 +663,7 @@
             + [thin, pl.BlockSpec(scale.shape, lambda i, *_: (0, 0)), pl.BlockSpec(w_out.shape, lambda i, *_: (0, 0, 0, 0))],
             out_specs=[wide] * 2
             + [pl.BlockSpec((2, rows, depth), lambda i, *_: (0, i, 0)), pl.BlockSpec((2 * utt, depth), lambda i, *_: (0, 0))]
-            + [thin] * (pairs * parts),
+            + [pl.BlockSpec((pairs, rows, LANES), lambda i, *_: (0, i, 0))] * parts,
         ),
         out_shape=[
             shape((frames, depth), F32),
@@ -671,7 +671,7 @@
             shape((2, frames, depth), BF),
             shape((2 * utt, depth), F32),
         ]
-        + [shape((frames, LANES), BF)] * (pairs * parts),
+        + [shape((pairs, frames, LANES), BF)] * parts,
         compiler_params=pltpu.CompilerParams(
             dimension_semantics=("arbitrary",), vmem_limit_bytes=48 * MIB
         ),
@@ -1621,9 +1621,10 @@
     feed_sum = lax.psum_scatter(grad_feed, "dp", scatter_dimension=0, axis_index_groups=same_core)
     feed_shard = lax.psum_scatter(feed_sum, "tensor", scatter_dimension=0)
 
+    grad_parts = exchange(grad_context)
     grad_mine = []
     for pair in range(pairs):
-        grad = jnp.stack(exchange(grad_context[pair * parts : (pair + 1) * parts]))
+        grad = jnp.stack([block[pair] for block in grad_parts])
         if pair == pairs - 1 and pairs > 1:
             grad = after(grad, feed_sum)
         grads = attend_back(

time: 856 us -> 879 us (1.027)
  waiting for transfers between devices: 14.8 us -> 45.1 us
    ppermute x17 -> x14, waiting for transfers between devices: 14.7 us -> 45 us  [partner(): return lax.ppermute(value, both, pattern)]
    pallas_call x2, Pallas kernels: 164 us -> 151 us  [attend_back(): pl.pallas_call(functools.partial(attend_back_kernel, bq=bq, bk=bk, utt=ut...]
    pallas_call x1, Pallas kernels: 102 us -> 114 us  [finish(): pl.pallas_call(functools.partial(finish_kernel, pairs=pairs, parts=parts,...]
    unnamed x139 -> x127, local copies, waits for them, and re-layouts: 19.9 us -> 18.7 us
  transfers between devices with their start and end apart: 24 -> 21, of which waited for: 4 -> 4; matrix products, arithmetic and copies ran while one was open for 2% -> 2% of each run, Pallas kernels for 48% -> 45%
where the time goes in v5:
time: 879 us; the launch traced here: 869 us
  Pallas kernels  727 us (83%)
  waiting for transfers between devices  45.1 us (5%)
  local copies, waits for them, and re-layouts  38.9 us (4%)
  starting transfers between devices  17.6 us (2%)
  between operations  15.1 us (2%)
  matrix products  14.4 us (2%)
  other arithmetic  11.7 us (1%)
    pallas_call x2, Pallas kernels, attend_back(): pl.pallas_call(functools.partial(attend_back_kernel, bq=bq, bk=bk, utt=ut...  151 us
    pallas_call x1, Pallas kernels, front(): pl.pallas_call(functools.partial(front_kernel, parts=parts, utt=utt), in_...  128 us
    pallas_call x1, Pallas kernels, finish(): pl.pallas_call(functools.partial(finish_kernel, pairs=pairs, parts=parts,...  114 us
    pallas_call x1, Pallas kernels, sums(): pl.pallas_call(functools.partial(sums_kernel, rows_all=rows_all, parts=pa...  104 us
    pallas_call x1, Pallas kernels, feed(): pl.pallas_call(functools.partial(feed_kernel, parts=parts), grid=(groups...  87.9 us
    pallas_call x2, Pallas kernels, attend(): pl.pallas_call(functools.partial(attend_kernel, bq=bq, bk=bk, per_part=pe...  78.1 us
    ppermute x14, waiting for transfers between devices, partner(): return lax.ppermute(value, both, pattern)  45 us
    pallas_call x1, Pallas kernels, join(): pl.pallas_call(functools.partial(join_kernel, pairs=pairs, parts=parts),...  25.6 us
  transfers between devices with their start and end apart: 21, of which 4 were waited for; matrix products, arithmetic and copies ran while one was open for 2% of the time, Pallas kernels for 45%

profile of v5, /device:TPU:0, one launch (start us, length us, event | category | flops | bytes accessed | tf_op | source)
XLA Modules:
  0.0 869.4 jit_solution(6252462694498551614)
XLA Ops:
  7.2 0.5 collective-permute-start.6
  7.8 0.9 copy-done
  9.0 1.0 constant_dynamic-slice_fusion
  10.0 0.8 pad_maximum_fusion.2
  11.3 2.8 copy.56
  14.5 0.2 fusion.1
  15.0 127.7 %front.1 = (bf16[1024,1024]{1,0:T(8,128)(2,1)}, bf16[4,1024,1024]{2,1,0:T(8,128)(2,1)}, f32[4096,128]{1,0:T(8,128)}, f32[4096,128]{1,0:T(8,128)}, bf16[4096,128]...) custom-call(s32[4]{0:T(128)S(1)} %bitcast.84, ...), custom_call_target="tpu_custom_call" | custom-call | flops 82500001792 | tf_op jit(solution)/shard_map/front/pallas_call | solution.py:1445
  142.7 1.1 copy-done.29
  143.9 1.0 copy-done.36
  144.8 1.0 copy-done.38
  146.0 2.1 collective-permute-start.4
  148.3 0.2 select_reduce_fusion.2
  148.7 0.4 copy-done.53
  149.1 1.6 copy-done.28
  150.7 1.4 copy-done.30
  152.1 12.0 %project.1.q_ref.k_ref.v_ref = bf16[6,4096,128]{2,1,0:T(8,128)(2,1)S(1)} custom-call(bf16[4096,1024]{1,0:T(8,128)(2,1)} %bitcast.115, bf16[768,1024]{1,0:T(8,128)(2,1)S(1)} %copy-done.30, f32[4096,128]{1,0:T(8,128)S(1)} %copy-done.27, f32[4096,128]{1,0:T(8,128)S(1)} %copy-done.28), custom_call_target="tpu_custom_call" | custom-call | flops 12099999744 | tf_op jit(solution)/shard_map/project/pallas_call | solution.py:105
  164.1 2.6 copy-done.24
  166.7 39.0 %attend.2 = (bf16[4,1024,128]{2,1,0:T(8,128)(2,1)S(1)}, f32[4096,128]{1,0:T(8,128)S(1)}) custom-call(s32[2]{0:T(128)S(1)} %pad_add_fusion.own_ref, s32[4]{0:T(128)S(1)} %get-tuple-element.144.low_ref, s32[4]{0:T(128)S(1)} %get-tuple-element.143.high_ref, bf16[6,4096,128]{2,1,0:T(8,128)(2,1)} %copy-done.24, bf16[6,4096,128]{2,1,0:T(8,128)(2,1)} %copy-done.24, ...), custom_call_target="tpu_custom_call" | custom-call | flops 38499999744 | tf_op jit(solution)/shard_map/attend/pallas_call | solution.py:181
  205.8 3.2 collective-permute-start.3
  209.1 1.6 collective-permute-start.1
  210.7 0.4 fusion.26
  211.1 0.6 fusion.35
  211.7 0.2 broadcast_select_fusion.1.cot_own_ref.cot_ref
  212.0 2.6 collective-permute-start.7
  214.6 1.0 collective-permute-start.5
  215.6 39.0 %attend.3 = (bf16[4,1024,128]{2,1,0:T(8,128)(2,1)S(1)}, f32[4096,128]{1,0:T(8,128)S(1)}) custom-call(s32[2]{0:T(128)S(1)} %pad_add_fusion.own_ref, s32[4]{0:T(128)S(1)} %get-tuple-element.144.low_ref, s32[4]{0:T(128)S(1)} %get-tuple-element.143.high_ref, bf16[6,4096,128]{2,1,0:T(8,128)(2,1)} %copy-done.24, bf16[6,4096,128]{2,1,0:T(8,128)(2,1)} %copy-done.24, ...), custom_call_target="tpu_custom_call" | custom-call | flops 38499999744 | tf_op jit(solution)/shard_map/attend/pallas_call | solution.py:181
  254.7 1.3 copy-done.34
  256.3 25.6 %join.1 = (f32[1024,1024]{1,0:T(8,128)}, bf16[1024,1024]{1,0:T(8,128)(2,1)S(1)}, bf16[4,1024,128]{2,1,0:T(8,128)(2,1)S(1)}) custom-call(bf16[1024,128]{1,0:T(8,128)(2,1)S(1)} %get-tuple-element.115.refs_0_.refs_1_, bf16[1024,128]{1,0:T(8,128)(2,1)S(1)} %collective-permute-done.1.refs_1_.refs_2_, ...), custom_call_target="tpu_custom_call" | custom-call | flops 19800000512 | tf_op jit(solution)/shard_map/join/pallas_call | solution.py:594
  281.9 1.3 copy-done.32
  283.3 87.9 %feed.1 = (f32[1024,1024]{1,0:T(8,128)}, bf16[1024,1024]{1,0:T(8,128)(2,1)}, f32[1024,1024]{1,0:T(8,128)}, bf16[1024,1024]{1,0:T(8,128)(2,1)}, bf16[16,288,1024]...) custom-call(bf16[1024,1024]{1,0:T(8,128)(2,1)} %copy-done.32, bf16[1024,1024]{1,0:T(8,128)(2,1)} %copy-done.43, ...), custom_call_target="tpu_custom_call" | custom-call | flops 92400001024 | tf_op jit(solution)/shard_map/feed/pallas_call | solution.py:456
  371.2 0.5 collective-permute-start.9
  371.7 3.9 collective-permute-done.8.gin_in_ref
  375.6 3.0 collective-permute-done.9.out_in_ref
  378.6 1.3 copy-done.58
  379.9 16.7 %turn.1 = (f32[1024,1024]{1,0:T(8,128)}, bf16[1024,1024]{1,0:T(8,128)(2,1)S(1)}, bf16[2,1024,1024]{2,1,0:T(8,128)(2,1)}, f32[8,1024]{1,0:T(8,128)S(1)}, bf16[2,1...) custom-call(s32[2]{0:T(128)S(1)} %pad_add_fusion.own_ref, ...), custom_call_target="tpu_custom_call" | custom-call | flops 16499999744 | tf_op jit(solution)/shard_map/turn/pallas_call | solution.py:657
  396.7 5.5 out_grad.1
  402.2 3.7 copy-done.3
  406.0 0.5 copy-done.7
  406.9 2.6 collective-permute-start.11
  409.5 0.5 and_select_fusion
  410.1 0.6 convert_multiply_fusion
  410.8 0.9 collective-permute-start.10
  411.8 27.9 %collective-permute-done.11 = bf16[2,1024,128]{2,1,0:T(8,128)(2,1)S(1)} collective-permute-done((bf16[2,1024,128]{2,1,0:T(8,128)(2,1)S(1)}, bf16[2,1024,128]{2,1,0:T(8,128)(2,1)S(1)}, u32[]{:S(2)}, u32[]{:S(2)}) %collective-permute-start.11) | collective-permute-done | bytes 524320 | tf_op jit(solution)/shard_map/ppermute | solution.py:1515
  439.8 10.2 %collective-permute-done.13 = bf16[2,1024,128]{2,1,0:T(8,128)(2,1)S(1)} collective-permute-done((bf16[2,1024,128]{2,1,0:T(8,128)(2,1)S(1)}, bf16[2,1024,128]{2,1,0:T(8,128)(2,1)S(1)}, u32[]{:S(2)}, u32[]{:S(2)}) %collective-permute-start.13) | collective-permute-done | bytes 524320 | tf_op jit(solution)/shard_map/ppermute | solution.py:1515
  450.0 1.1 pad_maximum_fusion.do_ref
  451.1 75.6 %attend_back.2.refs_4_ = bf16[4,3,1024,128]{3,2,1,0:T(8,128)(2,1)} custom-call(s32[2]{0:T(128)} %copy-done.23, s32[8]{0:T(128)} %get-tuple-element.142.low_ref, s32[8]{0:T(128)} %get-tuple-element.141.high_ref, bf16[6,4096,128]{2,1,0:T(8,128)(2,1)} %copy-done.24, bf16[6,4096,128]{2,1,0:T(8,128)(2,1)} %copy-done.24, bf16[6,4096,128]{2,1,0:T(8,128)(2,1)} %copy-done.24, ...), custom_call_target="tpu_custom_call" | custom-call | flops 72600002560 | tf_op jit(solution)/shard_map/attend_back/pallas_call | solution.py:310
  526.7 3.4 slice_bitcast_fusion.1
  530.1 0.5 collective-permute-start.15
  530.6 1.6 collective-permute-start.14
  532.2 1.1 pad_maximum_fusion.1.do_ref
  533.3 3.1 slice_bitcast_fusion
  536.5 75.1 %attend_back.3.refs_5_ = bf16[4,3,1024,128]{3,2,1,0:T(8,128)(2,1)} custom-call(s32[2]{0:T(128)} %copy-done.23, s32[8]{0:T(128)} %get-tuple-element.142.low_ref, s32[8]{0:T(128)} %get-tuple-element.141.high_ref, bf16[6,4096,128]{2,1,0:T(8,128)(2,1)} %copy-done.24, bf16[6,4096,128]{2,1,0:T(8,128)(2,1)} %copy-done.24, bf16[6,4096,128]{2,1,0:T(8,128)(2,1)} %copy-done.24, ...), custom_call_target="tpu_custom_call" | custom-call | flops 72600002560 | tf_op jit(solution)/shard_map/attend_back/pallas_call | solution.py:310
  611.6 114.2 %finish.1 = (bf16[1024,1024]{1,0:T(8,128)(2,1)}, bf16[768,1024]{1,0:T(8,128)(2,1)}, f32[8,1024]{1,0:T(8,128)}, bf16[8,288,1024]{2,1,0:T(8,128)(2,1)}, bf16[1024,1024]{1,0:T(8,128)(2,1)}) custom-call(bf16[3,1024,128]{2,1,0:T(8,128)(2,1)} %get-tuple-element.111.refs_0_, bf16[3,1024,128]{2,1,0:T(8,128)(2,1)} %collective-permute-done.14.refs_1_, ...), custom_call_target="tpu_custom_call" | custom-call | flops 65999998976 | tf_op jit(solution)/shard_map/finish/pallas_call | solution.py:1068
  725.9 1.4 select_maximum_fusion.sums_ref
  727.3 103.7 %sums.1 = (bf16[2048,1024]{1,0:T(8,128)(2,1)}, f32[8,20,1024]{2,1,0:T(8,128)}, bf16[1024,1024]{1,0:T(8,128)(2,1)}) custom-call(bf16[1024,1024]{1,0:T(8,128)(2,1)} %bitcast.110, bf16[1024,1024]{1,0:T(8,128)(2,1)} %get-tuple-element.88.inputs_in_hbm, bf16[1024,1024]{1,0:T(8,128)(2,1)} %bitcast.113, bf16[1024,1024]{1,0:T(8,128)(2,1)} %get-tuple-element.106.skips_in_hbm, ...), custom_call_target="tpu_custom_call" | custom-call | flops 109999996928 | tf_op jit(solution)/shard_map/sums/pallas_call | solution.py:1205
  831.0 1.7 copy.59
  832.8 4.4 convolution_bitcast_fusion
  837.2 4.4 convolution_bitcast_fusion.1
  841.6 2.1 copy.65
  844.3 6.8 fusion.29
  851.1 0.5 copy.70
  851.7 1.1 bitcast_convert_fusion
  852.8 4.6 spread_out.1
  857.4 5.0 fusion.3
  (195 shorter events, 4.1 us)
Async XLA Ops:
  7.2 3.8 copy-start.51
  7.2 138.6 %all-gather.5.cloned.1.call-start = ((), (), s32[]{:S(2)}) async-start(), calls=%async_computation.3 | async-start | bytes 2621440 | tf_op jit(solution)/shard_map/all_gather | solution.py:1568
  7.2 7.1 collective-permute-start.6
  7.8 6.4 collective-permute-start
  10.8 3.7 copy-start.40
  10.8 272.4 %all-gather.7.cloned.1.call-start = ((), (), s32[]{:S(2)}) async-start(), calls=%async_computation.4 | async-start | bytes 10485760 | tf_op jit(solution)/shard_map/all_gather | solution.py:1569
  11.3 3.7 copy-start.10
  14.3 196.3 %copy-start.6 = (s32[4,1]{0,1:T(1,128)}, s32[4,1]{0,1:T(1,128)S(1)}, u32[]{:S(2)}) copy-start(s32[4,1]{0,1:T(1,128)S(1)} %reduce-window.13) | copy-start | bytes 52
  14.5 196.2 %copy-start.46 = (f32[4,128]{1,0:T(4,128)}, f32[4,128]{1,0:T(4,128)S(1)}, u32[]{:S(2)}) copy-start(f32[4,128]{1,0:T(4,128)S(1)} %get-tuple-element.133) | copy-start | bytes 6148
  14.5 196.2 %copy-start.48 = (f32[4,128]{1,0:T(4,128)}, f32[4,128]{1,0:T(4,128)S(1)}, u32[]{:S(2)}) copy-start(f32[4,128]{1,0:T(4,128)S(1)} %get-tuple-element.134) | copy-start | bytes 6148
  145.8 390.6 %reduce-scatter.7.cloned.1.call-start = ((), (), s32[]{:S(2)}) async-start(), calls=%async_computation.5 | async-start | bytes 11796480
  146.0 233.9 %copy-start.23 = (s32[2]{0:T(128)}, s32[2]{0:T(128)S(1)}, u32[]{:S(2)}) copy-start(s32[2]{0:T(128)S(1)} %pad_add_fusion.own_ref) | copy-start | bytes 28
  146.0 65.8 %collective-permute-start.4 = (bf16[1024,1024]{1,0:T(8,128)(2,1)}, bf16[1024,1024]{1,0:T(8,128)(2,1)}, u32[]{:S(2)}, u32[]{:S(2)}) collective-permute-start(bf16[1024,1024]{1,0:T(8,128)(2,1)} %bitcast.97), channel_id=1, source_target_pairs={{2,4},{3,5},{4,2},{5,3},{10,12},{11,13},{12,10},{13,11},{18,20},{1... | collective-permute-start | bytes 6291464 | tf_op jit(solution)/shard_map/ppermute | solution.py:1507
  152.1 14.6 %copy-start.37 = (bf16[4096,128]{1,0:T(8,128)(2,1)S(1)}, bf16[4096,128]{1,0:T(8,128)(2,1)}, u32[]{:S(2)}) copy-start(bf16[4096,128]{1,0:T(8,128)(2,1)} %copy-done.36) | copy-start | bytes 3145732
  152.1 14.6 %copy-start.39 = (bf16[4096,128]{1,0:T(8,128)(2,1)S(1)}, bf16[4096,128]{1,0:T(8,128)(2,1)}, u32[]{:S(2)}) copy-start(bf16[4096,128]{1,0:T(8,128)(2,1)} %copy-done.38) | copy-start | bytes 3145732
  205.7 5.4 copy-start.4
  205.7 5.4 copy-start.35
  205.7 5.0 copy-start.41
  205.7 6.0 copy-start.42
  205.8 50.2 %collective-permute-start.3 = (bf16[1024,128]{1,0:T(8,128)(2,1)S(1)}, bf16[1024,128]{1,0:T(8,128)(2,1)S(1)}, u32[]{:S(2)}, u32[]{:S(2)}) collective-permute-start(bf16[1024,128]{1,0:T(8,128)(2,1)S(1)} %get-tuple-element.112), channel_id=1, source_target_pairs={{0,5},{1,4},{2,7},{3,6},{4,1},{5,0},{6,3},{7,2},{8,13},{9,12},{10,... | collective-permute-start | bytes 786440 | tf_op jit(solution)/shard_map/ppermute | solution.py:1515
  209.0 47.0 %collective-permute-start.2 = (bf16[1024,128]{1,0:T(8,128)(2,1)S(1)}, bf16[1024,128]{1,0:T(8,128)(2,1)S(1)}, u32[]{:S(2)}, u32[]{:S(2)}) collective-permute-start(bf16[1024,128]{1,0:T(8,128)(2,1)S(1)} %get-tuple-element.113), channel_id=1, source_target_pairs={{0,4},{1,5},{2,6},{3,7},{4,0},{5,1},{6,2},{7,3},{8,12},{9,13},{10,... | collective-permute-start | bytes 786440 | tf_op jit(solution)/shard_map/ppermute | solution.py:1515
  209.1 46.9 %collective-permute-start.1 = (bf16[1024,128]{1,0:T(8,128)(2,1)S(1)}, bf16[1024,128]{1,0:T(8,128)(2,1)S(1)}, u32[]{:S(2)}, u32[]{:S(2)}) collective-permute-start(bf16[1024,128]{1,0:T(8,128)(2,1)S(1)} %get-tuple-element.114), channel_id=1, source_target_pairs={{0,1},{1,0},{2,3},{3,2},{4,5},{5,4},{6,7},{7,6},{8,9},{9,8},{10,11... | collective-permute-start | bytes 786440 | tf_op jit(solution)/shard_map/ppermute | solution.py:1515
  212.0 42.7 %copy-start.43 = (bf16[1024,1024]{1,0:T(8,128)(2,1)}, bf16[1024,1024]{1,0:T(8,128)(2,1)S(1)}, u32[]{:S(2)}) copy-start(bf16[1024,1024]{1,0:T(8,128)(2,1)S(1)} %broadcast_select_fusion.1.cot_own_ref.cot_ref) | copy-start | bytes 6291460
  212.0 44.3 %copy-start.31 = (bf16[8,4,32,1024]{3,2,1,0:T(8,128)(2,1)S(1)}, bf16[8,4,32,1024]{3,2,1,0:T(8,128)(2,1)}, u32[]{:S(2)}) copy-start(bf16[8,4,32,1024]{3,2,1,0:T(8,128)(2,1)} %get-tuple-element.65.refs_5_.w_out_ref) | copy-start | bytes 6291460
  212.0 71.3 %collective-permute-start.7 = (bf16[1024,1024]{1,0:T(8,128)(2,1)S(1)}, bf16[1024,1024]{1,0:T(8,128)(2,1)}, u32[]{:S(2)}, u32[]{:S(2)}) collective-permute-start(bf16[1024,1024]{1,0:T(8,128)(2,1)S(1)} %broadcast_select_fusion.1.cot_own_ref.cot_ref), channel_id=1, source_target_pairs={{0,4},{1,5},{2,6},{3,7},{4,0},{5,1},{6,2},{7,3},{8,12},{9,13},{10,... | collective-permute-start | bytes 6291464 | tf_op jit(solution)/shard_map/ppermute | solution.py:1515
  214.6 41.4 %collective-permute-start.5 = (bf16[1024,1024]{1,0:T(8,128)(2,1)S(1)}, bf16[1024,1024]{1,0:T(8,128)(2,1)S(1)}, u32[]{:S(2)}, u32[]{:S(2)}) collective-permute-start(bf16[1024,1024]{1,0:T(8,128)(2,1)S(1)} %copy-done.8), channel_id=1, source_target_pairs={{2,4},{3,5},{4,2},{5,3},{10,12},{11,13},{12,10},{13,11},{18,20},{1... | collective-permute-start | bytes 6291464 | tf_op jit(solution)/shard_map/ppermute | solution.py:1507
  256.0 25.9 %copy-start.33 = (bf16[4,1024,128]{2,1,0:T(8,128)(2,1)}, bf16[4,1024,128]{2,1,0:T(8,128)(2,1)S(1)}, u32[]{:S(2)}) copy-start(bf16[4,1024,128]{2,1,0:T(8,128)(2,1)S(1)} %get-tuple-element.64.refs_4_.ctx_ref) | copy-start | bytes 3145732
  256.0 25.9 %copy-start.17 = (bf16[1024,128]{1,0:T(8,128)(2,1)}, bf16[1024,128]{1,0:T(8,128)(2,1)S(1)}, u32[]{:S(2)}) copy-start(bf16[1024,128]{1,0:T(8,128)(2,1)S(1)} %collective-permute-done.3.refs_3_.refs_4_) | copy-start | bytes 786436
  256.0 25.9 %copy-start.19 = (bf16[1024,128]{1,0:T(8,128)(2,1)}, bf16[1024,128]{1,0:T(8,128)(2,1)S(1)}, u32[]{:S(2)}) copy-start(bf16[1024,128]{1,0:T(8,128)(2,1)S(1)} %collective-permute-done.2.refs_2_.refs_3_) | copy-start | bytes 786436
  256.0 25.9 %copy-start.21 = (bf16[1024,128]{1,0:T(8,128)(2,1)}, bf16[1024,128]{1,0:T(8,128)(2,1)S(1)}, u32[]{:S(2)}) copy-start(bf16[1024,128]{1,0:T(8,128)(2,1)S(1)} %collective-permute-done.1.refs_1_.refs_2_) | copy-start | bytes 786436
  256.0 25.9 %copy-start.9 = (bf16[1024,1024]{1,0:T(8,128)(2,1)}, bf16[1024,1024]{1,0:T(8,128)(2,1)S(1)}, u32[]{:S(2)}) copy-start(bf16[1024,1024]{1,0:T(8,128)(2,1)S(1)} %collective-permute-done.5.refs_7_.refs_9_) | copy-start | bytes 6291460
  256.2 123.7 %copy-start.5 = (s32[1024,128]{1,0:T(8,128)}, s32[1024,128]{1,0:T(8,128)S(1)}, u32[]{:S(2)}) copy-start(s32[1024,128]{1,0:T(8,128)S(1)} %broadcast_in_dim.56.refs_8_.segment_ref.refs_13_) | copy-start | bytes 1572868
  283.2 87.9 %copy-start.25 = (bf16[4,1024,128]{2,1,0:T(8,128)(2,1)}, bf16[4,1024,128]{2,1,0:T(8,128)(2,1)S(1)}, u32[]{:S(2)}) copy-start(bf16[4,1024,128]{2,1,0:T(8,128)(2,1)S(1)} %get-tuple-element.81.refs_5_) | copy-start | bytes 3145732
  371.1 4.4 collective-permute-start.8
  371.2 7.4 collective-permute-start.9
  379.9 16.7 %copy-start.2 = (bf16[16,288,1024]{2,1,0:T(8,128)(2,1)S(1)}, bf16[16,288,1024]{2,1,0:T(8,128)(2,1)}, u32[]{:S(2)}) copy-start(bf16[16,288,1024]{2,1,0:T(8,128)(2,1)} %get-tuple-element.82.refs_6_) | copy-start | bytes 28311556
  379.9 16.7 %copy-start.18 = (bf16[1024,128]{1,0:T(8,128)(2,1)S(1)}, bf16[1024,128]{1,0:T(8,128)(2,1)}, u32[]{:S(2)}) copy-start(bf16[1024,128]{1,0:T(8,128)(2,1)} %copy-done.17) | copy-start | bytes 786436
  379.9 16.7 %copy-start.20 = (bf16[1024,128]{1,0:T(8,128)(2,1)S(1)}, bf16[1024,128]{1,0:T(8,128)(2,1)}, u32[]{:S(2)}) copy-start(bf16[1024,128]{1,0:T(8,128)(2,1)} %copy-done.19) | copy-start | bytes 786436
  379.9 16.7 %copy-start.22 = (bf16[1024,128]{1,0:T(8,128)(2,1)S(1)}, bf16[1024,128]{1,0:T(8,128)(2,1)}, u32[]{:S(2)}) copy-start(bf16[1024,128]{1,0:T(8,128)(2,1)} %copy-done.21) | copy-start | bytes 786436
  379.9 16.7 %copy-start.26 = (bf16[4,1024,128]{2,1,0:T(8,128)(2,1)S(1)}, bf16[4,1024,128]{2,1,0:T(8,128)(2,1)}, u32[]{:S(2)}) copy-start(bf16[4,1024,128]{2,1,0:T(8,128)(2,1)} %copy-done.25) | copy-start | bytes 3145732
  396.6 5.6 copy-start.11
  396.6 5.6 copy-start.13
  396.6 5.6 copy-start.15
  405.9 4.2 copy-start.14
  405.9 4.2 copy-start.47
  405.9 4.2 copy-start.49
  405.9 4.8 copy-start.12
  405.9 205.7 %reduce-scatter.5.cloned.1.call-start = ((), (), s32[]{:S(2)}) async-start(), calls=%async_computation.2 | async-start | bytes 2949120 | tf_op jit(solution)/shard_map/reduce_scatter | solution.py:1622
  406.9 32.8 %collective-permute-start.11 = (bf16[2,1024,128]{2,1,0:T(8,128)(2,1)S(1)}, bf16[2,1024,128]{2,1,0:T(8,128)(2,1)S(1)}, u32[]{:S(2)}, u32[]{:S(2)}) collective-permute-start(bf16[2,1024,128]{2,1,0:T(8,128)(2,1)S(1)} %copy-done.16), channel_id=1, source_target_pairs={{0,1},{1,0},{2,3},{3,2},{4,5},{5,4},{6,7},{7,6},{8,9},{9,8},{10,11... | collective-permute-start | bytes 1572872 | tf_op jit(solution)/shard_map/ppermute | solution.py:1515
  410.0 29.7 %collective-permute-start.12 = (bf16[2,1024,128]{2,1,0:T(8,128)(2,1)S(1)}, bf16[2,1024,128]{2,1,0:T(8,128)(2,1)S(1)}, u32[]{:S(2)}, u32[]{:S(2)}) collective-permute-start(bf16[2,1024,128]{2,1,0:T(8,128)(2,1)S(1)} %copy-done.14), channel_id=1, source_target_pairs={{0,4},{1,5},{2,6},{3,7},{4,0},{5,1},{6,2},{7,3},{8,12},{9,13},{10,... | collective-permute-start | bytes 1572872 | tf_op jit(solution)/shard_map/ppermute | solution.py:1515
  410.7 39.3 %collective-permute-start.13 = (bf16[2,1024,128]{2,1,0:T(8,128)(2,1)S(1)}, bf16[2,1024,128]{2,1,0:T(8,128)(2,1)S(1)}, u32[]{:S(2)}, u32[]{:S(2)}) collective-permute-start(bf16[2,1024,128]{2,1,0:T(8,128)(2,1)S(1)} %copy-done.12), channel_id=1, source_target_pairs={{0,5},{1,4},{2,7},{3,6},{4,1},{5,0},{6,3},{7,2},{8,13},{9,12},{10,... | collective-permute-start | bytes 1572872 | tf_op jit(solution)/shard_map/ppermute | solution.py:1515
  410.8 122.5 %collective-permute-start.10 = (bf16[2,1024,1024]{2,1,0:T(8,128)(2,1)}, bf16[2,1024,1024]{2,1,0:T(8,128)(2,1)S(1)}, u32[]{:S(2)}, u32[]{:S(2)}) collective-permute-start(bf16[2,1024,1024]{2,1,0:T(8,128)(2,1)} %get-tuple-element.74), channel_id=1, source_target_pairs={{2,4},{3,5},{4,2},{5,3},{10,12},{11,13},{12,10},{13,11},{18,20},{1... | collective-permute-start | bytes 12582920 | tf_op jit(solution)/shard_map/ppermute | solution.py:1507
  526.7 6.6 copy-start.45
  530.1 81.5 %collective-permute-start.16 = (bf16[3,1024,128]{2,1,0:T(8,128)(2,1)}, bf16[3,1024,128]{2,1,0:T(8,128)(2,1)}, u32[]{:S(2)}, u32[]{:S(2)}) collective-permute-start(bf16[3,1024,128]{2,1,0:T(8,128)(2,1)} %get-tuple-element.108), channel_id=1, source_target_pairs={{0,5},{1,4},{2,7},{3,6},{4,1},{5,0},{6,3},{7,2},{8,13},{9,12},{10,... | collective-permute-start | bytes 2359304 | tf_op jit(solution)/shard_map/ppermute | solution.py:1515
  530.1 81.5 %collective-permute-start.15 = (bf16[3,1024,128]{2,1,0:T(8,128)(2,1)S(1)}, bf16[3,1024,128]{2,1,0:T(8,128)(2,1)}, u32[]{:S(2)}, u32[]{:S(2)}) collective-permute-start(bf16[3,1024,128]{2,1,0:T(8,128)(2,1)S(1)} %get-tuple-element.109), channel_id=1, source_target_pairs={{0,4},{1,5},{2,6},{3,7},{4,0},{5,1},{6,2},{7,3},{8,12},{9,13},{10,... | collective-permute-start | bytes 2359304 | tf_op jit(solution)/shard_map/ppermute | solution.py:1515
  530.6 81.0 %collective-permute-start.14 = (bf16[3,1024,128]{2,1,0:T(8,128)(2,1)S(1)}, bf16[3,1024,128]{2,1,0:T(8,128)(2,1)}, u32[]{:S(2)}, u32[]{:S(2)}) collective-permute-start(bf16[3,1024,128]{2,1,0:T(8,128)(2,1)S(1)} %get-tuple-element.110), channel_id=1, source_target_pairs={{0,1},{1,0},{2,3},{3,2},{4,5},{5,4},{6,7},{7,6},{8,9},{9,8},{10,11... | collective-permute-start | bytes 2359304 | tf_op jit(solution)/shard_map/ppermute | solution.py:1515
  611.6 114.2 %copy-start.50 = (f32[4,256]{1,0:T(4,128)S(1)}, f32[4,256]{1,0:T(4,128)}, u32[]{:S(2)}) copy-start(f32[4,256]{1,0:T(4,128)} %convert_multiply_fusion) | copy-start | bytes 12292
  727.3 105.5 %copy-start.59 = (bf16[1024,1024]{1,0:T(8,128)(2,1)S(1)}, bf16[1024,1024]{1,0:T(8,128)(2,1)}, u32[]{:S(2)}) copy-start(bf16[1024,1024]{1,0:T(8,128)(2,1)} %get-tuple-element.87.grad_ref) | copy-start | bytes 6291460
  832.8 4.4 copy-start.56
  832.8 4.4 copy-start.60
  837.2 4.4 copy-start.44
  844.3 6.9 slice-start
  844.3 6.8 slice-start.1
  852.8 9.6 %copy-start.1 = (bf16[1024,1024]{1,0:T(8,128)(2,1)S(1)}, bf16[1024,1024]{1,0:T(8,128)(2,1)}, u32[]{:S(2)}) copy-start(bf16[1024,1024]{1,0:T(8,128)(2,1)} %param.21) | copy-start | bytes 6291460
  (20 other events, 35.5 us)
Sparse Core Ops, SparseCore 0:
  11.0 76.3 all-gather.4
  145.9 87.4 all-gather.6
  406.0 95.6 reduce-scatter.6
  536.6 69.3 reduce-scatter.4
